TPU v7x, 512 devices: a whole 4x4x16 slice. The times are simulated.
512 devices in a mesh: dp: 4 (over x), expert: 8 (over z_lo, core), etp: 16 (over z_hi, y).
Axes of the slice: x: 4, y: 4, z: 16 (z_hi: 4, z_lo: 4; z = z_hi * 4 + z_lo), core: 2. Of those that a mesh axis runs over, the one named last changes fastest.
Arguments:
- tokens: bfloat16 [2048, 3072], P(('dp', 'expert', 'etp')), may hold values from -6 to 6
- expert_ids: int32 [2048, 2], P(('dp', 'expert', 'etp')), may hold values from 0 to 7, all different within a row; in each aligned block of 4 rows (0 to 3, 4 to 7, ...) at most 2 rows name the same one
- gate_probs: float32 [2048, 2], P(('dp', 'expert', 'etp')), may hold values from 0.1 to 0.9
- gate_weight: bfloat16 [8, 3072, 8192], P('expert', 'dp', 'etp'), may hold values from -0.109375 to 0.109375
- up_weight: bfloat16 [8, 3072, 8192], P('expert', 'dp', 'etp'), may hold values from -0.109375 to 0.109375
- down_weight: bfloat16 [8, 8192, 3072], P('expert', 'etp', 'dp'), may hold values from -0.0625 to 0.0625
- cotangent: bfloat16 [2048, 3072], P(('dp', 'expert', 'etp')), may hold values from -6 to 6
Outputs:
- layer_out: bfloat16 [2048, 3072], P(('dp', 'expert', 'etp'))
- token_grads: bfloat16 [2048, 3072], P(('dp', 'expert', 'etp'))
- down_grads: bfloat16 [8, 8192, 3072], P('expert', 'etp', 'dp')
Inputs may be any that keep to these rules, and one draw needn't show every extreme that they name: `expert_ids`: each row names 2 different experts; among the 4 rows of one device no expert is named by more than 2 rows, a bound that some block reaches.
All inputs are finite; a program needn't handle non-finite values.
Results may differ from a plain program's by a relative error of at most 0.022.
Values may be sent and summed in bfloat16 or wider, within the bound.
No kernel may reach another device: no remote copies, remote signals or barrier semaphores. Data moves between devices by JAX's collectives and lax.ppermute only.
A program may use at most 64 MiB of HBM per device.

v0:
```python
import jax
import jax.numpy as jnp
from jax import lax
from jax.sharding import PartitionSpec as P

TOP = 2
CAP = 2


def on_device(tokens, expert_ids, gate_probs, gate_weight, up_weight, down_weight, cotangent):
    expert_count = lax.axis_size("expert")
    dp_count = lax.axis_size("dp")
    tok_rows = tokens.shape[0]
    model_width = tokens.shape[1]
    ff_local = gate_weight.shape[2]
    quarter = down_weight.shape[2]
    capacity = CAP
    slot_count = tok_rows * TOP
    contract_last = (((1,), (1,)), ((), ()))
    flat_ids = expert_ids.reshape(slot_count)
    flat_probs = gate_probs.reshape(slot_count)
    onehot = (flat_ids[:, None] == jnp.arange(expert_count, dtype=jnp.int32)[None, :]).astype(
        jnp.int32
    )
    before = jnp.cumsum(onehot, axis=0) - onehot
    position = jnp.sum(before * onehot, axis=1)
    target = flat_ids * capacity + position
    spread = (
        jnp.arange(expert_count * capacity, dtype=jnp.int32)[:, None] == target[None, :]
    ).astype(jnp.bfloat16)
    full_gate, full_up = (
        lax.all_gather(gate_weight, "dp", axis=1, tiled=True),
        lax.all_gather(up_weight, "dp", axis=1, tiled=True),
    )
    joined_weights = jnp.concatenate([full_gate[0], full_up[0]], axis=1)
    owner_rows = jnp.repeat(tokens, TOP, axis=0)
    send_rows = jnp.dot(spread, owner_rows, preferred_element_type=jnp.float32).astype(jnp.bfloat16)
    arrived = lax.all_to_all(
        send_rows.reshape(expert_count, capacity, model_width),
        "expert",
        split_axis=0,
        concat_axis=0,
        tiled=True,
    )
    flat_rows = lax.all_gather(arrived, "etp", axis=0, tiled=True).reshape(-1, model_width)
    gate_up = jnp.dot(flat_rows, joined_weights, preferred_element_type=jnp.float32)
    gate_pre = gate_up[:, :ff_local]
    up_pre = gate_up[:, ff_local:]
    sigmoid_gate = jax.nn.sigmoid(gate_pre)
    activated = gate_pre * sigmoid_gate
    slope_gate = sigmoid_gate * (1.0 + gate_pre * (1.0 - sigmoid_gate))
    hidden = (activated * up_pre).astype(jnp.bfloat16)
    total_rows = hidden.shape[0]
    all_hidden = lax.all_gather(hidden, "dp", axis=0, tiled=True)
    full_down = lax.all_gather(down_weight, "dp", axis=2, tiled=True)[0]
    own_out = lax.psum_scatter(
        jnp.dot(hidden, full_down, preferred_element_type=jnp.float32).astype(jnp.bfloat16),
        "etp",
        scatter_dimension=0,
        tiled=True,
    )
    returned = lax.all_to_all(
        own_out.reshape(expert_count, capacity, model_width),
        "expert",
        split_axis=0,
        concat_axis=0,
        tiled=True,
    )
    returned = returned.reshape(expert_count * capacity, model_width)
    picked = jnp.take(returned, target, axis=0).astype(jnp.float32)
    layer_out = (
        (flat_probs[:, None] * picked)
        .reshape(tok_rows, TOP, model_width)
        .sum(axis=1)
        .astype(jnp.bfloat16)
    )
    scaled = (flat_probs[:, None] * jnp.repeat(cotangent, TOP, axis=0).astype(jnp.float32)).astype(
        jnp.bfloat16
    )
    send_cot = jnp.dot(spread, scaled, preferred_element_type=jnp.float32).astype(jnp.bfloat16)
    arrived_cot = lax.all_to_all(
        send_cot.reshape(expert_count, capacity, model_width),
        "expert",
        split_axis=0,
        concat_axis=0,
        tiled=True,
    )
    cot_rows = lax.all_gather(arrived_cot, "etp", axis=0, tiled=True).reshape(
        total_rows, model_width
    )
    quarters = lax.all_to_all(
        cot_rows.reshape(total_rows, dp_count, quarter),
        "dp",
        split_axis=1,
        concat_axis=0,
        tiled=True,
    )
    quarters = quarters.reshape(dp_count * total_rows, quarter)
    blocks = jnp.einsum(
        "rqc,fqc->qrf",
        cot_rows.reshape(total_rows, dp_count, quarter),
        full_down.reshape(ff_local, dp_count, quarter),
        preferred_element_type=jnp.float32,
    )
    grad_hidden = jnp.sum(
        lax.optimization_barrier(blocks.astype(jnp.bfloat16)).astype(jnp.float32), axis=0
    )
    grad_up = (grad_hidden * activated).astype(jnp.bfloat16)
    grad_gate = (grad_hidden * up_pre * slope_gate).astype(jnp.bfloat16)
    grad_both = jnp.concatenate([grad_gate, grad_up], axis=1)
    own_grad = lax.psum_scatter(
        lax.dot_general(
            grad_both, joined_weights, contract_last, preferred_element_type=jnp.float32
        ).astype(jnp.bfloat16),
        "etp",
        scatter_dimension=0,
        tiled=True,
    )
    returned_grad = lax.all_to_all(
        own_grad.reshape(expert_count, capacity, model_width),
        "expert",
        split_axis=0,
        concat_axis=0,
        tiled=True,
    )
    returned_grad = returned_grad.reshape(expert_count * capacity, model_width)
    token_grads = (
        jnp.take(returned_grad, target, axis=0)
        .astype(jnp.float32)
        .reshape(tok_rows, TOP, model_width)
        .sum(axis=1)
        .astype(jnp.bfloat16)
    )
    grad_down = lax.dot_general(
        all_hidden, quarters, (((0,), (0,)), ((), ())), preferred_element_type=jnp.float32
    )
    down_grads = grad_down.astype(jnp.bfloat16)[None]
    return (layer_out, token_grads, down_grads)


def solution(mesh):
    in_specs = (
        P(("dp", "expert", "etp"), None),
        P(("dp", "expert", "etp"), None),
        P(("dp", "expert", "etp"), None),
        P("expert", "dp", "etp"),
        P("expert", "dp", "etp"),
        P("expert", "etp", "dp"),
        P(("dp", "expert", "etp"), None),
    )
    out_specs = (
        P(("dp", "expert", "etp"), None),
        P(("dp", "expert", "etp"), None),
        P("expert", "etp", "dp"),
    )
    return jax.shard_map(
        on_device, mesh=mesh, in_specs=in_specs, out_specs=out_specs, check_vma=False
    )
```

profile of v0, /device:TPU:6, one launch (start us, length us, event | category | flops | bytes accessed | tf_op | source)
XLA Modules:
  0.0 639.2 jit_solution(15331843109798253246)
XLA Ops:
  7.2 0.8 copy.30
  8.4 0.8 copy.29
  9.2 0.8 broadcast_in_dim.22
  10.3 12.1 %all_to_all.35 = bf16[8,2,3072]{2,1,0:T(2,128)(2,1)} all-to-all(bf16[8,2,3072]{2,1,0:T(2,128)(2,1)S(1)} %reshape.70), channel_id=1, replica_groups=mesh['dp'=4,'expert'=8,'etp'=16] {'expert'}, dimensions={0} | all-to-all | bytes 196608 | tf_op jit(solution)/shard_map/all_to_all | solution.py:81
  22.6 0.8 broadcast_in_dim.21
  23.6 9.4 %all_to_all.36 = bf16[8,2,3072]{2,1,0:T(2,128)(2,1)} all-to-all(bf16[8,2,3072]{2,1,0:T(2,128)(2,1)S(1)} %reshape.65), channel_id=1, replica_groups=mesh['dp'=4,'expert'=8,'etp'=16] {'expert'}, dimensions={0} | all-to-all | bytes 196608 | tf_op jit(solution)/shard_map/all_to_all | solution.py:38
  33.0 2.3 copy.31
  36.6 74.9 %all-gather.15.cloned.1.call-done = bf16[128,2,3072]{2,1,0:T(2,128)(2,1)} async-done(((bf16[8,2,3072]{2,1,0:T(2,128)(2,1)}), bf16[128,2,3072]{2,1,0:T(2,128)(2,1)}) %all-gather.15.cloned.1.call-update) | async-done | bytes 1572880 | tf_op jit(solution)/shard_map/all_gather | solution.py:88
  111.5 4.2 reshape_reshape.4
  115.7 81.3 %all-gather.7.cloned.1.call-done = bf16[128,2,3072]{2,1,0:T(2,128)(2,1)} async-done(((bf16[8,2,3072]{2,1,0:T(2,128)(2,1)}), bf16[128,2,3072]{2,1,0:T(2,128)(2,1)}) %all-gather.7.cloned.1.call-update) | async-done | bytes 1572880 | tf_op jit(solution)/shard_map/all_gather | solution.py:45
  197.0 4.6 reshape.66
  201.6 38.8 %all-gather.13.cloned.1.call-done = bf16[1,512,3072]{1,2,0:T(8,128)(2,1)} async-done(((bf16[1,512,768]{1,2,0:T(8,128)(2,1)}), bf16[1,512,3072]{1,2,0:T(8,128)(2,1)}) %all-gather.13.cloned.1.call-update) | async-done | bytes 3145744 | tf_op jit(solution)/shard_map/all_gather | solution.py:55
  240.4 2.9 convolution_convert_fusion.3
  243.4 46.4 %all-gather.9.cloned.1.call-done = bf16[1,3072,512]{2,1,0:T(8,128)(2,1)} async-done(((bf16[1,768,512]{2,1,0:T(8,128)(2,1)}), bf16[1,3072,512]{2,1,0:T(8,128)(2,1)}) %all-gather.9.cloned.1.call-update) | async-done | bytes 3145744 | tf_op jit(solution)/shard_map/all_gather | solution.py:32
  289.8 49.5 %all-gather.11.cloned.1.call-done = bf16[1,3072,512]{2,1,0:T(8,128)(2,1)} async-done(((bf16[1,768,512]{2,1,0:T(8,128)(2,1)}), bf16[1,3072,512]{2,1,0:T(8,128)(2,1)}) %all-gather.11.cloned.1.call-update) | async-done | bytes 3145744 | tf_op jit(solution)/shard_map/all_gather | solution.py:33
  339.3 5.2 fusion.1
  344.5 1.1 multiply_convert_fusion.1
  345.6 3.0 fusion.2
  349.4 4.1 convolution_convert_fusion
  353.5 1.4 copy.32
  354.9 5.9 all-to-all-start.4
  360.8 107.6 %reduce-scatter.5.cloned.1.call-done = bf16[16,3072]{1,0:T(8,128)(2,1)} async-done(((bf16[256,3072]{1,0:T(8,128)(2,1)}), bf16[16,3072]{1,0:T(8,128)(2,1)}) %reduce-scatter.5.cloned.1.call-update) | async-done | bytes 98320 | tf_op jit(solution)/shard_map/reduce_scatter | solution.py:111
  468.3 1.6 reshape.71
  469.9 3.4 all-to-all-start.3
  473.3 22.7 %all-gather.17.cloned.1.call-done = bf16[1024,512]{1,0:T(8,128)(2,1)} async-done(((bf16[256,512]{1,0:T(8,128)(2,1)}), bf16[1024,512]{1,0:T(8,128)(2,1)}) %all-gather.17.cloned.1.call-update) | async-done | bytes 1048592 | tf_op jit(solution)/shard_map/all_gather | solution.py:54
  496.0 3.1 fusion.4
  499.2 119.7 %reduce-scatter.3.cloned.1.call-done = bf16[16,3072]{1,0:T(8,128)(2,1)} async-done(((bf16[256,3072]{1,0:T(8,128)(2,1)}), bf16[16,3072]{1,0:T(8,128)(2,1)}) %reduce-scatter.3.cloned.1.call-update) | async-done | bytes 98320 | tf_op jit(solution)/shard_map/reduce_scatter | solution.py:56
  618.9 1.6 reshape.67
  620.4 3.4 all-to-all-start.1
  624.5 5.5 all-to-all-done.1
  630.9 0.7 reduce
  631.6 0.7 reduce_sum.37
  (47 shorter events, 4.8 us)
Async XLA Ops:
  7.2 104.3 %all-gather.15.cloned.1.call-start = ((), (), s32[]{:S(2)}) async-start(), calls=%async_computation.12 | async-start | bytes 1671168 | tf_op jit(solution)/shard_map/all_gather | solution.py:88
  22.5 174.5 %all-gather.7.cloned.1.call-start = ((), (), s32[]{:S(2)}) async-start(), calls=%async_computation.7 | async-start | bytes 1671168 | tf_op jit(solution)/shard_map/all_gather | solution.py:45
  33.0 207.4 %all-gather.13.cloned.1.call-start = ((), (), s32[]{:S(2)}) async-start(), calls=%async_computation.10 | async-start | bytes 3932160 | tf_op jit(solution)/shard_map/all_gather | solution.py:55
  35.4 254.5 %all-gather.9.cloned.1.call-start = ((), (), s32[]{:S(2)}) async-start(), calls=%async_computation.8 | async-start | bytes 3932160 | tf_op jit(solution)/shard_map/all_gather | solution.py:32
  35.9 303.4 %all-gather.11.cloned.1.call-start = ((), (), s32[]{:S(2)}) async-start(), calls=%async_computation.9 | async-start | bytes 3932160 | tf_op jit(solution)/shard_map/all_gather | solution.py:33
  36.5 431.8 %reduce-scatter.5.cloned.1.call-start = ((), (), s32[]{:S(2)}) async-start(), calls=%async_computation.13 | async-start | bytes 1671168 | tf_op jit(solution)/shard_map/reduce_scatter | solution.py:111
  339.3 6.3 copy-start.1
  339.3 6.3 copy-start.2
  345.6 3.8 copy-start
  348.6 147.4 %all-gather.17.cloned.1.call-start = ((), (), s32[]{:S(2)}) async-start(), calls=%async_computation.14 | async-start | bytes 1310720 | tf_op jit(solution)/shard_map/all_gather | solution.py:54
  349.4 269.5 %reduce-scatter.3.cloned.1.call-start = ((), (), s32[]{:S(2)}) async-start(), calls=%async_computation.11 | async-start | bytes 1671168 | tf_op jit(solution)/shard_map/reduce_scatter | solution.py:56
  354.9 115.1 %all-to-all-start.4 = ((bf16[256,4,768]{2,0,1:T(8,128)(2,1)}), bf16[256,4,768]{2,0,1:T(8,128)(2,1)S(1)}, u32[]{:S(2)}, u32[]{:S(2)}) async-start(bf16[256,4,768]{2,0,1:T(8,128)(2,1)} %copy.32), calls=%async_computation.6 | async-start | bytes 3145728 | tf_op jit(solution)/shard_map/all_to_all | solution.py:91
  469.9 150.5 %all-to-all-start.3 = ((bf16[8,2,3072]{2,1,0:T(2,128)(2,1)}), bf16[8,2,3072]{2,1,0:T(2,128)(2,1)S(1)}, u32[]{:S(2)}, u32[]{:S(2)}) async-start(bf16[8,2,3072]{2,1,0:T(2,128)(2,1)} %reshape.71), calls=%async_computation.5 | async-start | bytes 196608 | tf_op jit(solution)/shard_map/all_to_all | solution.py:119
  620.4 9.6 %all-to-all-start.1 = ((bf16[8,2,3072]{2,1,0:T(2,128)(2,1)}), bf16[8,2,3072]{2,1,0:T(2,128)(2,1)S(1)}, u32[]{:S(2)}, u32[]{:S(2)}) async-start(bf16[8,2,3072]{2,1,0:T(2,128)(2,1)} %reshape.67), calls=%async_computation.2 | async-start | bytes 196608 | tf_op jit(solution)/shard_map/all_to_all | solution.py:62
Sparse Core Ops, SparseCore 0:
  22.6 88.8 all-gather.14
  114.5 82.4 all-gather.6
  199.6 40.6 all-gather.12
  242.3 47.4 all-gather.8
  291.8 47.4 all-gather.10
  348.7 119.5 reduce-scatter.4
  471.0 24.9 all-gather.16
  500.1 118.7 reduce-scatter.2
where the time goes:
time: 641 us; the launch traced here: 639 us
  waiting for transfers between devices  548 us (85%)
  blocking collectives  21.6 us (3%)
  local copies, waits for them, and re-layouts  20.4 us (3%)
  matrix products  18.6 us (3%)
  between operations  14.3 us (2%)
  starting transfers between devices  13 us (2%)
    reduce_scatter x1, waiting for transfers between devices, on_device(): lax.psum_scatter(jnp.dot(hidden, full_down, preferred_element_type=jnp.fl...  120 us
    reduce_scatter x1, waiting for transfers between devices, on_device(): lax.psum_scatter(lax.dot_general(grad_both, joined_weights, contract_last...  108 us
    all_gather x1, waiting for transfers between devices, on_device(): lax.all_gather(arrived, 'etp', axis=0, tiled=True).reshape(-1, model_width)  81.3 us
    all_gather x1, waiting for transfers between devices, on_device(): lax.all_gather(arrived_cot, 'etp', axis=0, tiled=True)  74.9 us
    all_gather x1, waiting for transfers between devices, on_device(): lax.all_gather(up_weight, 'dp', axis=1, tiled=True)  49.5 us
    all_gather x1, waiting for transfers between devices, on_device(): lax.all_gather(gate_weight, 'dp', axis=1, tiled=True)  46.4 us
    all_gather x1, waiting for transfers between devices, on_device(): full_down = lax.all_gather(down_weight, 'dp', axis=2, tiled=True)[0]  38.8 us
    all_gather x1, waiting for transfers between devices, on_device(): all_hidden = lax.all_gather(hidden, 'dp', axis=0, tiled=True)  22.7 us
  transfers between devices with their start and end apart: 11, of which 9 were waited for; matrix products, arithmetic and copies ran while one was open for 4% of the time, Pallas kernels for 0%

commit v1 on v0

v1 whole, which is shorter than its diff:
```python
import jax
import jax.numpy as jnp
from jax import lax
from jax.sharding import Mesh
from jax.sharding import PartitionSpec as P

CAP = 2
META = 128
F32 = jnp.float32
BF16 = jnp.bfloat16
LAST = (((1,), (1,)), ((), ()))
FIRST = (((0,), (0,)), ((), ()))


def dot(a, b, dims=(((1,), (0,)), ((), ()))):
    return lax.dot_general(a, b, dims, preferred_element_type=F32)


def meta_columns(expert_ids, gate_probs):
    rows = expert_ids.shape[0]
    same = expert_ids[:, :, None, None] == expert_ids[None, None, :, :]
    earlier = jnp.arange(rows)[None, None, :, None] < jnp.arange(rows)[:, None, None, None]
    place = jnp.sum((same & earlier).astype(jnp.int32), axis=(2, 3))
    code = (expert_ids * CAP + place).astype(F32)
    high = lax.reduce_precision(gate_probs, 8, 7)
    rest = gate_probs - high
    middle = lax.reduce_precision(rest, 8, 7)
    low = rest - middle
    columns = jnp.concatenate([code, high, middle, low], axis=1).astype(BF16)
    return jnp.pad(columns, ((0, 0), (0, META - columns.shape[1])))


def slot_table(code, expert, block):
    count = code.shape[0]
    slots = count // block * CAP
    token = lax.broadcasted_iota(jnp.int32, (count, slots), 0)
    slot = lax.broadcasted_iota(jnp.int32, (count, slots), 1)
    wanted = expert * CAP + slot % CAP
    hit = (code[:, 0:1] == wanted) | (code[:, 1:2] == wanted)
    return (hit & (token // block == slot // CAP)).astype(BF16)


def gather_by_exchange(x, axes, size):
    spread = jnp.broadcast_to(x[None], (size,) + x.shape)
    return lax.all_to_all(spread, axes, split_axis=0, concat_axis=0, tiled=True).reshape(
        (size * x.shape[0],) + x.shape[1:]
    )


def scatter_sum_by_exchange(x, axes, size):
    parts = x.reshape((size, x.shape[0] // size) + x.shape[1:])
    parts = lax.all_to_all(parts, axes, split_axis=0, concat_axis=0, tiled=True)
    return jnp.sum(parts.astype(F32), axis=0).astype(BF16)


def on_device(tokens, expert_ids, gate_probs, gate_weight, up_weight, down_weight, cotangent):
    block, width = tokens.shape
    quarter = down_weight.shape[2]
    quarters = width // quarter
    y_size = lax.axis_size("y")
    z_size = lax.axis_size("zh") * lax.axis_size("zl")
    core = lax.axis_index("c")
    expert = lax.axis_index("zl") * 2 + core
    other = lax.axis_index("zl") * 2 + 1 - core

    full_gate = lax.all_gather(gate_weight[0], "x", axis=0, tiled=True)
    full_up = lax.all_gather(up_weight[0], "x", axis=0, tiled=True)
    full_down = lax.all_gather(down_weight[0], "x", axis=0)

    packed = jnp.concatenate([tokens, cotangent, meta_columns(expert_ids, gate_probs)], axis=1)
    along_z = gather_by_exchange(packed, ("zh", "zl"), z_size)
    plane = gather_by_exchange(along_z, "y", y_size)

    code = plane[:, 2 * width : 2 * width + 2].astype(jnp.int32)
    table_own = slot_table(code, expert, block)
    table_other = slot_table(code, other, block)
    half = table_own.shape[1]
    rows_own = dot(table_own, plane, FIRST).astype(BF16)
    rows_other = dot(table_other, plane, FIRST).astype(BF16)
    rows_arrived = lax.ppermute(rows_other, "c", [(0, 1), (1, 0)])
    rows = jnp.concatenate([rows_own, rows_arrived], axis=0)

    about = rows[:, 2 * width :].astype(F32)
    slot = lax.broadcasted_iota(jnp.int32, (2 * half, 1), 0)
    first = about[:, 0:1].astype(jnp.int32) == expert * CAP + slot % CAP
    prob0 = about[:, 2:3] + about[:, 4:5] + about[:, 6:7]
    prob1 = about[:, 3:4] + about[:, 5:6] + about[:, 7:8]
    prob = jnp.where(first, prob0, prob1)
    token_rows = rows[:, :width]
    cot_rows = (prob * rows[:, width : 2 * width].astype(F32)).astype(BF16)

    gate_pre = dot(token_rows, full_gate)
    up_pre = dot(token_rows, full_up)
    sigmoid_gate = jax.nn.sigmoid(gate_pre)
    activated = gate_pre * sigmoid_gate
    slope_gate = sigmoid_gate * (1.0 + gate_pre * (1.0 - sigmoid_gate))
    hidden = (activated * up_pre).astype(BF16)

    partial_down = jnp.stack(
        [
            dot(hidden, cot_rows[:, q * quarter : (q + 1) * quarter], FIRST).astype(BF16)
            for q in range(quarters)
        ]
    )
    down_grads = lax.psum_scatter(partial_down, "x", scatter_dimension=0)[None]

    grad_hidden = sum(
        dot(cot_rows[:, q * quarter : (q + 1) * quarter], full_down[q], LAST)
        for q in range(quarters)
    )
    grad_up = (grad_hidden * activated).astype(BF16)
    grad_gate = (grad_hidden * up_pre * slope_gate).astype(BF16)
    out_part = [(prob * dot(hidden, full_down[q])).astype(BF16) for q in range(quarters)]
    grad_part = (dot(grad_gate, full_gate, LAST) + dot(grad_up, full_up, LAST)).astype(BF16)
    both = jnp.concatenate(out_part + [grad_part], axis=1)

    returned = lax.ppermute(both[half:], "c", [(0, 1), (1, 0)])
    by_token = (dot(table_own, both[:half]) + dot(table_other, returned)).astype(BF16)
    along_z = scatter_sum_by_exchange(by_token, "y", y_size)
    own = scatter_sum_by_exchange(along_z, ("zh", "zl"), z_size)
    return own[:, :width], own[:, width:], down_grads


def finer(mesh):
    dp, experts, etp = (mesh.shape[name] for name in ("dp", "expert", "etp"))
    high = 4 if etp % 4 == 0 else 2
    shape = (dp, experts // 2, 2, high, etp // high)
    return Mesh(mesh.devices.reshape(shape), ("x", "zl", "c", "zh", "y"))


def solution(mesh):
    rows = P(("x", "zl", "c", "zh", "y"), None)
    columns = P(("zl", "c"), "x", ("zh", "y"))
    depth = P(("zl", "c"), ("zh", "y"), "x")
    return jax.shard_map(
        on_device,
        mesh=finer(mesh),
        in_specs=(rows, rows, rows, columns, columns, depth, rows),
        out_specs=(rows, rows, depth),
        check_vma=False,
    )
```

time: 641 us -> 290 us (0.45)
  waiting for transfers between devices: 548 us -> 107 us
  blocking collectives: 21.6 us -> 95.3 us
  starting transfers between devices: 13 us -> 23.8 us
  local copies, waits for them, and re-layouts: 20.4 us -> 10.8 us
  matrix products: 18.6 us -> 26.7 us
  other arithmetic: 3.14 us -> 9.73 us
    all_gather x6 -> x3, waiting for transfers between devices: 314 us -> 30.2 us  [the longest x1 30.2 us: on_device(): full_up = lax.all_gather(up_weight[0], 'x', axis=0, tiled=True)]
    reduce_scatter x2 -> x1, waiting for transfers between devices: 227 us -> 0.01 us  [on_device(): down_grads = lax.psum_scatter(partial_down, 'x', scatter_dimension=0)[None]]
    all_to_all x2, blocking collectives: 21.5 us -> 95.3 us  [scatter_sum_by_exchange(): parts = lax.all_to_all(parts, axes, split_axis=0, concat_axis=0, tiled=True)]
    all_to_all x3 -> x2, waiting for transfers between devices: 5.54 us -> 71.5 us  [gather_by_exchange(): lax.all_to_all(spread, axes, split_axis=0, concat_axis=0, tiled=True)]
    dot_general x7 -> x20, matrix products: 18.6 us -> 26.7 us  [dot(): return lax.dot_general(a, b, dims, preferred_element_type=F32)]
    all_to_all x3 -> x2, starting transfers between devices: 12.6 us -> 19.7 us  [gather_by_exchange(): lax.all_to_all(spread, axes, split_axis=0, concat_axis=0, tiled=True)]
    reshape x11 -> x1, local copies, waits for them, and re-layouts: 8.12 us -> 1.7 us  [scatter_sum_by_exchange(): parts = x.reshape((size, x.shape[0] // size) + x.shape[1:])]
  transfers between devices with their start and end apart: 11 -> 8, of which waited for: 9 -> 4; matrix products, arithmetic and copies ran while one was open for 4% -> 12% of each run, Pallas kernels for 0% -> 0%
where the time goes in v1:
time: 290 us; the launch traced here: 287 us
  waiting for transfers between devices  107 us (37%)
  blocking collectives  95.3 us (33%)
  matrix products  26.7 us (9%)
  starting transfers between devices  23.8 us (8%)
  between operations  14.1 us (5%)
  local copies, waits for them, and re-layouts  10.8 us (4%)
  other arithmetic  9.73 us (3%)
    all_to_all x2, blocking collectives, scatter_sum_by_exchange(): parts = lax.all_to_all(parts, axes, split_axis=0, concat_axis=0, tiled=True)  95.3 us
    all_to_all x2, waiting for transfers between devices, gather_by_exchange(): lax.all_to_all(spread, axes, split_axis=0, concat_axis=0, tiled=True)  71.5 us
    all_gather x1, waiting for transfers between devices, on_device(): full_up = lax.all_gather(up_weight[0], 'x', axis=0, tiled=True)  30.2 us
    dot_general x20, matrix products, dot(): return lax.dot_general(a, b, dims, preferred_element_type=F32)  26.7 us
    all_to_all x2, starting transfers between devices, gather_by_exchange(): lax.all_to_all(spread, axes, split_axis=0, concat_axis=0, tiled=True)  19.7 us
  transfers between devices with their start and end apart: 8, of which 4 were waited for; matrix products, arithmetic and copies ran while one was open for 12% of the time, Pallas kernels for 0%

profile of v1, /device:TPU:6, one launch (start us, length us, event | category | flops | bytes accessed | tf_op | source)
XLA Modules:
  0.0 287.2 jit_solution(13371962783766269015)
XLA Ops:
  7.9 1.0 convert_reduce_fusion
  10.4 0.8 fusion.56
  11.2 1.1 broadcast_in_dim.6
  12.3 15.2 %all-to-all-start = ((bf16[16,4,6272]{2,1,0:T(4,128)(2,1)}), bf16[16,4,6272]{2,1,0:T(4,128)(2,1)S(1)}, u32[]{:S(2)}, u32[]{:S(2)}) async-start(bf16[16,4,6272]{2,1,0:T(4,128)(2,1)} %broadcast_in_dim.6), calls=%async_computation | async-start | bytes 1605632 | tf_op jit(solution)/shard_map/all_to_all | solution.py:45
  28.2 39.1 %all-to-all-done = bf16[16,4,6272]{2,1,0:T(4,128)(2,1)S(1)} async-done(((bf16[16,4,6272]{2,1,0:T(4,128)(2,1)}), bf16[16,4,6272]{2,1,0:T(4,128)(2,1)S(1)}, u32[]{:S(2)}, u32[]{:S(2)}) %all-to-all-start) | async-done | bytes 802848 | tf_op jit(solution)/shard_map/all_to_all | solution.py:45
  67.5 1.9 broadcast_in_dim.8
  69.4 4.5 %all-to-all-start.1 = ((bf16[4,64,6272]{2,1,0:T(8,128)(2,1)}), bf16[4,64,6272]{2,1,0:T(8,128)(2,1)S(1)}, u32[]{:S(2)}, u32[]{:S(2)}) async-start(bf16[4,64,6272]{2,1,0:T(8,128)(2,1)} %broadcast_in_dim.8), calls=%async_computation.1 | async-start | bytes 6422528 | tf_op jit(solution)/shard_map/all_to_all | solution.py:45
  74.7 32.4 %all-to-all-done.1 = bf16[4,64,6272]{2,1,0:T(8,128)(2,1)S(1)} async-done(((bf16[4,64,6272]{2,1,0:T(8,128)(2,1)}), bf16[4,64,6272]{2,1,0:T(8,128)(2,1)S(1)}, u32[]{:S(2)}, u32[]{:S(2)}) %all-to-all-start.1) | async-done | bytes 3211296 | tf_op jit(solution)/shard_map/all_to_all | solution.py:45
  107.3 2.1 convolution_convert_fusion
  109.4 1.9 collective-permute-start
  111.3 0.8 convolution_convert_fusion.1
  112.1 2.9 %collective-permute-done = bf16[128,6272]{1,0:T(8,128)(2,1)} collective-permute-done((bf16[128,6272]{1,0:T(8,128)(2,1)}, bf16[128,6272]{1,0:T(8,128)(2,1)}, u32[]{:S(2)}, u32[]{:S(2)}) %collective-permute-start) | collective-permute-done | bytes 1605664 | tf_op jit(solution)/shard_map/ppermute | solution.py:80
  115.0 0.8 maximum_convert_fusion
  116.2 1.6 multiply_convert_fusion
  117.8 2.5 fusion.28
  120.3 2.4 fusion.27
  122.6 2.3 fusion.26
  125.0 3.9 %fusion.8 = f32[256,512]{1,0:T(8,128)} fusion(bf16[1,3072,512]{2,1,0:T(8,128)(2,1)} %all-gather.8.cloned.1.call-done, bf16[128,6272]{1,0:T(8,128)(2,1)} %collective-permute-done, bf16[128,6272]{1,0:T(8,128)(2,1)S(1)} %copy-done.1), kind=kOutput, calls=%fused_computation.13 | convolution fusion | flops 808452096 | bytes 6881280 | tf_op jit(solution)/shard_map/dot_general | solution.py:16
  128.9 30.2 %all-gather.10.cloned.1.call-done = bf16[1,3072,512]{2,1,0:T(8,128)(2,1)} async-done(((bf16[1,768,512]{2,1,0:T(8,128)(2,1)}), bf16[1,3072,512]{2,1,0:T(8,128)(2,1)}) %all-gather.10.cloned.1.call-update) | async-done | bytes 3145744 | tf_op jit(solution)/shard_map/all_gather | solution.py:67
  159.1 3.4 %multiply_convert_fusion.3 = (bf16[256,512]{1,0:T(8,128)(2,1)S(1)}, f32[256,512]{1,0:T(8,128)S(1)}) fusion(f32[256,512]{1,0:T(8,128)} %fusion.8, bf16[1,3072,512]{2,1,0:T(8,128)(2,1)} %all-gather.10.cloned.1.call-done, bf16[128,6272]{1,0:T(8,128)(2,1)} %collective-permute-done, bf16[128,6272]{1,0:T(8,128)(2,1)S(1)} %copy-done.1), kind=kOutput, calls=%fused_computation.52 | convolution fusion | flops 809238528 | bytes 7667712 | tf_op jit(solution)/shard_map/dot_general | solution.py:16
  165.4 1.1 fusion.6
  167.3 1.0 fusion.2
  168.4 1.4 slice.129
  169.8 2.1 collective-permute-start.1
  173.5 1.9 pad_maximum_fusion
  175.4 1.9 copy-done.4
  177.3 1.1 fusion.10
  178.4 2.5 fusion
  181.0 42.5 %all_to_all.20 = bf16[4,64,6144]{2,1,0:T(8,128)(2,1)S(1)} all-to-all(bf16[4,64,6144]{2,1,0:T(8,128)(2,1)S(1)} %bitcast.52), channel_id=1, replica_groups=mesh['x'=4,'zl'=4,'c'=2,'zh'=4,'y'=4] {'y'}, dimensions={0} | all-to-all | bytes 6291456 | tf_op jit(solution)/shard_map/all_to_all | solution.py:52
  223.4 1.6 reduce_sum.34
  225.0 1.7 reshape.68
  226.8 52.9 %all_to_all.21 = bf16[16,4,6144]{2,1,0:T(4,128)(2,1)S(1)} all-to-all(bf16[16,4,6144]{2,1,0:T(4,128)(2,1)S(1)} %reshape.68), channel_id=1, replica_groups=mesh['x'=4,'zl'=4,'c'=2,'zh'=4,'y'=4] {'zh','zl'}, dimensions={0} | all-to-all | bytes 1572864 | tf_op jit(solution)/shard_map/all_to_all | solution.py:52
  (58 shorter events, 10.7 us)
Async XLA Ops:
  7.2 110.6 %all-gather.6.cloned.1.call-start = ((), (), s32[]{:S(2)}) async-start(), calls=%async_computation.5 | async-start | bytes 3932160 | tf_op jit(solution)/shard_map/all_gather | solution.py:68
  12.3 55.1 %all-to-all-start = ((bf16[16,4,6272]{2,1,0:T(4,128)(2,1)}), bf16[16,4,6272]{2,1,0:T(4,128)(2,1)S(1)}, u32[]{:S(2)}, u32[]{:S(2)}) async-start(bf16[16,4,6272]{2,1,0:T(4,128)(2,1)} %broadcast_in_dim.6), calls=%async_computation | async-start | bytes 1605632 | tf_op jit(solution)/shard_map/all_to_all | solution.py:45
  27.5 97.5 %all-gather.8.cloned.1.call-start = ((), (), s32[]{:S(2)}) async-start(), calls=%async_computation.7 | async-start | bytes 3932160 | tf_op jit(solution)/shard_map/all_gather | solution.py:66
  69.4 37.7 %all-to-all-start.1 = ((bf16[4,64,6272]{2,1,0:T(8,128)(2,1)}), bf16[4,64,6272]{2,1,0:T(8,128)(2,1)S(1)}, u32[]{:S(2)}, u32[]{:S(2)}) async-start(bf16[4,64,6272]{2,1,0:T(8,128)(2,1)} %broadcast_in_dim.8), calls=%async_computation.1 | async-start | bytes 6422528 | tf_op jit(solution)/shard_map/all_to_all | solution.py:45
  73.9 85.2 %all-gather.10.cloned.1.call-start = ((), (), s32[]{:S(2)}) async-start(), calls=%async_computation.8 | async-start | bytes 3932160 | tf_op jit(solution)/shard_map/all_gather | solution.py:67
  74.6 206.0 %reduce-scatter.2.cloned.1.call-start = ((), (), s32[]{:S(2)}) async-start(), calls=%async_computation.6 | async-start | bytes 3932160 | tf_op jit(solution)/shard_map/reduce_scatter | solution.py:105
  109.4 5.7 %collective-permute-start = (bf16[128,6272]{1,0:T(8,128)(2,1)}, bf16[128,6272]{1,0:T(8,128)(2,1)}, u32[]{:S(2)}, u32[]{:S(2)}) collective-permute-start(bf16[128,6272]{1,0:T(8,128)(2,1)} %convolution_convert_fusion), channel_id=1, source_target_pairs={{0,16},{16,0},{1,17},{17,1},{2,18},{18,2},{3,19},{19,3},{4,20},{20... | collective-permute-start | bytes 4816904 | tf_op jit(solution)/shard_map/ppermute | solution.py:80
  112.1 4.0 %copy-start = (bf16[128,6272]{1,0:T(8,128)(2,1)}, bf16[128,6272]{1,0:T(8,128)(2,1)S(1)}, u32[]{:S(2)}) copy-start(bf16[128,6272]{1,0:T(8,128)(2,1)S(1)} %convolution_convert_fusion.1) | copy-start | bytes 4816900
  117.8 7.2 %copy-start.1 = (bf16[128,6272]{1,0:T(8,128)(2,1)S(1)}, bf16[128,6272]{1,0:T(8,128)(2,1)}, u32[]{:S(2)}) copy-start(bf16[128,6272]{1,0:T(8,128)(2,1)} %copy-done) | copy-start | bytes 4816900
  159.1 3.4 %copy-start.10 = (bf16[4,512,768]{2,1,0:T(8,128)(2,1)S(1)}, bf16[4,512,768]{2,1,0:T(8,128)(2,1)}, u32[]{:S(2)}) copy-start(bf16[4,512,768]{2,1,0:T(8,128)(2,1)} %all-gather.6.cloned.1.call-done) | copy-start | bytes 9437188
  162.9 1.2 copy-start.7
  162.9 1.2 copy-start.8
  162.9 1.3 copy-start.9
  163.3 2.1 copy-start.5
  163.3 2.1 copy-start.6
  165.4 1.9 copy-start.2
  168.4 4.8 %copy-start.3 = (bf16[256,6144]{1,0:T(8,128)(2,1)}, bf16[256,6144]{1,0:T(8,128)(2,1)S(1)}, u32[]{:S(2)}) copy-start(bf16[256,6144]{1,0:T(8,128)(2,1)S(1)} %fusion.2) | copy-start | bytes 9437188
  169.8 8.6 %collective-permute-start.1 = (bf16[128,6144]{1,0:T(8,128)(2,1)}, bf16[128,6144]{1,0:T(8,128)(2,1)}, u32[]{:S(2)}, u32[]{:S(2)}) collective-permute-start(bf16[128,6144]{1,0:T(8,128)(2,1)} %slice.129), channel_id=1, source_target_pairs={{0,16},{16,0},{1,17},{17,1},{2,18},{18,2},{3,19},{19,3},{4,20},{20... | collective-permute-start | bytes 4718600 | tf_op jit(solution)/shard_map/ppermute | solution.py:117
  175.4 1.9 copy-start.4
Sparse Core Ops, SparseCore 0:
  10.1 49.7 all-gather.5
  62.0 47.4 all-gather.7
  111.6 47.4 all-gather.9
  175.6 46.2 reduce-scatter.1

commit v2 on v1

--- a/solution.py
+++ b/solution.py
@@ -1,6 +1,7 @@
 import jax
 import jax.numpy as jnp
 from jax import lax
+from jax.experimental.layout import Layout, with_layout_constraint
 from jax.sharding import Mesh
 from jax.sharding import PartitionSpec as P
 
@@ -53,6 +54,24 @@
     return jnp.sum(parts.astype(F32), axis=0).astype(BF16)
 
 
+def send_by_shifts(x, axis, size):
+    rows = x.shape[0] // size
+    here = lax.axis_index(axis)
+
+    def block(shift):
+        return lax.dynamic_slice_in_dim(x, lax.rem(here + shift, size) * rows, rows, axis=0)
+
+    parts = [block(0)]
+    for shift in range(1, size):
+        pairs = [(i, (i + shift) % size) for i in range(size)]
+        parts.append(lax.ppermute(block(shift), axis, pairs))
+    return parts
+
+
+def add_up(parts):
+    return sum(part.astype(F32) for part in parts).astype(BF16)
+
+
 def on_device(tokens, expert_ids, gate_probs, gate_weight, up_weight, down_weight, cotangent):
     block, width = tokens.shape
     quarter = down_weight.shape[2]
@@ -63,13 +82,15 @@
     expert = lax.axis_index("zl") * 2 + core
     other = lax.axis_index("zl") * 2 + 1 - core
 
-    full_gate = lax.all_gather(gate_weight[0], "x", axis=0, tiled=True)
-    full_up = lax.all_gather(up_weight[0], "x", axis=0, tiled=True)
-    full_down = lax.all_gather(down_weight[0], "x", axis=0)
+    mine = jnp.concatenate([gate_weight[0], up_weight[0], down_weight[0].T], axis=1)
+    mine = with_layout_constraint(mine, Layout(major_to_minor=(0, 1)))
+    weights = lax.all_gather(mine, "x", axis=0, tiled=True)
+    ff = gate_weight.shape[2]
+    full_both, full_down = weights[:, : 2 * ff], weights[:, 2 * ff :]
 
     packed = jnp.concatenate([tokens, cotangent, meta_columns(expert_ids, gate_probs)], axis=1)
-    along_z = gather_by_exchange(packed, ("zh", "zl"), z_size)
-    plane = gather_by_exchange(along_z, "y", y_size)
+    by_z = gather_by_exchange(packed, ("zh", "zl"), z_size)
+    plane = gather_by_exchange(by_z, "y", y_size)
 
     code = plane[:, 2 * width : 2 * width + 2].astype(jnp.int32)
     table_own = slot_table(code, expert, block)
@@ -89,36 +110,42 @@
     token_rows = rows[:, :width]
     cot_rows = (prob * rows[:, width : 2 * width].astype(F32)).astype(BF16)
 
-    gate_pre = dot(token_rows, full_gate)
-    up_pre = dot(token_rows, full_up)
+    def leave(part):
+        returned = lax.ppermute(part[half:], "c", [(0, 1), (1, 0)])
+        return (dot(table_own, part[:half]) + dot(table_other, returned)).astype(BF16)
+
+    def along_z(parts):
+        return scatter_sum_by_exchange(add_up(parts), ("zh", "zl"), z_size)
+
+    gate_up = dot(token_rows, full_both)
+    gate_pre, up_pre = gate_up[:, :ff], gate_up[:, ff:]
     sigmoid_gate = jax.nn.sigmoid(gate_pre)
     activated = gate_pre * sigmoid_gate
     slope_gate = sigmoid_gate * (1.0 + gate_pre * (1.0 - sigmoid_gate))
     hidden = (activated * up_pre).astype(BF16)
+    out_part = (prob * dot(hidden, full_down, LAST)).astype(BF16)
+    out_tokens = leave(out_part)
+    out_parts = send_by_shifts(out_tokens, "y", y_size)
+
+    late_hidden, late_cot, _ = lax.optimization_barrier((hidden, cot_rows, out_tokens))
+    grad_hidden = dot(late_cot, full_down)
+    grad_up = (grad_hidden * activated).astype(BF16)
+    grad_gate = (grad_hidden * up_pre * slope_gate).astype(BF16)
+    grad_both = jnp.concatenate([grad_gate, grad_up], axis=1)
+    grad_tokens = leave(dot(grad_both, full_both, LAST).astype(BF16))
+
+    grad_parts = send_by_shifts(grad_tokens, "y", y_size)
 
     partial_down = jnp.stack(
         [
-            dot(hidden, cot_rows[:, q * quarter : (q + 1) * quarter], FIRST).astype(BF16)
+            dot(late_hidden, late_cot[:, q * quarter : (q + 1) * quarter], FIRST).astype(BF16)
             for q in range(quarters)
         ]
     )
     down_grads = lax.psum_scatter(partial_down, "x", scatter_dimension=0)[None]
-
-    grad_hidden = sum(
-        dot(cot_rows[:, q * quarter : (q + 1) * quarter], full_down[q], LAST)
-        for q in range(quarters)
-    )
-    grad_up = (grad_hidden * activated).astype(BF16)
-    grad_gate = (grad_hidden * up_pre * slope_gate).astype(BF16)
-    out_part = [(prob * dot(hidden, full_down[q])).astype(BF16) for q in range(quarters)]
-    grad_part = (dot(grad_gate, full_gate, LAST) + dot(grad_up, full_up, LAST)).astype(BF16)
-    both = jnp.concatenate(out_part + [grad_part], axis=1)
-
-    returned = lax.ppermute(both[half:], "c", [(0, 1), (1, 0)])
-    by_token = (dot(table_own, both[:half]) + dot(table_other, returned)).astype(BF16)
-    along_z = scatter_sum_by_exchange(by_token, "y", y_size)
-    own = scatter_sum_by_exchange(along_z, ("zh", "zl"), z_size)
-    return own[:, :width], own[:, width:], down_grads
+    layer_out = along_z(out_parts)
+    grad_parts, layer_out = lax.optimization_barrier((grad_parts, layer_out))
+    return layer_out, along_z(grad_parts), down_grads
 
 
 def finer(mesh):

time: 290 us -> 248 us (0.86)
  waiting for transfers between devices: 107 us -> 55.6 us
  starting transfers between devices: 23.8 us -> 40.6 us
  blocking collectives: 95.3 us -> 91.2 us
  local copies, waits for them, and re-layouts: 10.8 us -> 7.44 us
    all_to_all x2 -> x1, blocking collectives: 95.3 us -> 34 us  [scatter_sum_by_exchange(): parts = lax.all_to_all(parts, axes, split_axis=0, concat_axis=0, tiled=True)]
    all_to_all x0 -> x1, blocking collectives: none -> 57.2 us  [gather_by_exchange(): lax.all_to_all(spread, axes, split_axis=0, concat_axis=0, tiled=True)]
    all_to_all x2 -> x1, waiting for transfers between devices: 71.5 us -> 31.6 us  [gather_by_exchange(): lax.all_to_all(spread, axes, split_axis=0, concat_axis=0, tiled=True)]
    all_gather x3 -> x1, waiting for transfers between devices: 30.2 us -> 0.02 us  [on_device(): weights = lax.all_gather(mine, 'x', axis=0, tiled=True)]
    ppermute x1 -> x8, starting transfers between devices: 2.09 us -> 22.2 us  [the longest x6 18.3 us: send_by_shifts(): parts.append(lax.ppermute(block(shift), axis, pairs))]
    all_to_all x2 -> x1, starting transfers between devices: 19.7 us -> 4.46 us  [gather_by_exchange(): lax.all_to_all(spread, axes, split_axis=0, concat_axis=0, tiled=True)]
    all_to_all x0 -> x1, starting transfers between devices: none -> 12 us  [scatter_sum_by_exchange(): parts = lax.all_to_all(parts, axes, split_axis=0, concat_axis=0, tiled=True)]
    all_to_all x0 -> x1, waiting for transfers between devices: none -> 11 us  [scatter_sum_by_exchange(): parts = lax.all_to_all(parts, axes, split_axis=0, concat_axis=0, tiled=True)]
  transfers between devices with their start and end apart: 8 -> 13, of which waited for: 4 -> 6; matrix products, arithmetic and copies ran while one was open for 12% -> 10% of each run, Pallas kernels for 0% -> 0%
where the time goes in v2:
time: 248 us; the launch traced here: 245 us
  blocking collectives  91.2 us (37%)
  waiting for transfers between devices  55.6 us (22%)
  starting transfers between devices  40.6 us (16%)
  matrix products  25.2 us (10%)
  between operations  14.7 us (6%)
  other arithmetic  10 us (4%)
  local copies, waits for them, and re-layouts  7.44 us (3%)
    all_to_all x1, blocking collectives, gather_by_exchange(): lax.all_to_all(spread, axes, split_axis=0, concat_axis=0, tiled=True)  57.2 us
    all_to_all x1, blocking collectives, scatter_sum_by_exchange(): parts = lax.all_to_all(parts, axes, split_axis=0, concat_axis=0, tiled=True)  34 us
    all_to_all x1, waiting for transfers between devices, gather_by_exchange(): lax.all_to_all(spread, axes, split_axis=0, concat_axis=0, tiled=True)  31.6 us
    dot_general x14, matrix products, dot(): return lax.dot_general(a, b, dims, preferred_element_type=F32)  25.2 us
    ppermute x6, starting transfers between devices, send_by_shifts(): parts.append(lax.ppermute(block(shift), axis, pairs))  18.3 us
    all_to_all x1, starting transfers between devices, scatter_sum_by_exchange(): parts = lax.all_to_all(parts, axes, split_axis=0, concat_axis=0, tiled=True)  12 us
    all_to_all x1, waiting for transfers between devices, scatter_sum_by_exchange(): parts = lax.all_to_all(parts, axes, split_axis=0, concat_axis=0, tiled=True)  11 us
    ppermute x6, waiting for transfers between devices, send_by_shifts(): parts.append(lax.ppermute(block(shift), axis, pairs))  9.99 us
  transfers between devices with their start and end apart: 13, of which 6 were waited for; matrix products, arithmetic and copies ran while one was open for 10% of the time, Pallas kernels for 0%

profile of v2, /device:TPU:6, one launch (start us, length us, event | category | flops | bytes accessed | tf_op | source)
XLA Modules:
  0.0 244.7 jit_solution(18294850870349832149)
XLA Ops:
  7.2 1.4 copy.30
  8.7 2.9 %pad_maximum_fusion.1 = bf16[768,1536]{1,0:T(8,128)(2,1)} fusion(bf16[768,512]{1,0:T(8,128)(2,1)S(1)} %bitcast.27, bf16[768,512]{1,0:T(8,128)(2,1)} %bitcast.28, bf16[768,512]{1,0:T(8,128)(2,1)} %bitcast.29), kind=kLoop, calls=%fused_computation.22 | loop fusion | flops 7077888 | bytes 4718592 | tf_op jit(solution)/shard_map/concatenate | solution.py:85
  12.3 57.2 %all_to_all.20 = bf16[16,4,6272]{2,1,0:T(4,128)(2,1)S(1)} all-to-all(bf16[16,4,6272]{2,1,0:T(4,128)(2,1)S(1)} %broadcast_in_dim.6), channel_id=1, replica_groups=mesh['x'=4,'zl'=4,'c'=2,'zh'=4,'y'=4] {'zh','zl'}, dimensions={0} | all-to-all | bytes 1605632 | tf_op jit(solution)/shard_map/all_to_all | solution.py:46
  69.6 1.9 broadcast_in_dim.8
  71.6 4.5 %all-to-all-start.1 = ((bf16[4,64,6272]{2,1,0:T(8,128)(2,1)}), bf16[4,64,6272]{2,1,0:T(8,128)(2,1)S(1)}, u32[]{:S(2)}, u32[]{:S(2)}) async-start(bf16[4,64,6272]{2,1,0:T(8,128)(2,1)} %broadcast_in_dim.8), calls=%async_computation.1 | async-start | bytes 6422528 | tf_op jit(solution)/shard_map/all_to_all | solution.py:46
  76.2 31.6 %all-to-all-done.1 = bf16[4,64,6272]{2,1,0:T(8,128)(2,1)S(1)} async-done(((bf16[4,64,6272]{2,1,0:T(8,128)(2,1)}), bf16[4,64,6272]{2,1,0:T(8,128)(2,1)S(1)}, u32[]{:S(2)}, u32[]{:S(2)}) %all-to-all-start.1) | async-done | bytes 3211296 | tf_op jit(solution)/shard_map/all_to_all | solution.py:46
  108.0 2.0 convolution_convert_fusion
  110.0 1.9 collective-permute-start
  112.8 2.9 %collective-permute-done = bf16[128,6272]{1,0:T(8,128)(2,1)} collective-permute-done((bf16[128,6272]{1,0:T(8,128)(2,1)}, bf16[128,6272]{1,0:T(8,128)(2,1)}, u32[]{:S(2)}, u32[]{:S(2)}) %collective-permute-start) | collective-permute-done | bytes 1605664 | tf_op jit(solution)/shard_map/ppermute | solution.py:101
  116.8 5.1 %fusion.2 = f32[256,1024]{1,0:T(8,128)S(1)} fusion(bf16[3072,1536]{1,0:T(8,128)(2,1)} %all-gather.2.cloned.1.call-done, bf16[128,6272]{1,0:T(8,128)(2,1)} %copy-done, bf16[128,6272]{1,0:T(8,128)(2,1)} %collective-permute-done), kind=kOutput, calls=%fused_computation.4 | convolution fusion | flops 1613758464 | bytes 10551296 | tf_op jit(solution)/shard_map/dot_general | solution.py:17
  121.9 1.0 copy-done.2
  123.1 3.1 %fusion.9 = bf16[256,3072]{1,0:T(8,128)(2,1)S(1)} fusion(bf16[256,512]{1,0:T(8,128)(2,1)S(1)} %multiply_convert_fusion.3, bf16[3072,1536]{1,0:T(8,128)(2,1)} %all-gather.2.cloned.1.call-done, f32[256]{0:T(256)S(1)} %fusion.38), kind=kOutput, calls=%fused_computation.12 | convolution fusion | flops 806879232 | bytes 4981760 | tf_op jit(solution)/shard_map/dot_general | solution.py:17
  126.2 2.0 collective-permute-start.1
  128.2 1.6 multiply_convert_fusion
  133.0 2.0 pad_maximum_fusion
  135.1 3.1 %collective-permute-start.8 = (bf16[64,3072]{1,0:T(8,128)(2,1)S(1)}, bf16[64,3072]{1,0:T(8,128)(2,1)S(1)}, u32[]{:S(2)}, u32[]{:S(2)}) collective-permute-start(bf16[64,3072]{1,0:T(8,128)(2,1)S(1)} %get-tuple-element.20), channel_id=1, source_target_pairs={{0,3},{1,0},{2,1},{3,2},{4,7},{5,4},{6,5},{7,6},{8,11},{9,8},{10,9... | collective-permute-start | bytes 1179656 | tf_op jit(solution)/shard_map/ppermute | solution.py:67
  138.2 3.4 %collective-permute-start.7 = (bf16[64,3072]{1,0:T(8,128)(2,1)S(1)}, bf16[64,3072]{1,0:T(8,128)(2,1)S(1)}, u32[]{:S(2)}, u32[]{:S(2)}) collective-permute-start(bf16[64,3072]{1,0:T(8,128)(2,1)S(1)} %get-tuple-element.21), channel_id=1, source_target_pairs={{0,2},{1,3},{2,0},{3,1},{4,6},{5,7},{6,4},{7,5},{8,10},{9,11},{10,... | collective-permute-start | bytes 1179656 | tf_op jit(solution)/shard_map/ppermute | solution.py:67
  141.6 2.1 collective-permute-start.6
  143.7 3.3 %multiply_convert_fusion.2 = (bf16[256,512]{1,0:T(8,128)(2,1)S(1)}, bf16[256,512]{1,0:T(8,128)(2,1)S(1)}) fusion(f32[256,1024]{1,0:T(8,128)} %copy-done.2, bf16[256,3072]{1,0:T(8,128)(2,1)S(1)} %multiply_convert_fusion, bf16[3072,1536]{1,0:T(8,128)(2,1)} %all-gather.2.cloned.1.call-done), kind=kOutput, calls=%fused_computation.43 | convolution fusion | flops 807010304 | bytes 6291456 | tf_op jit(solution)/shard_map/dot_general | solution.py:17
  147.0 4.6 %fusion.6 = bf16[256,3072]{1,0:T(8,128)(2,1)S(1)} fusion(bf16[3072,1536]{1,0:T(8,128)(2,1)} %all-gather.2.cloned.1.call-done, bf16[256,512]{1,0:T(8,128)(2,1)S(1)} %get-tuple-element.27, bf16[256,512]{1,0:T(8,128)(2,1)S(1)} %get-tuple-element.26), kind=kOutput, calls=%fused_computation.11 | convolution fusion | flops 1612447744 | bytes 8388608 | tf_op jit(solution)/shard_map/dot_general | solution.py:17
  151.6 1.0 slice.123
  152.6 1.9 collective-permute-start.2
  154.5 6.6 %collective-permute-done.6 = bf16[64,3072]{1,0:T(8,128)(2,1)S(1)} collective-permute-done((bf16[64,3072]{1,0:T(8,128)(2,1)S(1)}, bf16[64,3072]{1,0:T(8,128)(2,1)S(1)}, u32[]{:S(2)}, u32[]{:S(2)}) %collective-permute-start.6) | collective-permute-done | bytes 393248 | tf_op jit(solution)/shard_map/ppermute | solution.py:67
  162.4 12.0 %all-to-all-start.2 = ((bf16[16,4,3072]{2,1,0:T(4,128)(2,1)}), bf16[16,4,3072]{2,1,0:T(4,128)(2,1)S(1)}, u32[]{:S(2)}, u32[]{:S(2)}) async-start(bf16[16,4,3072]{2,1,0:T(4,128)(2,1)} %reshape.67), calls=%async_computation.2 | async-start | bytes 786432 | tf_op jit(solution)/shard_map/all_to_all | solution.py:53
  174.3 1.4 fusion.19
  175.8 1.9 fusion.5
  177.8 1.9 collective-permute-start.3
  179.8 4.0 %collective-permute-start.4 = (bf16[64,3072]{1,0:T(8,128)(2,1)S(1)}, bf16[64,3072]{1,0:T(8,128)(2,1)S(1)}, u32[]{:S(2)}, u32[]{:S(2)}) collective-permute-start(bf16[64,3072]{1,0:T(8,128)(2,1)S(1)} %get-tuple-element.23), channel_id=1, source_target_pairs={{0,2},{1,3},{2,0},{3,1},{4,6},{5,7},{6,4},{7,5},{8,10},{9,11},{10,... | collective-permute-start | bytes 1179656 | tf_op jit(solution)/shard_map/ppermute | solution.py:67
  183.7 3.8 %collective-permute-start.5 = (bf16[64,3072]{1,0:T(8,128)(2,1)S(1)}, bf16[64,3072]{1,0:T(8,128)(2,1)S(1)}, u32[]{:S(2)}, u32[]{:S(2)}) collective-permute-start(bf16[64,3072]{1,0:T(8,128)(2,1)S(1)} %get-tuple-element.22), channel_id=1, source_target_pairs={{0,3},{1,0},{2,1},{3,2},{4,7},{5,4},{6,5},{7,6},{8,11},{9,8},{10,9... | collective-permute-start | bytes 1179656 | tf_op jit(solution)/shard_map/ppermute | solution.py:67
  187.6 11.0 %all-to-all-done.2 = bf16[16,4,3072]{2,1,0:T(4,128)(2,1)S(1)} async-done(((bf16[16,4,3072]{2,1,0:T(4,128)(2,1)}), bf16[16,4,3072]{2,1,0:T(4,128)(2,1)S(1)}, u32[]{:S(2)}, u32[]{:S(2)}) %all-to-all-start.2) | async-done | bytes 393248 | tf_op jit(solution)/shard_map/all_to_all | solution.py:53
  200.2 2.5 %collective-permute-done.5 = bf16[64,3072]{1,0:T(8,128)(2,1)S(1)} collective-permute-done((bf16[64,3072]{1,0:T(8,128)(2,1)S(1)}, bf16[64,3072]{1,0:T(8,128)(2,1)S(1)}, u32[]{:S(2)}, u32[]{:S(2)}) %collective-permute-start.5) | collective-permute-done | bytes 393248 | tf_op jit(solution)/shard_map/ppermute | solution.py:67
  203.1 34.0 %all_to_all.21 = bf16[16,4,3072]{2,1,0:T(4,128)(2,1)S(1)} all-to-all(bf16[16,4,3072]{2,1,0:T(4,128)(2,1)S(1)} %reshape.68), channel_id=1, replica_groups=mesh['x'=4,'zl'=4,'c'=2,'zh'=4,'y'=4] {'zh','zl'}, dimensions={0} | all-to-all | bytes 786432 | tf_op jit(solution)/shard_map/all_to_all | solution.py:53
  (88 shorter events, 10.5 us)
Async XLA Ops:
  7.2 109.6 %all-gather.2.cloned.1.call-start = ((), (), s32[]{:S(2)}) async-start(), calls=%async_computation.5 | async-start | bytes 11796480 | tf_op jit(solution)/shard_map/all_gather | solution.py:87
  8.6 3.0 %copy-start.19 = (s32[4,2]{0,1:T(2,128)S(1)}, s32[4,2]{0,1:T(2,128)}, u32[]{:S(2)}) copy-start(s32[4,2]{0,1:T(2,128)} %param.8) | copy-start | bytes 100
  8.6 3.2 %copy-start.20 = (f32[4,2]{0,1:T(2,128)S(1)}, f32[4,2]{0,1:T(2,128)}, u32[]{:S(2)}) copy-start(f32[4,2]{0,1:T(2,128)} %param.9) | copy-start | bytes 100
  8.6 3.4 %copy-start.3 = (bf16[4,3072]{1,0:T(4,128)(2,1)S(1)}, bf16[4,3072]{1,0:T(4,128)(2,1)}, u32[]{:S(2)}) copy-start(bf16[4,3072]{1,0:T(4,128)(2,1)} %param.13) | copy-start | bytes 73732
  8.7 3.4 %copy-start.4 = (bf16[4,3072]{1,0:T(4,128)(2,1)S(1)}, bf16[4,3072]{1,0:T(4,128)(2,1)}, u32[]{:S(2)}) copy-start(bf16[4,3072]{1,0:T(4,128)(2,1)} %param.7) | copy-start | bytes 73732
  71.6 36.2 %all-to-all-start.1 = ((bf16[4,64,6272]{2,1,0:T(8,128)(2,1)}), bf16[4,64,6272]{2,1,0:T(8,128)(2,1)S(1)}, u32[]{:S(2)}, u32[]{:S(2)}) async-start(bf16[4,64,6272]{2,1,0:T(8,128)(2,1)} %broadcast_in_dim.8), calls=%async_computation.1 | async-start | bytes 6422528 | tf_op jit(solution)/shard_map/all_to_all | solution.py:46
  76.0 161.9 %reduce-scatter.2.cloned.1.call-start = ((), (), s32[]{:S(2)}) async-start(), calls=%async_computation.6 | async-start | bytes 3932160 | tf_op jit(solution)/shard_map/reduce_scatter | solution.py:145
  76.0 54.5 %copy-start.5 = (pred[256]{0:T(512)(128)(4,1)}, pred[256]{0:T(512)(128)(4,1)S(1)}, u32[]{:S(2)}) copy-start(pred[256]{0:T(512)(128)(4,1)S(1)} %compare_and_fusion.1) | copy-start | bytes 772
  76.0 54.5 %copy-start.7 = (s32[128]{0:T(128)}, s32[128]{0:T(128)S(1)}, u32[]{:S(2)}) copy-start(s32[128]{0:T(128)S(1)} %get-tuple-element.35) | copy-start | bytes 1540
  76.1 54.5 %copy-start.9 = (s32[128]{0:T(128)}, s32[128]{0:T(128)S(1)}, u32[]{:S(2)}) copy-start(s32[128]{0:T(128)S(1)} %get-tuple-element.36) | copy-start | bytes 1540
  76.1 54.5 %copy-start.11 = (s32[128]{0:T(128)}, s32[128]{0:T(128)S(1)}, u32[]{:S(2)}) copy-start(s32[128]{0:T(128)S(1)} %get-tuple-element.37) | copy-start | bytes 1540
  76.1 54.5 %copy-start.13 = (s32[128]{0:T(128)}, s32[128]{0:T(128)S(1)}, u32[]{:S(2)}) copy-start(s32[128]{0:T(128)S(1)} %get-tuple-element.38) | copy-start | bytes 1540
  76.1 54.5 %copy-start.15 = (pred[128]{0:T(512)(128)(4,1)}, pred[128]{0:T(512)(128)(4,1)S(1)}, u32[]{:S(2)}) copy-start(pred[128]{0:T(512)(128)(4,1)S(1)} %get-tuple-element.31) | copy-start | bytes 388
  76.1 54.5 %copy-start.17 = (pred[128]{0:T(512)(128)(4,1)}, pred[128]{0:T(512)(128)(4,1)S(1)}, u32[]{:S(2)}) copy-start(pred[128]{0:T(512)(128)(4,1)S(1)} %get-tuple-element.32) | copy-start | bytes 388
  110.0 5.7 %collective-permute-start = (bf16[128,6272]{1,0:T(8,128)(2,1)}, bf16[128,6272]{1,0:T(8,128)(2,1)}, u32[]{:S(2)}, u32[]{:S(2)}) collective-permute-start(bf16[128,6272]{1,0:T(8,128)(2,1)} %convolution_convert_fusion), channel_id=1, source_target_pairs={{0,16},{16,0},{1,17},{17,1},{2,18},{18,2},{3,19},{19,3},{4,20},{20... | collective-permute-start | bytes 4816904 | tf_op jit(solution)/shard_map/ppermute | solution.py:101
  123.0 5.2 %copy-start.1 = (bf16[128,6272]{1,0:T(8,128)(2,1)S(1)}, bf16[128,6272]{1,0:T(8,128)(2,1)}, u32[]{:S(2)}) copy-start(bf16[128,6272]{1,0:T(8,128)(2,1)} %copy-done) | copy-start | bytes 4816900
  126.2 4.4 %collective-permute-start.1 = (bf16[128,3072]{1,0:T(8,128)(2,1)S(1)}, bf16[128,3072]{1,0:T(8,128)(2,1)S(1)}, u32[]{:S(2)}, u32[]{:S(2)}) collective-permute-start(bf16[128,3072]{1,0:T(8,128)(2,1)S(1)} %slice.121), channel_id=1, source_target_pairs={{0,16},{16,0},{1,17},{17,1},{2,18},{18,2},{3,19},{19,3},{4,20},{20... | collective-permute-start | bytes 2359304 | tf_op jit(solution)/shard_map/ppermute | solution.py:114
  135.1 19.4 %collective-permute-start.8 = (bf16[64,3072]{1,0:T(8,128)(2,1)S(1)}, bf16[64,3072]{1,0:T(8,128)(2,1)S(1)}, u32[]{:S(2)}, u32[]{:S(2)}) collective-permute-start(bf16[64,3072]{1,0:T(8,128)(2,1)S(1)} %get-tuple-element.20), channel_id=1, source_target_pairs={{0,3},{1,0},{2,1},{3,2},{4,7},{5,4},{6,5},{7,6},{8,11},{9,8},{10,9... | collective-permute-start | bytes 1179656 | tf_op jit(solution)/shard_map/ppermute | solution.py:67
  138.2 16.3 %collective-permute-start.7 = (bf16[64,3072]{1,0:T(8,128)(2,1)S(1)}, bf16[64,3072]{1,0:T(8,128)(2,1)S(1)}, u32[]{:S(2)}, u32[]{:S(2)}) collective-permute-start(bf16[64,3072]{1,0:T(8,128)(2,1)S(1)} %get-tuple-element.21), channel_id=1, source_target_pairs={{0,2},{1,3},{2,0},{3,1},{4,6},{5,7},{6,4},{7,5},{8,10},{9,11},{10,... | collective-permute-start | bytes 1179656 | tf_op jit(solution)/shard_map/ppermute | solution.py:67
  141.6 19.5 %collective-permute-start.6 = (bf16[64,3072]{1,0:T(8,128)(2,1)S(1)}, bf16[64,3072]{1,0:T(8,128)(2,1)S(1)}, u32[]{:S(2)}, u32[]{:S(2)}) collective-permute-start(bf16[64,3072]{1,0:T(8,128)(2,1)S(1)} %get-tuple-element.19), channel_id=1, source_target_pairs={{0,1},{1,2},{2,3},{3,0},{4,5},{5,6},{6,7},{7,4},{8,9},{9,10},{10,1... | collective-permute-start | bytes 1179656 | tf_op jit(solution)/shard_map/ppermute | solution.py:67
  152.6 23.2 %collective-permute-start.2 = (bf16[128,3072]{1,0:T(8,128)(2,1)}, bf16[128,3072]{1,0:T(8,128)(2,1)}, u32[]{:S(2)}, u32[]{:S(2)}) collective-permute-start(bf16[128,3072]{1,0:T(8,128)(2,1)} %slice.123), channel_id=1, source_target_pairs={{0,16},{16,0},{1,17},{17,1},{2,18},{18,2},{3,19},{19,3},{4,20},{20... | collective-permute-start | bytes 2359304 | tf_op jit(solution)/shard_map/ppermute | solution.py:114
  161.4 14.4 %copy-start.6 = (pred[256]{0:T(512)(128)(4,1)S(1)}, pred[256]{0:T(512)(128)(4,1)}, u32[]{:S(2)}) copy-start(pred[256]{0:T(512)(128)(4,1)} %copy-done.5) | copy-start | bytes 772
  161.4 14.4 %copy-start.8 = (s32[128]{0:T(128)S(1)}, s32[128]{0:T(128)}, u32[]{:S(2)}) copy-start(s32[128]{0:T(128)} %copy-done.7) | copy-start | bytes 1540
  161.4 14.4 %copy-start.10 = (s32[128]{0:T(128)S(1)}, s32[128]{0:T(128)}, u32[]{:S(2)}) copy-start(s32[128]{0:T(128)} %copy-done.9) | copy-start | bytes 1540
  161.4 14.4 %copy-start.12 = (s32[128]{0:T(128)S(1)}, s32[128]{0:T(128)}, u32[]{:S(2)}) copy-start(s32[128]{0:T(128)} %copy-done.11) | copy-start | bytes 1540
  161.4 14.4 %copy-start.14 = (s32[128]{0:T(128)S(1)}, s32[128]{0:T(128)}, u32[]{:S(2)}) copy-start(s32[128]{0:T(128)} %copy-done.13) | copy-start | bytes 1540
  161.4 14.4 %copy-start.16 = (pred[128]{0:T(512)(128)(4,1)S(1)}, pred[128]{0:T(512)(128)(4,1)}, u32[]{:S(2)}) copy-start(pred[128]{0:T(512)(128)(4,1)} %copy-done.15) | copy-start | bytes 388
  161.4 14.4 %copy-start.18 = (pred[128]{0:T(512)(128)(4,1)S(1)}, pred[128]{0:T(512)(128)(4,1)}, u32[]{:S(2)}) copy-start(pred[128]{0:T(512)(128)(4,1)} %copy-done.17) | copy-start | bytes 388
  162.4 36.3 %all-to-all-start.2 = ((bf16[16,4,3072]{2,1,0:T(4,128)(2,1)}), bf16[16,4,3072]{2,1,0:T(4,128)(2,1)S(1)}, u32[]{:S(2)}, u32[]{:S(2)}) async-start(bf16[16,4,3072]{2,1,0:T(4,128)(2,1)} %reshape.67), calls=%async_computation.2 | async-start | bytes 786432 | tf_op jit(solution)/shard_map/all_to_all | solution.py:53
  177.8 22.4 %collective-permute-start.3 = (bf16[64,3072]{1,0:T(8,128)(2,1)S(1)}, bf16[64,3072]{1,0:T(8,128)(2,1)S(1)}, u32[]{:S(2)}, u32[]{:S(2)}) collective-permute-start(bf16[64,3072]{1,0:T(8,128)(2,1)S(1)} %get-tuple-element.24), channel_id=1, source_target_pairs={{0,1},{1,2},{2,3},{3,0},{4,5},{5,6},{6,7},{7,4},{8,9},{9,10},{10,1... | collective-permute-start | bytes 1179656 | tf_op jit(solution)/shard_map/ppermute | solution.py:67
  179.8 20.5 %collective-permute-start.4 = (bf16[64,3072]{1,0:T(8,128)(2,1)S(1)}, bf16[64,3072]{1,0:T(8,128)(2,1)S(1)}, u32[]{:S(2)}, u32[]{:S(2)}) collective-permute-start(bf16[64,3072]{1,0:T(8,128)(2,1)S(1)} %get-tuple-element.23), channel_id=1, source_target_pairs={{0,2},{1,3},{2,0},{3,1},{4,6},{5,7},{6,4},{7,5},{8,10},{9,11},{10,... | collective-permute-start | bytes 1179656 | tf_op jit(solution)/shard_map/ppermute | solution.py:67
  183.7 19.0 %collective-permute-start.5 = (bf16[64,3072]{1,0:T(8,128)(2,1)S(1)}, bf16[64,3072]{1,0:T(8,128)(2,1)S(1)}, u32[]{:S(2)}, u32[]{:S(2)}) collective-permute-start(bf16[64,3072]{1,0:T(8,128)(2,1)S(1)} %get-tuple-element.22), channel_id=1, source_target_pairs={{0,3},{1,0},{2,1},{3,2},{4,7},{5,4},{6,5},{7,6},{8,11},{9,8},{10,9... | collective-permute-start | bytes 1179656 | tf_op jit(solution)/shard_map/ppermute | solution.py:67
  (2 other events, 3.9 us)
Sparse Core Ops, SparseCore 0:
  11.8 102.8 all-gather.1
  135.1 44.1 reduce-scatter.1

commit v3 on v2

--- a/solution.py
+++ b/solution.py
@@ -31,11 +31,9 @@
     return jnp.pad(columns, ((0, 0), (0, META - columns.shape[1])))
 
 
-def slot_table(code, expert, block):
-    count = code.shape[0]
-    slots = count // block * CAP
-    token = lax.broadcasted_iota(jnp.int32, (count, slots), 0)
-    slot = lax.broadcasted_iota(jnp.int32, (count, slots), 1)
+def slot_table(code, token, expert, block):
+    slots = code.shape[0] // block * CAP
+    slot = lax.broadcasted_iota(jnp.int32, (1, slots), 1)
     wanted = expert * CAP + slot % CAP
     hit = (code[:, 0:1] == wanted) | (code[:, 1:2] == wanted)
     return (hit & (token // block == slot // CAP)).astype(BF16)
@@ -72,34 +70,67 @@
     return sum(part.astype(F32) for part in parts).astype(BF16)
 
 
+def pass_on(x, axis, shift):
+    size = lax.axis_size(axis)
+    return lax.ppermute(x, axis, [(i, (i + shift) % size) for i in range(size)])
+
+
+def roll_columns(x, start):
+    return lax.dynamic_slice_in_dim(jnp.concatenate([x, x], axis=1), start, x.shape[1], axis=1)
+
+
 def on_device(tokens, expert_ids, gate_probs, gate_weight, up_weight, down_weight, cotangent):
     block, width = tokens.shape
+    ff = gate_weight.shape[2]
     quarter = down_weight.shape[2]
     quarters = width // quarter
-    y_size = lax.axis_size("y")
-    z_size = lax.axis_size("zh") * lax.axis_size("zl")
+    y_size, low_size, high_size = (lax.axis_size(name) for name in ("y", "zl", "zh"))
+    group = lax.axis_index("x")
     core = lax.axis_index("c")
     expert = lax.axis_index("zl") * 2 + core
     other = lax.axis_index("zl") * 2 + 1 - core
 
-    mine = jnp.concatenate([gate_weight[0], up_weight[0], down_weight[0].T], axis=1)
+    def columns(x, q):
+        return x[:, q * quarter : (q + 1) * quarter]
+
+    mine = jnp.concatenate([gate_weight[0], up_weight[0]], axis=1)
     mine = with_layout_constraint(mine, Layout(major_to_minor=(0, 1)))
-    weights = lax.all_gather(mine, "x", axis=0, tiled=True)
-    ff = gate_weight.shape[2]
-    full_both, full_down = weights[:, : 2 * ff], weights[:, 2 * ff :]
-
-    packed = jnp.concatenate([tokens, cotangent, meta_columns(expert_ids, gate_probs)], axis=1)
-    by_z = gather_by_exchange(packed, ("zh", "zl"), z_size)
-    plane = gather_by_exchange(by_z, "y", y_size)
-
+    own_down, mine = lax.optimization_barrier((down_weight[0], mine))
+    full_both = lax.all_gather(mine, "x", axis=0, tiled=True)
+    from_next = pass_on(own_down, "x", -1)
+    from_last = pass_on(own_down, "x", 1)
+
+    turned = roll_columns(cotangent, group * quarter)
+    packed = jnp.concatenate([tokens, turned, meta_columns(expert_ids, gate_probs)], axis=1)
+    by_z = lax.all_gather(packed[None], ("zh", "zl"), axis=0, tiled=True)
+    by_z, from_next, from_last = lax.optimization_barrier((by_z, from_next, from_last))
+    plane = gather_by_exchange(by_z.reshape(-1, packed.shape[1]), "y", y_size)
+    if quarters == 4:
+        across = pass_on(from_next[: ff // 2], "x", -1), pass_on(from_last[ff // 2 :], "x", 1)
+        plane, across = lax.optimization_barrier((plane, across))
+        downs = [own_down, from_next, jnp.concatenate(across, axis=0), from_last]
+    else:
+        downs = [own_down, from_next]
+
+    count = plane.shape[0]
     code = plane[:, 2 * width : 2 * width + 2].astype(jnp.int32)
-    table_own = slot_table(code, expert, block)
-    table_other = slot_table(code, other, block)
+    place = lax.broadcasted_iota(jnp.int32, (count, 1), 0)
+    table_own = slot_table(code, place, expert, block)
+    table_other = slot_table(code, place, other, block)
     half = table_own.shape[1]
     rows_own = dot(table_own, plane, FIRST).astype(BF16)
     rows_other = dot(table_other, plane, FIRST).astype(BF16)
     rows_arrived = lax.ppermute(rows_other, "c", [(0, 1), (1, 0)])
     rows = jnp.concatenate([rows_own, rows_arrived], axis=0)
+
+    def low_first(x):
+        split = x.reshape(y_size, high_size, low_size, block, x.shape[1])
+        return split.transpose(0, 2, 1, 3, 4).reshape(x.shape)
+
+    code_back = low_first(code)
+    place_back = low_first(place)
+    back_own = slot_table(code_back, place_back, expert, block)
+    back_other = slot_table(code_back, place_back, other, block)
 
     about = rows[:, 2 * width :].astype(F32)
     slot = lax.broadcasted_iota(jnp.int32, (2 * half, 1), 0)
@@ -112,10 +143,7 @@
 
     def leave(part):
         returned = lax.ppermute(part[half:], "c", [(0, 1), (1, 0)])
-        return (dot(table_own, part[:half]) + dot(table_other, returned)).astype(BF16)
-
-    def along_z(parts):
-        return scatter_sum_by_exchange(add_up(parts), ("zh", "zl"), z_size)
+        return (dot(back_own, part[:half]) + dot(back_other, returned)).astype(BF16)
 
     gate_up = dot(token_rows, full_both)
     gate_pre, up_pre = gate_up[:, :ff], gate_up[:, ff:]
@@ -123,29 +151,33 @@
     activated = gate_pre * sigmoid_gate
     slope_gate = sigmoid_gate * (1.0 + gate_pre * (1.0 - sigmoid_gate))
     hidden = (activated * up_pre).astype(BF16)
-    out_part = (prob * dot(hidden, full_down, LAST)).astype(BF16)
+    out_part = jnp.concatenate([(prob * dot(hidden, down)).astype(BF16) for down in downs], axis=1)
     out_tokens = leave(out_part)
     out_parts = send_by_shifts(out_tokens, "y", y_size)
 
-    late_hidden, late_cot, _ = lax.optimization_barrier((hidden, cot_rows, out_tokens))
-    grad_hidden = dot(late_cot, full_down)
+    late_hidden, _ = lax.optimization_barrier((hidden, out_part))
+    late_cot, _ = lax.optimization_barrier((cot_rows, out_tokens))
+    grad_hidden = sum(dot(columns(late_cot, s), downs[s], LAST) for s in range(quarters))
     grad_up = (grad_hidden * activated).astype(BF16)
     grad_gate = (grad_hidden * up_pre * slope_gate).astype(BF16)
     grad_both = jnp.concatenate([grad_gate, grad_up], axis=1)
     grad_tokens = leave(dot(grad_both, full_both, LAST).astype(BF16))
-
     grad_parts = send_by_shifts(grad_tokens, "y", y_size)
 
-    partial_down = jnp.stack(
-        [
-            dot(late_hidden, late_cot[:, q * quarter : (q + 1) * quarter], FIRST).astype(BF16)
-            for q in range(quarters)
-        ]
-    )
-    down_grads = lax.psum_scatter(partial_down, "x", scatter_dimension=0)[None]
-    layer_out = along_z(out_parts)
-    grad_parts, layer_out = lax.optimization_barrier((grad_parts, layer_out))
-    return layer_out, along_z(grad_parts), down_grads
+    partial_down = []
+    for q in range(quarters):
+        start = lax.rem(q - group + quarters, quarters) * quarter
+        block_q = lax.dynamic_slice_in_dim(cot_rows, start, quarter, axis=1)
+        partial_down.append(dot(late_hidden, block_q, FIRST).astype(BF16))
+    down_grads = lax.psum_scatter(jnp.stack(partial_down), "x", scatter_dimension=0)[None]
+
+    out_y, grad_tokens = lax.optimization_barrier((add_up(out_parts), grad_tokens))
+    out_low = scatter_sum_by_exchange(out_y, "zl", low_size)
+    grad_low = scatter_sum_by_exchange(add_up(grad_parts), "zl", low_size)
+    low = jnp.concatenate([out_low, grad_low], axis=1)
+    own = scatter_sum_by_exchange(low, "zh", high_size)
+    turn_back = lax.rem(quarters - group, quarters) * quarter
+    return roll_columns(own[:, :width], turn_back), own[:, width:], down_grads
 
 
 def finer(mesh):

time: 248 us -> 238 us (0.960)
  blocking collectives: 91.2 us -> 37.4 us
  waiting for transfers between devices: 55.6 us -> 75.4 us
  starting transfers between devices: 40.6 us -> 59.5 us
  local copies, waits for them, and re-layouts: 7.44 us -> 15.1 us
    all_to_all x2 -> x0, blocking collectives: 91.2 us -> none  [the longest x1 57.2 us: gather_by_exchange(): lax.all_to_all(spread, axes, split_axis=0, concat_axis=0, tiled=True)]
    all_gather x0 -> x1, blocking collectives: none -> 37.4 us  [on_device(): by_z = lax.all_gather(packed[None], ('zh', 'zl'), axis=0, tiled=True)]
    all_to_all x1, waiting for transfers between devices: 31.6 us -> 6.83 us  [gather_by_exchange(): lax.all_to_all(spread, axes, split_axis=0, concat_axis=0, tiled=True)]
    ppermute x0 -> x4, starting transfers between devices: none -> 16.7 us  [pass_on(): return lax.ppermute(x, axis, [(i, (i + shift) % size) for i in range(size)])]
    ppermute x6, waiting for transfers between devices: 9.99 us -> 26 us  [send_by_shifts(): parts.append(lax.ppermute(block(shift), axis, pairs))]
    ppermute x0 -> x4, waiting for transfers between devices: none -> 16 us  [pass_on(): return lax.ppermute(x, axis, [(i, (i + shift) % size) for i in range(size)])]
    all_to_all x1 -> x3, waiting for transfers between devices: 11 us -> 26.5 us  [scatter_sum_by_exchange(): parts = lax.all_to_all(parts, axes, split_axis=0, concat_axis=0, tiled=True)]
    slice x0 -> x3, local copies, waits for them, and re-layouts: none -> 4.19 us  [the longest x1 1.8 us: on_device(): from_last[ff // 2:]]
  transfers between devices with their start and end apart: 13 -> 19, of which waited for: 6 -> 10; matrix products, arithmetic and copies ran while one was open for 10% -> 14% of each run, Pallas kernels for 0% -> 0%
where the time goes in v3:
time: 238 us; the launch traced here: 237 us
  waiting for transfers between devices  75.4 us (32%)
  starting transfers between devices  59.5 us (25%)
  blocking collectives  37.4 us (16%)
  matrix products  23.5 us (10%)
  local copies, waits for them, and re-layouts  15.1 us (6%)
  between operations  14.8 us (6%)
  other arithmetic  11.2 us (5%)
    all_gather x1, blocking collectives, on_device(): by_z = lax.all_gather(packed[None], ('zh', 'zl'), axis=0, tiled=True)  37.4 us
    all_to_all x3, waiting for transfers between devices, scatter_sum_by_exchange(): parts = lax.all_to_all(parts, axes, split_axis=0, concat_axis=0, tiled=True)  26.5 us
    ppermute x6, waiting for transfers between devices, send_by_shifts(): parts.append(lax.ppermute(block(shift), axis, pairs))  26 us
    dot_general x20, matrix products, dot(): return lax.dot_general(a, b, dims, preferred_element_type=F32)  23.5 us
    ppermute x6, starting transfers between devices, send_by_shifts(): parts.append(lax.ppermute(block(shift), axis, pairs))  17.2 us
    ppermute x4, starting transfers between devices, pass_on(): return lax.ppermute(x, axis, [(i, (i + shift) % size) for i in range(size)])  16.7 us
    ppermute x4, waiting for transfers between devices, pass_on(): return lax.ppermute(x, axis, [(i, (i + shift) % size) for i in range(size)])  16 us
    all_to_all x3, starting transfers between devices, scatter_sum_by_exchange(): parts = lax.all_to_all(parts, axes, split_axis=0, concat_axis=0, tiled=True)  14.8 us
  transfers between devices with their start and end apart: 19, of which 10 were waited for; matrix products, arithmetic and copies ran while one was open for 14% of the time, Pallas kernels for 0%

profile of v3, /device:TPU:6, one launch (start us, length us, event | category | flops | bytes accessed | tf_op | source)
XLA Modules:
  0.0 236.8 jit_solution(10882492606290327445)
XLA Ops:
  7.3 2.8 %pad_maximum_fusion.2 = bf16[768,1024]{1,0:T(8,128)(2,1)} fusion(bf16[768,512]{1,0:T(8,128)(2,1)} %bitcast.56, bf16[768,512]{1,0:T(8,128)(2,1)} %bitcast.57), kind=kLoop, calls=%fused_computation.14 | loop fusion | flops 3145728 | bytes 3145728 | tf_op jit(solution)/shard_map/concatenate | solution.py:96
  10.1 2.7 %collective-permute-start = (bf16[512,768]{1,0:T(8,128)(2,1)S(1)}, bf16[512,768]{1,0:T(8,128)(2,1)S(1)}, u32[]{:S(2)}, u32[]{:S(2)}) collective-permute-start(bf16[512,768]{1,0:T(8,128)(2,1)S(1)} %bitcast.51), channel_id=1, source_target_pairs={{0,384},{128,0},{256,128},{384,256},{1,385},{129,1},{257,129},{385... | collective-permute-start | bytes 2359304 | tf_op jit(solution)/shard_map/ppermute | solution.py:75
  12.9 6.9 %collective-permute-start.1 = (bf16[512,768]{1,0:T(8,128)(2,1)S(1)}, bf16[512,768]{1,0:T(8,128)(2,1)}, u32[]{:S(2)}, u32[]{:S(2)}) collective-permute-start(bf16[512,768]{1,0:T(8,128)(2,1)S(1)} %bitcast.52), channel_id=1, source_target_pairs={{0,128},{128,256},{256,384},{384,0},{1,129},{129,257},{257,385},{3... | collective-permute-start | bytes 2359304 | tf_op jit(solution)/shard_map/ppermute | solution.py:75
  20.4 37.4 %all-gather.1 = bf16[16,4,6272]{2,1,0:T(4,128)(2,1)S(1)} all-gather(bf16[1,4,6272]{2,1,0:T(4,128)(2,1)S(1)} %fusion.56), channel_id=2, replica_groups=mesh['x'=4,'zl'=4,'c'=2,'zh'=4,'y'=4] {'zh','zl'}, dimensions={0}, use_global_device_ids=true | all-gather | bytes 852992 | tf_op jit(solution)/shard_map/all_gather | solution.py:105
  57.9 1.9 broadcast_in_dim.16
  59.9 4.5 %all-to-all-start = ((bf16[4,64,6272]{2,1,0:T(8,128)(2,1)}), bf16[4,64,6272]{2,1,0:T(8,128)(2,1)S(1)}, u32[]{:S(2)}, u32[]{:S(2)}) async-start(bf16[4,64,6272]{2,1,0:T(8,128)(2,1)} %broadcast_in_dim.16), calls=%async_computation | async-start | bytes 6422528 | tf_op jit(solution)/shard_map/all_to_all | solution.py:44
  69.8 5.1 %collective-permute-start.3 = (bf16[256,768]{1,0:T(8,128)(2,1)}, bf16[256,768]{1,0:T(8,128)(2,1)}, u32[]{:S(2)}, u32[]{:S(2)}) collective-permute-start(bf16[256,768]{1,0:T(8,128)(2,1)} %slice.92), channel_id=1, source_target_pairs={{0,128},{128,256},{256,384},{384,0},{1,129},{129,257},{257,385},{3... | collective-permute-start | bytes 1179656 | tf_op jit(solution)/shard_map/ppermute | solution.py:75
  75.0 12.8 %collective-permute-done.2 = bf16[256,768]{1,0:T(8,128)(2,1)} collective-permute-done((bf16[256,768]{1,0:T(8,128)(2,1)}, bf16[256,768]{1,0:T(8,128)(2,1)}, u32[]{:S(2)}, u32[]{:S(2)}) %collective-permute-start.2) | collective-permute-done | bytes 393248 | tf_op jit(solution)/shard_map/ppermute | solution.py:75
  87.8 3.1 %collective-permute-done.3 = bf16[256,768]{1,0:T(8,128)(2,1)} collective-permute-done((bf16[256,768]{1,0:T(8,128)(2,1)}, bf16[256,768]{1,0:T(8,128)(2,1)}, u32[]{:S(2)}, u32[]{:S(2)}) %collective-permute-start.3) | collective-permute-done | bytes 393248 | tf_op jit(solution)/shard_map/ppermute | solution.py:75
  91.0 6.8 %all-to-all-done = bf16[4,64,6272]{2,1,0:T(8,128)(2,1)S(1)} async-done(((bf16[4,64,6272]{2,1,0:T(8,128)(2,1)}), bf16[4,64,6272]{2,1,0:T(8,128)(2,1)S(1)}, u32[]{:S(2)}, u32[]{:S(2)}) %all-to-all-start) | async-done | bytes 3211296 | tf_op jit(solution)/shard_map/all_to_all | solution.py:44
  98.0 2.0 convolution_convert_fusion
  109.4 5.1 %fusion.2 = f32[256,1024]{1,0:T(8,128)S(1)} fusion(bf16[3072,1024]{1,0:T(8,128)(2,1)} %all-gather.4.cloned.1.call-done, bf16[128,6272]{1,0:T(8,128)(2,1)} %collective-permute-done.4, bf16[128,6272]{1,0:T(8,128)(2,1)} %copy-done), kind=kOutput, calls=%fused_computation.10 | convolution fusion | flops 1613758464 | bytes 10551296 | tf_op jit(solution)/shard_map/dot_general | solution.py:17
  120.0 2.4 %collective-permute-start.5 = (bf16[128,3072]{1,0:T(8,128)(2,1)}, bf16[128,3072]{1,0:T(8,128)(2,1)}, u32[]{:S(2)}, u32[]{:S(2)}) collective-permute-start(bf16[128,3072]{1,0:T(8,128)(2,1)} %slice.134), channel_id=1, source_target_pairs={{0,16},{16,0},{1,17},{17,1},{2,18},{18,2},{3,19},{19,3},{4,20},{20... | collective-permute-start | bytes 2359304 | tf_op jit(solution)/shard_map/ppermute | solution.py:145
  124.0 1.9 pad_maximum_fusion
  133.1 3.1 %collective-permute-start.8 = (bf16[64,3072]{1,0:T(8,128)(2,1)S(1)}, bf16[64,3072]{1,0:T(8,128)(2,1)S(1)}, u32[]{:S(2)}, u32[]{:S(2)}) collective-permute-start(bf16[64,3072]{1,0:T(8,128)(2,1)S(1)} %get-tuple-element.28), channel_id=1, source_target_pairs={{0,3},{1,0},{2,1},{3,2},{4,7},{5,4},{6,5},{7,6},{8,11},{9,8},{10,9... | collective-permute-start | bytes 1179656 | tf_op jit(solution)/shard_map/ppermute | solution.py:65
  136.1 3.4 %collective-permute-start.7 = (bf16[64,3072]{1,0:T(8,128)(2,1)S(1)}, bf16[64,3072]{1,0:T(8,128)(2,1)S(1)}, u32[]{:S(2)}, u32[]{:S(2)}) collective-permute-start(bf16[64,3072]{1,0:T(8,128)(2,1)S(1)} %get-tuple-element.29), channel_id=1, source_target_pairs={{0,2},{1,3},{2,0},{3,1},{4,6},{5,7},{6,4},{7,5},{8,10},{9,11},{10,... | collective-permute-start | bytes 1179656 | tf_op jit(solution)/shard_map/ppermute | solution.py:65
  139.5 2.1 collective-permute-start.6
  141.6 4.7 %convolution_convert_fusion.2 = bf16[256,3072]{1,0:T(8,128)(2,1)S(1)} fusion(bf16[3072,1024]{1,0:T(8,128)(2,1)} %all-gather.4.cloned.1.call-done, bf16[256,512]{1,0:T(8,128)(2,1)S(1)} %get-tuple-element.34, bf16[256,512]{1,0:T(8,128)(2,1)S(1)} %get-tuple-element.33), kind=kOutput, calls=%fused_computation.6 | convolution fusion | flops 1612447744 | bytes 8388608 | tf_op jit(solution)/shard_map/dot_general | solution.py:17
  146.4 1.9 collective-permute-start.9
  149.0 2.6 %collective-permute-done.7 = bf16[64,3072]{1,0:T(8,128)(2,1)S(1)} collective-permute-done((bf16[64,3072]{1,0:T(8,128)(2,1)S(1)}, bf16[64,3072]{1,0:T(8,128)(2,1)S(1)}, u32[]{:S(2)}, u32[]{:S(2)}) %collective-permute-start.7) | collective-permute-done | bytes 393248 | tf_op jit(solution)/shard_map/ppermute | solution.py:65
  151.6 7.1 %collective-permute-done.6 = bf16[64,3072]{1,0:T(8,128)(2,1)S(1)} collective-permute-done((bf16[64,3072]{1,0:T(8,128)(2,1)S(1)}, bf16[64,3072]{1,0:T(8,128)(2,1)S(1)}, u32[]{:S(2)}, u32[]{:S(2)}) %collective-permute-start.6) | collective-permute-done | bytes 393248 | tf_op jit(solution)/shard_map/ppermute | solution.py:65
  160.3 3.5 %all-to-all-start.1 = ((bf16[4,16,3072]{2,1,0:T(8,128)(2,1)}), bf16[4,16,3072]{2,1,0:T(8,128)(2,1)S(1)}, u32[]{:S(2)}, u32[]{:S(2)}) async-start(bf16[4,16,3072]{2,1,0:T(8,128)(2,1)} %bitcast.10), calls=%async_computation.1 | async-start | bytes 786432 | tf_op jit(solution)/shard_map/all_to_all | solution.py:51
  163.9 2.5 %collective-permute-start.12 = (bf16[64,3072]{1,0:T(8,128)(2,1)S(1)}, bf16[64,3072]{1,0:T(8,128)(2,1)S(1)}, u32[]{:S(2)}, u32[]{:S(2)}) collective-permute-start(bf16[64,3072]{1,0:T(8,128)(2,1)S(1)} %get-tuple-element.31), channel_id=1, source_target_pairs={{0,3},{1,0},{2,1},{3,2},{4,7},{5,4},{6,5},{7,6},{8,11},{9,8},{10,9... | collective-permute-start | bytes 1179656 | tf_op jit(solution)/shard_map/ppermute | solution.py:65
  166.4 3.4 %collective-permute-start.11 = (bf16[64,3072]{1,0:T(8,128)(2,1)S(1)}, bf16[64,3072]{1,0:T(8,128)(2,1)S(1)}, u32[]{:S(2)}, u32[]{:S(2)}) collective-permute-start(bf16[64,3072]{1,0:T(8,128)(2,1)S(1)} %get-tuple-element.32), channel_id=1, source_target_pairs={{0,2},{1,3},{2,0},{3,1},{4,6},{5,7},{6,4},{7,5},{8,10},{9,11},{10,... | collective-permute-start | bytes 1179656 | tf_op jit(solution)/shard_map/ppermute | solution.py:65
  169.8 2.7 %collective-permute-start.10 = (bf16[64,3072]{1,0:T(8,128)(2,1)S(1)}, bf16[64,3072]{1,0:T(8,128)(2,1)S(1)}, u32[]{:S(2)}, u32[]{:S(2)}) collective-permute-start(bf16[64,3072]{1,0:T(8,128)(2,1)S(1)} %get-tuple-element.30), channel_id=1, source_target_pairs={{0,1},{1,2},{2,3},{3,0},{4,5},{5,6},{6,7},{7,4},{8,9},{9,10},{10,1... | collective-permute-start | bytes 1179656 | tf_op jit(solution)/shard_map/ppermute | solution.py:65
  172.5 5.2 %collective-permute-done.12 = bf16[64,3072]{1,0:T(8,128)(2,1)S(1)} collective-permute-done((bf16[64,3072]{1,0:T(8,128)(2,1)S(1)}, bf16[64,3072]{1,0:T(8,128)(2,1)S(1)}, u32[]{:S(2)}, u32[]{:S(2)}) %collective-permute-start.12) | collective-permute-done | bytes 393248 | tf_op jit(solution)/shard_map/ppermute | solution.py:65
  177.7 4.2 %collective-permute-done.11 = bf16[64,3072]{1,0:T(8,128)(2,1)S(1)} collective-permute-done((bf16[64,3072]{1,0:T(8,128)(2,1)S(1)}, bf16[64,3072]{1,0:T(8,128)(2,1)S(1)}, u32[]{:S(2)}, u32[]{:S(2)}) %collective-permute-start.11) | collective-permute-done | bytes 393248 | tf_op jit(solution)/shard_map/ppermute | solution.py:65
  181.9 6.9 %collective-permute-done.10 = bf16[64,3072]{1,0:T(8,128)(2,1)S(1)} collective-permute-done((bf16[64,3072]{1,0:T(8,128)(2,1)S(1)}, bf16[64,3072]{1,0:T(8,128)(2,1)S(1)}, u32[]{:S(2)}, u32[]{:S(2)}) %collective-permute-start.10) | collective-permute-done | bytes 393248 | tf_op jit(solution)/shard_map/ppermute | solution.py:65
  189.7 4.8 %all-to-all-start.2 = ((bf16[4,16,3072]{2,1,0:T(8,128)(2,1)}), bf16[4,16,3072]{2,1,0:T(8,128)(2,1)S(1)}, u32[]{:S(2)}, u32[]{:S(2)}) async-start(bf16[4,16,3072]{2,1,0:T(8,128)(2,1)} %bitcast.11), calls=%async_computation.2 | async-start | bytes 786432 | tf_op jit(solution)/shard_map/all_to_all | solution.py:51
  194.6 11.8 %all-to-all-done.2 = bf16[4,16,3072]{2,1,0:T(8,128)(2,1)S(1)} async-done(((bf16[4,16,3072]{2,1,0:T(8,128)(2,1)}), bf16[4,16,3072]{2,1,0:T(8,128)(2,1)S(1)}, u32[]{:S(2)}, u32[]{:S(2)}) %all-to-all-start.2) | async-done | bytes 393248 | tf_op jit(solution)/shard_map/all_to_all | solution.py:51
  207.2 6.6 %all-to-all-start.3 = ((bf16[4,4,6144]{2,1,0:T(4,128)(2,1)}), bf16[4,4,6144]{2,1,0:T(4,128)(2,1)S(1)}, u32[]{:S(2)}, u32[]{:S(2)}) async-start(bf16[4,4,6144]{2,1,0:T(4,128)(2,1)} %reshape.276), calls=%async_computation.3 | async-start | bytes 393216 | tf_op jit(solution)/shard_map/all_to_all | solution.py:51
  213.8 14.7 %all-to-all-done.3 = bf16[4,4,6144]{2,1,0:T(4,128)(2,1)S(1)} async-done(((bf16[4,4,6144]{2,1,0:T(4,128)(2,1)}), bf16[4,4,6144]{2,1,0:T(4,128)(2,1)S(1)}, u32[]{:S(2)}, u32[]{:S(2)}) %all-to-all-start.3) | async-done | bytes 196640 | tf_op jit(solution)/shard_map/all_to_all | solution.py:51
  (106 shorter events, 35.3 us)
Async XLA Ops:
  7.2 102.3 %all-gather.4.cloned.1.call-start = ((), (), s32[]{:S(2)}) async-start(), calls=%async_computation.5 | async-start | bytes 7864320 | tf_op jit(solution)/shard_map/all_gather | solution.py:99
  7.2 2.9 %copy-start.7 = (bf16[1,512,768]{2,1,0:T(8,128)(2,1)S(1)}, bf16[1,512,768]{2,1,0:T(8,128)(2,1)}, u32[]{:S(2)}) copy-start(bf16[1,512,768]{2,1,0:T(8,128)(2,1)} %param.12) | copy-start | bytes 2359300
  7.2 12.6 %copy-start.14 = (s32[4,2]{0,1:T(2,128)S(1)}, s32[4,2]{0,1:T(2,128)}, u32[]{:S(2)}) copy-start(s32[4,2]{0,1:T(2,128)} %param.8) | copy-start | bytes 100
  7.2 12.8 %copy-start.15 = (f32[4,2]{0,1:T(2,128)S(1)}, f32[4,2]{0,1:T(2,128)}, u32[]{:S(2)}) copy-start(f32[4,2]{0,1:T(2,128)} %param.9) | copy-start | bytes 100
  7.2 13.0 %copy-start.12 = (bf16[4,3072]{1,0:T(4,128)(2,1)S(1)}, bf16[4,3072]{1,0:T(4,128)(2,1)}, u32[]{:S(2)}) copy-start(bf16[4,3072]{1,0:T(4,128)(2,1)} %param.13) | copy-start | bytes 73732
  10.1 10.3 %copy-start.13 = (bf16[4,3072]{1,0:T(4,128)(2,1)S(1)}, bf16[4,3072]{1,0:T(4,128)(2,1)}, u32[]{:S(2)}) copy-start(bf16[4,3072]{1,0:T(4,128)(2,1)} %param.7) | copy-start | bytes 73732
  10.1 47.6 %collective-permute-start = (bf16[512,768]{1,0:T(8,128)(2,1)S(1)}, bf16[512,768]{1,0:T(8,128)(2,1)S(1)}, u32[]{:S(2)}, u32[]{:S(2)}) collective-permute-start(bf16[512,768]{1,0:T(8,128)(2,1)S(1)} %bitcast.51), channel_id=1, source_target_pairs={{0,384},{128,0},{256,128},{384,256},{1,385},{129,1},{257,129},{385... | collective-permute-start | bytes 2359304 | tf_op jit(solution)/shard_map/ppermute | solution.py:75
  12.9 44.9 %collective-permute-start.1 = (bf16[512,768]{1,0:T(8,128)(2,1)S(1)}, bf16[512,768]{1,0:T(8,128)(2,1)}, u32[]{:S(2)}, u32[]{:S(2)}) collective-permute-start(bf16[512,768]{1,0:T(8,128)(2,1)S(1)} %bitcast.52), channel_id=1, source_target_pairs={{0,128},{128,256},{256,384},{384,0},{1,129},{129,257},{257,385},{3... | collective-permute-start | bytes 2359304 | tf_op jit(solution)/shard_map/ppermute | solution.py:75
  57.8 2.1 copy-start.1
  59.9 37.9 %all-to-all-start = ((bf16[4,64,6272]{2,1,0:T(8,128)(2,1)}), bf16[4,64,6272]{2,1,0:T(8,128)(2,1)S(1)}, u32[]{:S(2)}, u32[]{:S(2)}) async-start(bf16[4,64,6272]{2,1,0:T(8,128)(2,1)} %broadcast_in_dim.16), calls=%async_computation | async-start | bytes 6422528 | tf_op jit(solution)/shard_map/all_to_all | solution.py:44
  64.4 165.6 %reduce-scatter.2.cloned.1.call-start = ((), (), s32[]{:S(2)}) async-start(), calls=%async_computation.6 | async-start | bytes 3932160 | tf_op jit(solution)/shard_map/reduce_scatter | solution.py:172
  66.1 21.7 %collective-permute-start.2 = (bf16[256,768]{1,0:T(8,128)(2,1)}, bf16[256,768]{1,0:T(8,128)(2,1)}, u32[]{:S(2)}, u32[]{:S(2)}) collective-permute-start(bf16[256,768]{1,0:T(8,128)(2,1)} %slice.91), channel_id=1, source_target_pairs={{0,384},{128,0},{256,128},{384,256},{1,385},{129,1},{257,129},{385... | collective-permute-start | bytes 1179656 | tf_op jit(solution)/shard_map/ppermute | solution.py:75
  69.8 21.1 %collective-permute-start.3 = (bf16[256,768]{1,0:T(8,128)(2,1)}, bf16[256,768]{1,0:T(8,128)(2,1)}, u32[]{:S(2)}, u32[]{:S(2)}) collective-permute-start(bf16[256,768]{1,0:T(8,128)(2,1)} %slice.92), channel_id=1, source_target_pairs={{0,128},{128,256},{256,384},{384,0},{1,129},{129,257},{257,385},{3... | collective-permute-start | bytes 1179656 | tf_op jit(solution)/shard_map/ppermute | solution.py:75
  100.1 6.6 %collective-permute-start.4 = (bf16[128,6272]{1,0:T(8,128)(2,1)}, bf16[128,6272]{1,0:T(8,128)(2,1)}, u32[]{:S(2)}, u32[]{:S(2)}) collective-permute-start(bf16[128,6272]{1,0:T(8,128)(2,1)} %convolution_convert_fusion), channel_id=1, source_target_pairs={{0,16},{16,0},{1,17},{17,1},{2,18},{18,2},{3,19},{19,3},{4,20},{20... | collective-permute-start | bytes 4816904 | tf_op jit(solution)/shard_map/ppermute | solution.py:123
  106.6 1.2 copy-start
  115.5 1.8 copy-start.2
  115.7 2.0 copy-start.8
  117.3 1.1 copy-start.5
  120.0 6.7 %collective-permute-start.5 = (bf16[128,3072]{1,0:T(8,128)(2,1)}, bf16[128,3072]{1,0:T(8,128)(2,1)}, u32[]{:S(2)}, u32[]{:S(2)}) collective-permute-start(bf16[128,3072]{1,0:T(8,128)(2,1)} %slice.134), channel_id=1, source_target_pairs={{0,16},{16,0},{1,17},{17,1},{2,18},{18,2},{3,19},{19,3},{4,20},{20... | collective-permute-start | bytes 2359304 | tf_op jit(solution)/shard_map/ppermute | solution.py:145
  126.6 1.9 copy-start.9
  128.5 1.5 copy-start.6
  130.1 1.2 copy-start.11
  133.1 15.9 %collective-permute-start.8 = (bf16[64,3072]{1,0:T(8,128)(2,1)S(1)}, bf16[64,3072]{1,0:T(8,128)(2,1)S(1)}, u32[]{:S(2)}, u32[]{:S(2)}) collective-permute-start(bf16[64,3072]{1,0:T(8,128)(2,1)S(1)} %get-tuple-element.28), channel_id=1, source_target_pairs={{0,3},{1,0},{2,1},{3,2},{4,7},{5,4},{6,5},{7,6},{8,11},{9,8},{10,9... | collective-permute-start | bytes 1179656 | tf_op jit(solution)/shard_map/ppermute | solution.py:65
  136.1 15.5 %collective-permute-start.7 = (bf16[64,3072]{1,0:T(8,128)(2,1)S(1)}, bf16[64,3072]{1,0:T(8,128)(2,1)S(1)}, u32[]{:S(2)}, u32[]{:S(2)}) collective-permute-start(bf16[64,3072]{1,0:T(8,128)(2,1)S(1)} %get-tuple-element.29), channel_id=1, source_target_pairs={{0,2},{1,3},{2,0},{3,1},{4,6},{5,7},{6,4},{7,5},{8,10},{9,11},{10,... | collective-permute-start | bytes 1179656 | tf_op jit(solution)/shard_map/ppermute | solution.py:65
  139.5 19.2 %collective-permute-start.6 = (bf16[64,3072]{1,0:T(8,128)(2,1)S(1)}, bf16[64,3072]{1,0:T(8,128)(2,1)S(1)}, u32[]{:S(2)}, u32[]{:S(2)}) collective-permute-start(bf16[64,3072]{1,0:T(8,128)(2,1)S(1)} %get-tuple-element.27), channel_id=1, source_target_pairs={{0,1},{1,2},{2,3},{3,0},{4,5},{5,6},{6,7},{7,4},{8,9},{9,10},{10,1... | collective-permute-start | bytes 1179656 | tf_op jit(solution)/shard_map/ppermute | solution.py:65
  146.4 13.3 %collective-permute-start.9 = (bf16[128,3072]{1,0:T(8,128)(2,1)S(1)}, bf16[128,3072]{1,0:T(8,128)(2,1)S(1)}, u32[]{:S(2)}, u32[]{:S(2)}) collective-permute-start(bf16[128,3072]{1,0:T(8,128)(2,1)S(1)} %slice.136), channel_id=1, source_target_pairs={{0,16},{16,0},{1,17},{17,1},{2,18},{18,2},{3,19},{19,3},{4,20},{20... | collective-permute-start | bytes 2359304 | tf_op jit(solution)/shard_map/ppermute | solution.py:145
  160.3 29.4 %all-to-all-start.1 = ((bf16[4,16,3072]{2,1,0:T(8,128)(2,1)}), bf16[4,16,3072]{2,1,0:T(8,128)(2,1)S(1)}, u32[]{:S(2)}, u32[]{:S(2)}) async-start(bf16[4,16,3072]{2,1,0:T(8,128)(2,1)} %bitcast.10), calls=%async_computation.1 | async-start | bytes 786432 | tf_op jit(solution)/shard_map/all_to_all | solution.py:51
  163.9 13.9 %collective-permute-start.12 = (bf16[64,3072]{1,0:T(8,128)(2,1)S(1)}, bf16[64,3072]{1,0:T(8,128)(2,1)S(1)}, u32[]{:S(2)}, u32[]{:S(2)}) collective-permute-start(bf16[64,3072]{1,0:T(8,128)(2,1)S(1)} %get-tuple-element.31), channel_id=1, source_target_pairs={{0,3},{1,0},{2,1},{3,2},{4,7},{5,4},{6,5},{7,6},{8,11},{9,8},{10,9... | collective-permute-start | bytes 1179656 | tf_op jit(solution)/shard_map/ppermute | solution.py:65
  166.4 15.5 %collective-permute-start.11 = (bf16[64,3072]{1,0:T(8,128)(2,1)S(1)}, bf16[64,3072]{1,0:T(8,128)(2,1)S(1)}, u32[]{:S(2)}, u32[]{:S(2)}) collective-permute-start(bf16[64,3072]{1,0:T(8,128)(2,1)S(1)} %get-tuple-element.32), channel_id=1, source_target_pairs={{0,2},{1,3},{2,0},{3,1},{4,6},{5,7},{6,4},{7,5},{8,10},{9,11},{10,... | collective-permute-start | bytes 1179656 | tf_op jit(solution)/shard_map/ppermute | solution.py:65
  169.8 19.0 %collective-permute-start.10 = (bf16[64,3072]{1,0:T(8,128)(2,1)S(1)}, bf16[64,3072]{1,0:T(8,128)(2,1)S(1)}, u32[]{:S(2)}, u32[]{:S(2)}) collective-permute-start(bf16[64,3072]{1,0:T(8,128)(2,1)S(1)} %get-tuple-element.30), channel_id=1, source_target_pairs={{0,1},{1,2},{2,3},{3,0},{4,5},{5,6},{6,7},{7,4},{8,9},{9,10},{10,1... | collective-permute-start | bytes 1179656 | tf_op jit(solution)/shard_map/ppermute | solution.py:65
  189.7 16.6 %all-to-all-start.2 = ((bf16[4,16,3072]{2,1,0:T(8,128)(2,1)}), bf16[4,16,3072]{2,1,0:T(8,128)(2,1)S(1)}, u32[]{:S(2)}, u32[]{:S(2)}) async-start(bf16[4,16,3072]{2,1,0:T(8,128)(2,1)} %bitcast.11), calls=%async_computation.2 | async-start | bytes 786432 | tf_op jit(solution)/shard_map/all_to_all | solution.py:51
  207.2 21.3 %all-to-all-start.3 = ((bf16[4,4,6144]{2,1,0:T(4,128)(2,1)}), bf16[4,4,6144]{2,1,0:T(4,128)(2,1)S(1)}, u32[]{:S(2)}, u32[]{:S(2)}) async-start(bf16[4,4,6144]{2,1,0:T(4,128)(2,1)} %reshape.276), calls=%async_computation.3 | async-start | bytes 393216 | tf_op jit(solution)/shard_map/all_to_all | solution.py:51
  (3 other events, 3.0 us)
Sparse Core Ops, SparseCore 0:
  10.2 84.6 all-gather.3
  126.1 37.6 reduce-scatter.1

commit v4 on v3

--- a/solution.py
+++ b/solution.py
@@ -90,9 +90,6 @@
     expert = lax.axis_index("zl") * 2 + core
     other = lax.axis_index("zl") * 2 + 1 - core
 
-    def columns(x, q):
-        return x[:, q * quarter : (q + 1) * quarter]
-
     mine = jnp.concatenate([gate_weight[0], up_weight[0]], axis=1)
     mine = with_layout_constraint(mine, Layout(major_to_minor=(0, 1)))
     own_down, mine = lax.optimization_barrier((down_weight[0], mine))
@@ -106,9 +103,10 @@
     by_z, from_next, from_last = lax.optimization_barrier((by_z, from_next, from_last))
     plane = gather_by_exchange(by_z.reshape(-1, packed.shape[1]), "y", y_size)
     if quarters == 4:
-        across = pass_on(from_next[: ff // 2], "x", -1), pass_on(from_last[ff // 2 :], "x", 1)
+        cut = quarter // 2
+        across = pass_on(from_next[:, :cut], "x", -1), pass_on(from_last[:, cut:], "x", 1)
         plane, across = lax.optimization_barrier((plane, across))
-        downs = [own_down, from_next, jnp.concatenate(across, axis=0), from_last]
+        downs = [own_down, from_next, *across, from_last]
     else:
         downs = [own_down, from_next]
 
@@ -153,27 +151,31 @@
     hidden = (activated * up_pre).astype(BF16)
     out_part = jnp.concatenate([(prob * dot(hidden, down)).astype(BF16) for down in downs], axis=1)
     out_tokens = leave(out_part)
-    out_parts = send_by_shifts(out_tokens, "y", y_size)
-
-    late_hidden, _ = lax.optimization_barrier((hidden, out_part))
-    late_cot, _ = lax.optimization_barrier((cot_rows, out_tokens))
-    grad_hidden = sum(dot(columns(late_cot, s), downs[s], LAST) for s in range(quarters))
+    out_y = scatter_sum_by_exchange(out_tokens, "y", y_size)
+
+    late_cot, _ = lax.optimization_barrier((cot_rows, out_part))
+    grad_hidden, column = 0.0, 0
+    for down in downs:
+        piece = late_cot[:, column : column + down.shape[1]]
+        grad_hidden, column = grad_hidden + dot(piece, down, LAST), column + down.shape[1]
     grad_up = (grad_hidden * activated).astype(BF16)
     grad_gate = (grad_hidden * up_pre * slope_gate).astype(BF16)
     grad_both = jnp.concatenate([grad_gate, grad_up], axis=1)
+    grad_both, late_hidden, _ = lax.optimization_barrier((grad_both, hidden, out_tokens))
     grad_tokens = leave(dot(grad_both, full_both, LAST).astype(BF16))
-    grad_parts = send_by_shifts(grad_tokens, "y", y_size)
-
     partial_down = []
     for q in range(quarters):
         start = lax.rem(q - group + quarters, quarters) * quarter
-        block_q = lax.dynamic_slice_in_dim(cot_rows, start, quarter, axis=1)
+        block_q = lax.dynamic_slice_in_dim(late_cot, start, quarter, axis=1)
         partial_down.append(dot(late_hidden, block_q, FIRST).astype(BF16))
-    down_grads = lax.psum_scatter(jnp.stack(partial_down), "x", scatter_dimension=0)[None]
-
-    out_y, grad_tokens = lax.optimization_barrier((add_up(out_parts), grad_tokens))
-    out_low = scatter_sum_by_exchange(out_y, "zl", low_size)
-    grad_low = scatter_sum_by_exchange(add_up(grad_parts), "zl", low_size)
+    partial_down = jnp.stack(partial_down)
+    out_y, grad_tokens, partial_down = lax.optimization_barrier((out_y, grad_tokens, partial_down))
+    down_grads = lax.psum_scatter(partial_down, "x", scatter_dimension=0)[None]
+
+    grad_y = scatter_sum_by_exchange(grad_tokens, "y", y_size)
+    out_low = add_up(send_by_shifts(out_y, "zl", low_size))
+    out_low, grad_y = lax.optimization_barrier((out_low, grad_y))
+    grad_low = scatter_sum_by_exchange(grad_y, "zl", low_size)
     low = jnp.concatenate([out_low, grad_low], axis=1)
     own = scatter_sum_by_exchange(low, "zh", high_size)
     turn_back = lax.rem(quarters - group, quarters) * quarter

time: 238 us -> 225 us (0.945)
  waiting for transfers between devices: 75.4 us -> 57.2 us
  blocking collectives: 37.4 us -> 49.3 us
  starting transfers between devices: 59.5 us -> 50 us
  matrix products: 23.5 us -> 29 us
  local copies, waits for them, and re-layouts: 15.1 us -> 11 us
    ppermute x6 -> x3, waiting for transfers between devices: 26 us -> 5.46 us  [send_by_shifts(): parts.append(lax.ppermute(block(shift), axis, pairs))]
    all_to_all x0 -> x1, blocking collectives: none -> 13.2 us  [scatter_sum_by_exchange(): parts = lax.all_to_all(parts, axes, split_axis=0, concat_axis=0, tiled=True)]
    ppermute x6 -> x3, starting transfers between devices: 17.2 us -> 9.56 us  [send_by_shifts(): parts.append(lax.ppermute(block(shift), axis, pairs))]
    dot_general x20 -> x22, matrix products: 23.5 us -> 29 us  [dot(): return lax.dot_general(a, b, dims, preferred_element_type=F32)]
    ppermute x4, waiting for transfers between devices: 16 us -> 19.2 us  [pass_on(): return lax.ppermute(x, axis, [(i, (i + shift) % size) for i in range(size)])]
    unnamed x34 -> x29, local copies, waits for them, and re-layouts: 4.92 us -> 1.79 us
  transfers between devices with their start and end apart: 19 -> 16, of which waited for: 10 -> 9; matrix products, arithmetic and copies ran while one was open for 14% -> 14% of each run, Pallas kernels for 0% -> 0%
where the time goes in v4:
time: 225 us; the launch traced here: 222 us
  waiting for transfers between devices  57.2 us (25%)
  starting transfers between devices  50 us (22%)
  blocking collectives  49.3 us (22%)
  matrix products  29 us (13%)
  between operations  14.7 us (7%)
  other arithmetic  11.3 us (5%)
  local copies, waits for them, and re-layouts  11 us (5%)
    all_gather x1, blocking collectives, on_device(): by_z = lax.all_gather(packed[None], ('zh', 'zl'), axis=0, tiled=True)  36.2 us
    dot_general x22, matrix products, dot(): return lax.dot_general(a, b, dims, preferred_element_type=F32)  29 us
    all_to_all x3, waiting for transfers between devices, scatter_sum_by_exchange(): parts = lax.all_to_all(parts, axes, split_axis=0, concat_axis=0, tiled=True)  25.6 us
    ppermute x4, waiting for transfers between devices, pass_on(): return lax.ppermute(x, axis, [(i, (i + shift) % size) for i in range(size)])  19.2 us
    ppermute x4, starting transfers between devices, pass_on(): return lax.ppermute(x, axis, [(i, (i + shift) % size) for i in range(size)])  15.5 us
    all_to_all x3, starting transfers between devices, scatter_sum_by_exchange(): parts = lax.all_to_all(parts, axes, split_axis=0, concat_axis=0, tiled=True)  13.8 us
    all_to_all x1, blocking collectives, scatter_sum_by_exchange(): parts = lax.all_to_all(parts, axes, split_axis=0, concat_axis=0, tiled=True)  13.2 us
    ppermute x3, starting transfers between devices, send_by_shifts(): parts.append(lax.ppermute(block(shift), axis, pairs))  9.56 us
  transfers between devices with their start and end apart: 16, of which 9 were waited for; matrix products, arithmetic and copies ran while one was open for 14% of the time, Pallas kernels for 0%

profile of v4, /device:TPU:6, one launch (start us, length us, event | category | flops | bytes accessed | tf_op | source)
XLA Modules:
  0.0 222.5 jit_solution(5143193016488359471)
XLA Ops:
  7.3 2.8 %pad_maximum_fusion.2 = bf16[768,1024]{1,0:T(8,128)(2,1)} fusion(bf16[768,512]{1,0:T(8,128)(2,1)} %bitcast.59, bf16[768,512]{1,0:T(8,128)(2,1)} %bitcast.60), kind=kLoop, calls=%fused_computation.14 | loop fusion | flops 3145728 | bytes 3145728 | tf_op jit(solution)/shard_map/concatenate | solution.py:93
  10.1 7.8 %collective-permute-start.1 = (bf16[512,768]{1,0:T(8,128)(2,1)S(1)}, bf16[512,768]{1,0:T(8,128)(2,1)S(1)}, u32[]{:S(2)}, u32[]{:S(2)}) collective-permute-start(bf16[512,768]{1,0:T(8,128)(2,1)S(1)} %bitcast.61), channel_id=1, source_target_pairs={{0,128},{128,256},{256,384},{384,0},{1,129},{129,257},{257,385},{3... | collective-permute-start | bytes 2359304 | tf_op jit(solution)/shard_map/ppermute | solution.py:75
  17.9 1.9 collective-permute-start
  20.4 36.2 %all-gather.1 = bf16[16,4,6272]{2,1,0:T(4,128)(2,1)S(1)} all-gather(bf16[1,4,6272]{2,1,0:T(4,128)(2,1)S(1)} %fusion.66), channel_id=2, replica_groups=mesh['x'=4,'zl'=4,'c'=2,'zh'=4,'y'=4] {'zh','zl'}, dimensions={0}, use_global_device_ids=true | all-gather | bytes 852992 | tf_op jit(solution)/shard_map/all_gather | solution.py:102
  57.6 2.0 broadcast_in_dim.16
  59.6 4.6 %all-to-all-start = ((bf16[4,64,6272]{2,1,0:T(8,128)(2,1)}), bf16[4,64,6272]{2,1,0:T(8,128)(2,1)S(1)}, u32[]{:S(2)}, u32[]{:S(2)}) async-start(bf16[4,64,6272]{2,1,0:T(8,128)(2,1)} %broadcast_in_dim.16), calls=%async_computation | async-start | bytes 6422528 | tf_op jit(solution)/shard_map/all_to_all | solution.py:44
  67.8 3.4 %collective-permute-start.3 = (bf16[512,384]{1,0:T(8,128)(2,1)}, bf16[512,384]{1,0:T(8,128)(2,1)}, u32[]{:S(2)}, u32[]{:S(2)}) collective-permute-start(bf16[512,384]{1,0:T(8,128)(2,1)} %slice.95), channel_id=1, source_target_pairs={{0,128},{128,256},{256,384},{384,0},{1,129},{129,257},{257,385},{3... | collective-permute-start | bytes 1179656 | tf_op jit(solution)/shard_map/ppermute | solution.py:75
  71.2 2.4 %collective-permute-start.2 = (bf16[512,384]{1,0:T(8,128)(2,1)}, bf16[512,384]{1,0:T(8,128)(2,1)}, u32[]{:S(2)}, u32[]{:S(2)}) collective-permute-start(bf16[512,384]{1,0:T(8,128)(2,1)} %slice.94), channel_id=1, source_target_pairs={{0,384},{128,0},{256,128},{384,256},{1,385},{129,1},{257,129},{385... | collective-permute-start | bytes 1179656 | tf_op jit(solution)/shard_map/ppermute | solution.py:75
  73.7 14.6 %collective-permute-done.3 = bf16[512,384]{1,0:T(8,128)(2,1)} collective-permute-done((bf16[512,384]{1,0:T(8,128)(2,1)}, bf16[512,384]{1,0:T(8,128)(2,1)}, u32[]{:S(2)}, u32[]{:S(2)}) %collective-permute-start.3) | collective-permute-done | bytes 393248 | tf_op jit(solution)/shard_map/ppermute | solution.py:75
  88.3 4.6 %collective-permute-done.2 = bf16[512,384]{1,0:T(8,128)(2,1)} collective-permute-done((bf16[512,384]{1,0:T(8,128)(2,1)}, bf16[512,384]{1,0:T(8,128)(2,1)}, u32[]{:S(2)}, u32[]{:S(2)}) %collective-permute-start.2) | collective-permute-done | bytes 393248 | tf_op jit(solution)/shard_map/ppermute | solution.py:75
  92.8 4.8 %all-to-all-done = bf16[4,64,6272]{2,1,0:T(8,128)(2,1)S(1)} async-done(((bf16[4,64,6272]{2,1,0:T(8,128)(2,1)}), bf16[4,64,6272]{2,1,0:T(8,128)(2,1)S(1)}, u32[]{:S(2)}, u32[]{:S(2)}) %all-to-all-start) | async-done | bytes 3211296 | tf_op jit(solution)/shard_map/all_to_all | solution.py:44
  97.8 1.9 convolution_convert_fusion
  99.8 1.9 collective-permute-start.4
  103.4 2.1 collective-permute-done.4
  108.2 5.1 %fusion.2 = f32[256,1024]{1,0:T(8,128)S(1)} fusion(bf16[3072,1024]{1,0:T(8,128)(2,1)} %all-gather.4.cloned.1.call-done, bf16[128,6272]{1,0:T(8,128)(2,1)} %collective-permute-done.4, bf16[128,6272]{1,0:T(8,128)(2,1)} %copy-done), kind=kOutput, calls=%fused_computation.10 | convolution fusion | flops 1613758464 | bytes 10551296 | tf_op jit(solution)/shard_map/dot_general | solution.py:17
  121.4 2.0 collective-permute-start.5
  125.6 1.8 fusion
  127.4 3.6 %all-to-all-start.1 = ((bf16[4,64,3072]{2,1,0:T(8,128)(2,1)}), bf16[4,64,3072]{2,1,0:T(8,128)(2,1)S(1)}, u32[]{:S(2)}, u32[]{:S(2)}) async-start(bf16[4,64,3072]{2,1,0:T(8,128)(2,1)} %bitcast.56), calls=%async_computation.1 | async-start | bytes 3145728 | tf_op jit(solution)/shard_map/all_to_all | solution.py:51
  132.3 4.6 %convolution_convert_fusion.2 = bf16[256,3072]{1,0:T(8,128)(2,1)S(1)} fusion(bf16[256,1024]{1,0:T(8,128)(2,1)S(1)} %copy-done.7, bf16[3072,1024]{1,0:T(8,128)(2,1)} %all-gather.4.cloned.1.call-done), kind=kOutput, calls=%fused_computation.6 | convolution fusion | flops 1611399168 | bytes 8388608 | tf_op jit(solution)/shard_map/dot_general | solution.py:17
  137.9 2.3 %collective-permute-start.6 = (bf16[128,3072]{1,0:T(8,128)(2,1)}, bf16[128,3072]{1,0:T(8,128)(2,1)}, u32[]{:S(2)}, u32[]{:S(2)}) collective-permute-start(bf16[128,3072]{1,0:T(8,128)(2,1)} %slice.140), channel_id=1, source_target_pairs={{0,16},{16,0},{1,17},{17,1},{2,18},{18,2},{3,19},{19,3},{4,20},{20... | collective-permute-start | bytes 2359304 | tf_op jit(solution)/shard_map/ppermute | solution.py:143
  141.0 1.9 pad_maximum_fusion
  144.7 3.0 %fusion.1 = bf16[256,3072]{1,0:T(8,128)(2,1)} fusion(f32[256,3072]{1,0:T(8,128)S(1)} %fusion.23, bf16[128,3072]{1,0:T(8,128)(2,1)} %collective-permute-done.6, s32[128]{0:T(128)S(1)} %get-tuple-element.50, s32[128]{0:T(128)S(1)} %get-tuple-element.49, s32[256]{0:T(256)S(1)} %and_select_fusion.2, s32[256]{0:T(256)S(1)} %bitcast.73, s32[256]{0:T(256)S(1)} %bitcast.69), kind=kOutput, calls=%fused_computation.5 | convolution fusion | flops 203063296 | bytes 5509120 | tf_op jit(solution)/shard_map/dot_general | solution.py:17
  147.7 4.8 %all-to-all-done.1 = bf16[4,64,3072]{2,1,0:T(8,128)(2,1)S(1)} async-done(((bf16[4,64,3072]{2,1,0:T(8,128)(2,1)}), bf16[4,64,3072]{2,1,0:T(8,128)(2,1)S(1)}, u32[]{:S(2)}, u32[]{:S(2)}) %all-to-all-start.1) | async-done | bytes 1572896 | tf_op jit(solution)/shard_map/all_to_all | solution.py:51
  153.6 3.7 %all-to-all-start.2 = ((bf16[4,64,3072]{2,1,0:T(8,128)(2,1)}), bf16[4,64,3072]{2,1,0:T(8,128)(2,1)S(1)}, u32[]{:S(2)}, u32[]{:S(2)}) async-start(bf16[4,64,3072]{2,1,0:T(8,128)(2,1)} %bitcast.15), calls=%async_computation.2 | async-start | bytes 3145728 | tf_op jit(solution)/shard_map/all_to_all | solution.py:51
  157.4 1.9 collective-permute-start.7
  159.3 5.7 %collective-permute-start.9 = (bf16[16,3072]{1,0:T(8,128)(2,1)S(1)}, bf16[16,3072]{1,0:T(8,128)(2,1)S(1)}, u32[]{:S(2)}, u32[]{:S(2)}) collective-permute-start(bf16[16,3072]{1,0:T(8,128)(2,1)S(1)} %get-tuple-element.40), channel_id=1, source_target_pairs={{0,96},{32,0},{64,32},{96,64},{1,97},{33,1},{65,33},{97,65},{2,98}... | collective-permute-start | bytes 294920 | tf_op jit(solution)/shard_map/ppermute | solution.py:65
  165.1 1.9 collective-permute-start.8
  168.0 4.4 %collective-permute-done.8 = bf16[16,3072]{1,0:T(8,128)(2,1)S(1)} collective-permute-done((bf16[16,3072]{1,0:T(8,128)(2,1)S(1)}, bf16[16,3072]{1,0:T(8,128)(2,1)S(1)}, u32[]{:S(2)}, u32[]{:S(2)}) %collective-permute-start.8) | collective-permute-done | bytes 98336 | tf_op jit(solution)/shard_map/ppermute | solution.py:65
  172.5 5.5 %all-to-all-done.2 = bf16[4,64,3072]{2,1,0:T(8,128)(2,1)S(1)} async-done(((bf16[4,64,3072]{2,1,0:T(8,128)(2,1)}), bf16[4,64,3072]{2,1,0:T(8,128)(2,1)S(1)}, u32[]{:S(2)}, u32[]{:S(2)}) %all-to-all-start.2) | async-done | bytes 1572896 | tf_op jit(solution)/shard_map/all_to_all | solution.py:51
  178.3 13.2 %all_to_all.25 = bf16[4,16,3072]{2,1,0:T(8,128)(2,1)S(1)} all-to-all(bf16[4,16,3072]{2,1,0:T(8,128)(2,1)S(1)} %bitcast.58), channel_id=1, replica_groups=mesh['x'=4,'zl'=4,'c'=2,'zh'=4,'y'=4] {'zl'}, dimensions={0} | all-to-all | bytes 786432 | tf_op jit(solution)/shard_map/all_to_all | solution.py:51
  192.4 6.5 %all-to-all-start.4 = ((bf16[4,4,6144]{2,1,0:T(4,128)(2,1)}), bf16[4,4,6144]{2,1,0:T(4,128)(2,1)S(1)}, u32[]{:S(2)}, u32[]{:S(2)}) async-start(bf16[4,4,6144]{2,1,0:T(4,128)(2,1)} %reshape.280), calls=%async_computation.4 | async-start | bytes 393216 | tf_op jit(solution)/shard_map/all_to_all | solution.py:51
  198.9 15.3 %all-to-all-done.4 = bf16[4,4,6144]{2,1,0:T(4,128)(2,1)S(1)} async-done(((bf16[4,4,6144]{2,1,0:T(4,128)(2,1)}), bf16[4,4,6144]{2,1,0:T(4,128)(2,1)S(1)}, u32[]{:S(2)}, u32[]{:S(2)}) %all-to-all-start.4) | async-done | bytes 196640 | tf_op jit(solution)/shard_map/all_to_all | solution.py:51
  (96 shorter events, 29.6 us)
Async XLA Ops:
  7.2 101.1 %all-gather.4.cloned.1.call-start = ((), (), s32[]{:S(2)}) async-start(), calls=%async_computation.6 | async-start | bytes 7864320 | tf_op jit(solution)/shard_map/all_gather | solution.py:96
  7.2 2.9 %copy-start.5 = (bf16[1,512,768]{2,1,0:T(8,128)(2,1)S(1)}, bf16[1,512,768]{2,1,0:T(8,128)(2,1)}, u32[]{:S(2)}) copy-start(bf16[1,512,768]{2,1,0:T(8,128)(2,1)} %param.12) | copy-start | bytes 2359300
  7.2 12.6 %copy-start.12 = (s32[4,2]{0,1:T(2,128)S(1)}, s32[4,2]{0,1:T(2,128)}, u32[]{:S(2)}) copy-start(s32[4,2]{0,1:T(2,128)} %param.8) | copy-start | bytes 100
  7.2 12.8 %copy-start.13 = (f32[4,2]{0,1:T(2,128)S(1)}, f32[4,2]{0,1:T(2,128)}, u32[]{:S(2)}) copy-start(f32[4,2]{0,1:T(2,128)} %param.9) | copy-start | bytes 100
  7.2 12.9 %copy-start.10 = (bf16[4,3072]{1,0:T(4,128)(2,1)S(1)}, bf16[4,3072]{1,0:T(4,128)(2,1)}, u32[]{:S(2)}) copy-start(bf16[4,3072]{1,0:T(4,128)(2,1)} %param.13) | copy-start | bytes 73732
  10.1 10.3 %copy-start.11 = (bf16[4,3072]{1,0:T(4,128)(2,1)S(1)}, bf16[4,3072]{1,0:T(4,128)(2,1)}, u32[]{:S(2)}) copy-start(bf16[4,3072]{1,0:T(4,128)(2,1)} %param.7) | copy-start | bytes 73732
  10.1 46.4 %collective-permute-start.1 = (bf16[512,768]{1,0:T(8,128)(2,1)S(1)}, bf16[512,768]{1,0:T(8,128)(2,1)S(1)}, u32[]{:S(2)}, u32[]{:S(2)}) collective-permute-start(bf16[512,768]{1,0:T(8,128)(2,1)S(1)} %bitcast.61), channel_id=1, source_target_pairs={{0,128},{128,256},{256,384},{384,0},{1,129},{129,257},{257,385},{3... | collective-permute-start | bytes 2359304 | tf_op jit(solution)/shard_map/ppermute | solution.py:75
  17.9 39.6 %collective-permute-start = (bf16[512,768]{1,0:T(8,128)(2,1)S(1)}, bf16[512,768]{1,0:T(8,128)(2,1)S(1)}, u32[]{:S(2)}, u32[]{:S(2)}) collective-permute-start(bf16[512,768]{1,0:T(8,128)(2,1)S(1)} %bitcast.62), channel_id=1, source_target_pairs={{0,384},{128,0},{256,128},{384,256},{1,385},{129,1},{257,129},{385... | collective-permute-start | bytes 2359304 | tf_op jit(solution)/shard_map/ppermute | solution.py:75
  56.5 0.9 copy-start.1
  57.4 2.1 copy-start.8
  59.6 38.0 %all-to-all-start = ((bf16[4,64,6272]{2,1,0:T(8,128)(2,1)}), bf16[4,64,6272]{2,1,0:T(8,128)(2,1)S(1)}, u32[]{:S(2)}, u32[]{:S(2)}) async-start(bf16[4,64,6272]{2,1,0:T(8,128)(2,1)} %broadcast_in_dim.16), calls=%async_computation | async-start | bytes 6422528 | tf_op jit(solution)/shard_map/all_to_all | solution.py:44
  67.8 20.5 %collective-permute-start.3 = (bf16[512,384]{1,0:T(8,128)(2,1)}, bf16[512,384]{1,0:T(8,128)(2,1)}, u32[]{:S(2)}, u32[]{:S(2)}) collective-permute-start(bf16[512,384]{1,0:T(8,128)(2,1)} %slice.95), channel_id=1, source_target_pairs={{0,128},{128,256},{256,384},{384,0},{1,129},{129,257},{257,385},{3... | collective-permute-start | bytes 1179656 | tf_op jit(solution)/shard_map/ppermute | solution.py:75
  71.2 21.6 %collective-permute-start.2 = (bf16[512,384]{1,0:T(8,128)(2,1)}, bf16[512,384]{1,0:T(8,128)(2,1)}, u32[]{:S(2)}, u32[]{:S(2)}) collective-permute-start(bf16[512,384]{1,0:T(8,128)(2,1)} %slice.94), channel_id=1, source_target_pairs={{0,384},{128,0},{256,128},{384,256},{1,385},{129,1},{257,129},{385... | collective-permute-start | bytes 1179656 | tf_op jit(solution)/shard_map/ppermute | solution.py:75
  99.8 5.7 %collective-permute-start.4 = (bf16[128,6272]{1,0:T(8,128)(2,1)}, bf16[128,6272]{1,0:T(8,128)(2,1)}, u32[]{:S(2)}, u32[]{:S(2)}) collective-permute-start(bf16[128,6272]{1,0:T(8,128)(2,1)} %convolution_convert_fusion), channel_id=1, source_target_pairs={{0,16},{16,0},{1,17},{17,1},{2,18},{18,2},{3,19},{19,3},{4,20},{20... | collective-permute-start | bytes 4816904 | tf_op jit(solution)/shard_map/ppermute | solution.py:121
  103.3 3.2 %copy-start = (bf16[128,6272]{1,0:T(8,128)(2,1)}, bf16[128,6272]{1,0:T(8,128)(2,1)S(1)}, u32[]{:S(2)}) copy-start(bf16[128,6272]{1,0:T(8,128)(2,1)S(1)} %convolution_convert_fusion.1) | copy-start | bytes 4816900
  108.2 5.3 %copy-start.6 = (bf16[1,512,768]{2,1,0:T(8,128)(2,1)S(1)}, bf16[1,512,768]{2,1,0:T(8,128)(2,1)}, u32[]{:S(2)}) copy-start(bf16[1,512,768]{2,1,0:T(8,128)(2,1)} %param.12) | copy-start | bytes 2359300
  113.3 1.1 copy-start.9
  114.5 3.0 %copy-start.2 = (bf16[512,768]{1,0:T(8,128)(2,1)S(1)}, bf16[512,768]{1,0:T(8,128)(2,1)}, u32[]{:S(2)}) copy-start(bf16[512,768]{1,0:T(8,128)(2,1)} %copy-done.1) | copy-start | bytes 2359300
  121.4 4.2 %collective-permute-start.5 = (bf16[128,3072]{1,0:T(8,128)(2,1)S(1)}, bf16[128,3072]{1,0:T(8,128)(2,1)S(1)}, u32[]{:S(2)}, u32[]{:S(2)}) collective-permute-start(bf16[128,3072]{1,0:T(8,128)(2,1)S(1)} %slice.138), channel_id=1, source_target_pairs={{0,16},{16,0},{1,17},{17,1},{2,18},{18,2},{3,19},{19,3},{4,20},{20... | collective-permute-start | bytes 2359304 | tf_op jit(solution)/shard_map/ppermute | solution.py:143
  127.4 25.1 %all-to-all-start.1 = ((bf16[4,64,3072]{2,1,0:T(8,128)(2,1)}), bf16[4,64,3072]{2,1,0:T(8,128)(2,1)S(1)}, u32[]{:S(2)}, u32[]{:S(2)}) async-start(bf16[4,64,3072]{2,1,0:T(8,128)(2,1)} %bitcast.56), calls=%async_computation.1 | async-start | bytes 3145728 | tf_op jit(solution)/shard_map/all_to_all | solution.py:51
  131.0 84.6 %reduce-scatter.2.cloned.1.call-start = ((), (), s32[]{:S(2)}) async-start(), calls=%async_computation.7 | async-start | bytes 3932160 | tf_op jit(solution)/shard_map/reduce_scatter | solution.py:173
  131.2 1.0 copy-start.7
  136.9 4.2 %copy-start.3 = (bf16[256,3072]{1,0:T(8,128)(2,1)}, bf16[256,3072]{1,0:T(8,128)(2,1)S(1)}, u32[]{:S(2)}) copy-start(bf16[256,3072]{1,0:T(8,128)(2,1)S(1)} %convolution_convert_fusion.2) | copy-start | bytes 4718596
  137.9 6.8 %collective-permute-start.6 = (bf16[128,3072]{1,0:T(8,128)(2,1)}, bf16[128,3072]{1,0:T(8,128)(2,1)}, u32[]{:S(2)}, u32[]{:S(2)}) collective-permute-start(bf16[128,3072]{1,0:T(8,128)(2,1)} %slice.140), channel_id=1, source_target_pairs={{0,16},{16,0},{1,17},{17,1},{2,18},{18,2},{3,19},{19,3},{4,20},{20... | collective-permute-start | bytes 2359304 | tf_op jit(solution)/shard_map/ppermute | solution.py:143
  153.6 3.7 %copy-start.4 = (bf16[64,3072]{1,0:T(8,128)(2,1)S(1)}, bf16[64,3072]{1,0:T(8,128)(2,1)}, u32[]{:S(2)}) copy-start(bf16[64,3072]{1,0:T(8,128)(2,1)} %reduce_sum.58) | copy-start | bytes 1179652
  153.6 24.4 %all-to-all-start.2 = ((bf16[4,64,3072]{2,1,0:T(8,128)(2,1)}), bf16[4,64,3072]{2,1,0:T(8,128)(2,1)S(1)}, u32[]{:S(2)}, u32[]{:S(2)}) async-start(bf16[4,64,3072]{2,1,0:T(8,128)(2,1)} %bitcast.15), calls=%async_computation.2 | async-start | bytes 3145728 | tf_op jit(solution)/shard_map/all_to_all | solution.py:51
  157.4 9.6 %collective-permute-start.7 = (bf16[16,3072]{1,0:T(8,128)(2,1)S(1)}, bf16[16,3072]{1,0:T(8,128)(2,1)S(1)}, u32[]{:S(2)}, u32[]{:S(2)}) collective-permute-start(bf16[16,3072]{1,0:T(8,128)(2,1)S(1)} %get-tuple-element.39), channel_id=1, source_target_pairs={{0,32},{32,64},{64,96},{96,0},{1,33},{33,65},{65,97},{97,1},{2,34}... | collective-permute-start | bytes 294920 | tf_op jit(solution)/shard_map/ppermute | solution.py:65
  159.3 8.7 %collective-permute-start.9 = (bf16[16,3072]{1,0:T(8,128)(2,1)S(1)}, bf16[16,3072]{1,0:T(8,128)(2,1)S(1)}, u32[]{:S(2)}, u32[]{:S(2)}) collective-permute-start(bf16[16,3072]{1,0:T(8,128)(2,1)S(1)} %get-tuple-element.40), channel_id=1, source_target_pairs={{0,96},{32,0},{64,32},{96,64},{1,97},{33,1},{65,33},{97,65},{2,98}... | collective-permute-start | bytes 294920 | tf_op jit(solution)/shard_map/ppermute | solution.py:65
  165.1 7.4 %collective-permute-start.8 = (bf16[16,3072]{1,0:T(8,128)(2,1)S(1)}, bf16[16,3072]{1,0:T(8,128)(2,1)S(1)}, u32[]{:S(2)}, u32[]{:S(2)}) collective-permute-start(bf16[16,3072]{1,0:T(8,128)(2,1)S(1)} %get-tuple-element.41), channel_id=1, source_target_pairs={{0,64},{32,96},{64,0},{96,32},{1,65},{33,97},{65,1},{97,33},{2,66}... | collective-permute-start | bytes 294920 | tf_op jit(solution)/shard_map/ppermute | solution.py:65
  192.4 21.8 %all-to-all-start.4 = ((bf16[4,4,6144]{2,1,0:T(4,128)(2,1)}), bf16[4,4,6144]{2,1,0:T(4,128)(2,1)S(1)}, u32[]{:S(2)}, u32[]{:S(2)}) async-start(bf16[4,4,6144]{2,1,0:T(4,128)(2,1)} %reshape.280), calls=%async_computation.4 | async-start | bytes 393216 | tf_op jit(solution)/shard_map/all_to_all | solution.py:51
Sparse Core Ops, SparseCore 0:
  10.2 84.6 all-gather.3
  153.7 37.5 reduce-scatter.1

commit v5 on v4

--- a/solution.py
+++ b/solution.py
@@ -1,7 +1,9 @@
 import jax
 import jax.numpy as jnp
 from jax import lax
+from jax.experimental import pallas as pl
 from jax.experimental.layout import Layout, with_layout_constraint
+from jax.experimental.pallas import tpu as pltpu
 from jax.sharding import Mesh
 from jax.sharding import PartitionSpec as P
 
@@ -75,6 +77,27 @@
     return lax.ppermute(x, axis, [(i, (i + shift) % size) for i in range(size)])
 
 
+def product_kernel(*refs):
+    rows_ref, block_refs, total_ref = refs[0], refs[1:-1], refs[-1]
+    column, total = 0, 0.0
+    for block_ref in block_refs:
+        size = block_ref.shape[1]
+        piece = rows_ref[:, column : column + size]
+        total, column = total + dot(piece, block_ref[...], LAST), column + size
+    total_ref[...] = total
+
+
+def product(rows, blocks):
+    return pl.pallas_call(
+        product_kernel,
+        out_shape=jax.ShapeDtypeStruct((rows.shape[0], blocks[0].shape[0]), F32),
+        in_specs=[pl.BlockSpec(memory_space=pltpu.VMEM)] * (1 + len(blocks)),
+        out_specs=pl.BlockSpec(memory_space=pltpu.VMEM),
+        compiler_params=pltpu.CompilerParams(vmem_limit_bytes=24 * 1024 * 1024),
+        cost_estimate=pl.CostEstimate(flops=1000, bytes_accessed=1000, transcendentals=0),
+    )(rows, *blocks)
+
+
 def roll_columns(x, start):
     return lax.dynamic_slice_in_dim(jnp.concatenate([x, x], axis=1), start, x.shape[1], axis=1)
 
@@ -98,10 +121,14 @@
     from_last = pass_on(own_down, "x", 1)
 
     turned = roll_columns(cotangent, group * quarter)
-    packed = jnp.concatenate([tokens, turned, meta_columns(expert_ids, gate_probs)], axis=1)
+    packed = jnp.concatenate([tokens, meta_columns(expert_ids, gate_probs), turned], axis=1)
+    wide = width + META
     by_z = lax.all_gather(packed[None], ("zh", "zl"), axis=0, tiled=True)
     by_z, from_next, from_last = lax.optimization_barrier((by_z, from_next, from_last))
-    plane = gather_by_exchange(by_z.reshape(-1, packed.shape[1]), "y", y_size)
+    by_z = by_z.reshape(-1, packed.shape[1])
+    plane = gather_by_exchange(by_z[:, :wide], "y", y_size)
+    cot_z, plane = lax.optimization_barrier((by_z[:, wide:], plane))
+    cot_plane = gather_by_exchange(cot_z, "y", y_size)
     if quarters == 4:
         cut = quarter // 2
         across = pass_on(from_next[:, :cut], "x", -1), pass_on(from_last[:, cut:], "x", 1)
@@ -111,15 +138,18 @@
         downs = [own_down, from_next]
 
     count = plane.shape[0]
-    code = plane[:, 2 * width : 2 * width + 2].astype(jnp.int32)
+    code = plane[:, width : width + 2].astype(jnp.int32)
     place = lax.broadcasted_iota(jnp.int32, (count, 1), 0)
     table_own = slot_table(code, place, expert, block)
     table_other = slot_table(code, place, other, block)
     half = table_own.shape[1]
-    rows_own = dot(table_own, plane, FIRST).astype(BF16)
-    rows_other = dot(table_other, plane, FIRST).astype(BF16)
-    rows_arrived = lax.ppermute(rows_other, "c", [(0, 1), (1, 0)])
-    rows = jnp.concatenate([rows_own, rows_arrived], axis=0)
+
+    def arrive(x):
+        rows_other = dot(table_other, x, FIRST).astype(BF16)
+        arrived = lax.ppermute(rows_other, "c", [(0, 1), (1, 0)])
+        return jnp.concatenate([dot(table_own, x, FIRST).astype(BF16), arrived], axis=0)
+
+    rows = arrive(plane)
 
     def low_first(x):
         split = x.reshape(y_size, high_size, low_size, block, x.shape[1])
@@ -130,14 +160,13 @@
     back_own = slot_table(code_back, place_back, expert, block)
     back_other = slot_table(code_back, place_back, other, block)
 
-    about = rows[:, 2 * width :].astype(F32)
+    about = rows[:, width:].astype(F32)
     slot = lax.broadcasted_iota(jnp.int32, (2 * half, 1), 0)
     first = about[:, 0:1].astype(jnp.int32) == expert * CAP + slot % CAP
     prob0 = about[:, 2:3] + about[:, 4:5] + about[:, 6:7]
     prob1 = about[:, 3:4] + about[:, 5:6] + about[:, 7:8]
     prob = jnp.where(first, prob0, prob1)
     token_rows = rows[:, :width]
-    cot_rows = (prob * rows[:, width : 2 * width].astype(F32)).astype(BF16)
 
     def leave(part):
         returned = lax.ppermute(part[half:], "c", [(0, 1), (1, 0)])
@@ -153,24 +182,22 @@
     out_tokens = leave(out_part)
     out_y = scatter_sum_by_exchange(out_tokens, "y", y_size)
 
-    late_cot, _ = lax.optimization_barrier((cot_rows, out_part))
-    grad_hidden, column = 0.0, 0
-    for down in downs:
-        piece = late_cot[:, column : column + down.shape[1]]
-        grad_hidden, column = grad_hidden + dot(piece, down, LAST), column + down.shape[1]
+    cot_plane, _ = lax.optimization_barrier((cot_plane, out_tokens))
+    cot_rows = (prob * arrive(cot_plane).astype(F32)).astype(BF16)
+    grad_hidden = product(cot_rows, downs)
     grad_up = (grad_hidden * activated).astype(BF16)
     grad_gate = (grad_hidden * up_pre * slope_gate).astype(BF16)
     grad_both = jnp.concatenate([grad_gate, grad_up], axis=1)
-    grad_both, late_hidden, _ = lax.optimization_barrier((grad_both, hidden, out_tokens))
     grad_tokens = leave(dot(grad_both, full_both, LAST).astype(BF16))
+    out_y, grad_tokens = lax.optimization_barrier((out_y, grad_tokens))
+
+    late_hidden, late_cot, _ = lax.optimization_barrier((hidden, cot_rows, grad_tokens))
     partial_down = []
     for q in range(quarters):
         start = lax.rem(q - group + quarters, quarters) * quarter
         block_q = lax.dynamic_slice_in_dim(late_cot, start, quarter, axis=1)
         partial_down.append(dot(late_hidden, block_q, FIRST).astype(BF16))
-    partial_down = jnp.stack(partial_down)
-    out_y, grad_tokens, partial_down = lax.optimization_barrier((out_y, grad_tokens, partial_down))
-    down_grads = lax.psum_scatter(partial_down, "x", scatter_dimension=0)[None]
+    down_grads = lax.psum_scatter(jnp.stack(partial_down), "x", scatter_dimension=0)[None]
 
     grad_y = scatter_sum_by_exchange(grad_tokens, "y", y_size)
     out_low = add_up(send_by_shifts(out_y, "zl", low_size))

time: 225 us -> 244 us (1.084)
  starting transfers between devices: 50 us -> 59 us
  local copies, waits for them, and re-layouts: 11 us -> 18.2 us
  waiting for transfers between devices: 57.2 us -> 50.4 us
  blocking collectives: 49.3 us -> 52.6 us
  matrix products: 29 us -> 31.8 us
    ppermute x4, waiting for transfers between devices: 19.2 us -> 7.76 us  [pass_on(): return lax.ppermute(x, axis, [(i, (i + shift) % size) for i in range(size)])]
    all_to_all x1 -> x2, starting transfers between devices: 4.65 us -> 9.3 us  [gather_by_exchange(): lax.all_to_all(spread, axes, split_axis=0, concat_axis=0, tiled=True)]
    unnamed x29 -> x59, local copies, waits for them, and re-layouts: 1.79 us -> 6.36 us
    all_gather x1, blocking collectives: 36.2 us -> 39.6 us  [on_device(): by_z = lax.all_gather(packed[None], ('zh', 'zl'), axis=0, tiled=True)]
    all_to_all x1 -> x2, waiting for transfers between devices: 4.79 us -> 7.97 us  [gather_by_exchange(): lax.all_to_all(spread, axes, split_axis=0, concat_axis=0, tiled=True)]
    all_to_all x3, waiting for transfers between devices: 25.6 us -> 28.3 us  [scatter_sum_by_exchange(): parts = lax.all_to_all(parts, axes, split_axis=0, concat_axis=0, tiled=True)]
    dot_general x22 -> x19, matrix products: 29 us -> 31.8 us  [dot(): return lax.dot_general(a, b, dims, preferred_element_type=F32)]
  transfers between devices with their start and end apart: 16 -> 18, of which waited for: 9 -> 10; matrix products, arithmetic and copies ran while one was open for 14% -> 18% of each run, Pallas kernels for 0% -> 0%
where the time goes in v5:
time: 244 us; the launch traced here: 240 us
  starting transfers between devices  59 us (24%)
  blocking collectives  52.6 us (22%)
  waiting for transfers between devices  50.4 us (21%)
  matrix products  31.8 us (13%)
  local copies, waits for them, and re-layouts  18.2 us (7%)
  between operations  14.8 us (6%)
  other arithmetic  12.1 us (5%)
    all_gather x1, blocking collectives, on_device(): by_z = lax.all_gather(packed[None], ('zh', 'zl'), axis=0, tiled=True)  39.6 us
    dot_general x19, matrix products, dot(): return lax.dot_general(a, b, dims, preferred_element_type=F32)  31.8 us
    all_to_all x3, waiting for transfers between devices, scatter_sum_by_exchange(): parts = lax.all_to_all(parts, axes, split_axis=0, concat_axis=0, tiled=True)  28.3 us
    ppermute x4, starting transfers between devices, pass_on(): return lax.ppermute(x, axis, [(i, (i + shift) % size) for i in range(size)])  16.7 us
    all_to_all x3, starting transfers between devices, scatter_sum_by_exchange(): parts = lax.all_to_all(parts, axes, split_axis=0, concat_axis=0, tiled=True)  15.5 us
    all_to_all x1, blocking collectives, scatter_sum_by_exchange(): parts = lax.all_to_all(parts, axes, split_axis=0, concat_axis=0, tiled=True)  13 us
    all_to_all x2, starting transfers between devices, gather_by_exchange(): lax.all_to_all(spread, axes, split_axis=0, concat_axis=0, tiled=True)  9.3 us
    ppermute x3, starting transfers between devices, send_by_shifts(): parts.append(lax.ppermute(block(shift), axis, pairs))  8.92 us
  transfers between devices with their start and end apart: 18, of which 10 were waited for; matrix products, arithmetic and copies ran while one was open for 18% of the time, Pallas kernels for 0%

profile of v5, /device:TPU:6, one launch (start us, length us, event | category | flops | bytes accessed | tf_op | source)
XLA Modules:
  0.0 240.0 jit_solution(2783310600134722289)
XLA Ops:
  7.2 2.8 %pad_maximum_fusion.3 = bf16[768,1024]{1,0:T(8,128)(2,1)} fusion(bf16[768,512]{1,0:T(8,128)(2,1)} %bitcast.57, bf16[768,512]{1,0:T(8,128)(2,1)} %bitcast.58), kind=kLoop, calls=%fused_computation.14 | loop fusion | flops 3145728 | bytes 3145728 | tf_op jit(solution)/shard_map/concatenate | solution.py:116
  11.1 2.7 %collective-permute-start = (bf16[512,768]{1,0:T(8,128)(2,1)S(1)}, bf16[512,768]{1,0:T(8,128)(2,1)S(1)}, u32[]{:S(2)}, u32[]{:S(2)}) collective-permute-start(bf16[512,768]{1,0:T(8,128)(2,1)S(1)} %bitcast.50), channel_id=1, source_target_pairs={{0,384},{128,0},{256,128},{384,256},{1,385},{129,1},{257,129},{385... | collective-permute-start | bytes 2359304 | tf_op jit(solution)/shard_map/ppermute | solution.py:77
  13.9 6.9 %collective-permute-start.1 = (bf16[512,768]{1,0:T(8,128)(2,1)S(1)}, bf16[512,768]{1,0:T(8,128)(2,1)S(1)}, u32[]{:S(2)}, u32[]{:S(2)}) collective-permute-start(bf16[512,768]{1,0:T(8,128)(2,1)S(1)} %bitcast.51), channel_id=1, source_target_pairs={{0,128},{128,256},{256,384},{384,0},{1,129},{129,257},{257,385},{3... | collective-permute-start | bytes 2359304 | tf_op jit(solution)/shard_map/ppermute | solution.py:77
  21.4 39.6 %all-gather.1 = bf16[16,4,6272]{2,1,0:T(4,128)(2,1)} all-gather(bf16[1,4,6272]{2,1,0:T(4,128)(2,1)S(1)} %fusion.41), channel_id=2, replica_groups=mesh['x'=4,'zl'=4,'c'=2,'zh'=4,'y'=4] {'zh','zl'}, dimensions={0}, use_global_device_ids=true | all-gather | bytes 852992 | tf_op jit(solution)/shard_map/all_gather | solution.py:126
  61.0 2.4 %reshape.280 = bf16[64,6272]{1,0:T(8,128)(2,1)} reshape(bf16[16,4,6272]{2,1,0:T(4,128)(2,1)} %all-gather.1) | data formatting | bytes 1605632 | tf_op jit(solution)/shard_map/reshape | solution.py:128
  65.7 4.8 %all-to-all-start = ((bf16[4,64,3200]{2,1,0:T(8,128)(2,1)}), bf16[4,64,3200]{2,1,0:T(8,128)(2,1)}, u32[]{:S(2)}, u32[]{:S(2)}) async-start(bf16[4,64,3200]{2,1,0:T(8,128)(2,1)} %broadcast_in_dim.7), calls=%async_computation | async-start | bytes 3276800 | tf_op jit(solution)/shard_map/all_to_all | solution.py:46
  71.3 2.0 collective-permute-start.2
  74.1 5.0 %collective-permute-start.3 = (bf16[512,384]{1,0:T(8,128)(2,1)}, bf16[512,384]{1,0:T(8,128)(2,1)S(1)}, u32[]{:S(2)}, u32[]{:S(2)}) collective-permute-start(bf16[512,384]{1,0:T(8,128)(2,1)} %slice.85), channel_id=1, source_target_pairs={{0,128},{128,256},{256,384},{384,0},{1,129},{129,257},{257,385},{3... | collective-permute-start | bytes 1179656 | tf_op jit(solution)/shard_map/ppermute | solution.py:77
  79.6 6.6 %all-to-all-done = bf16[4,64,3200]{2,1,0:T(8,128)(2,1)} async-done(((bf16[4,64,3200]{2,1,0:T(8,128)(2,1)}), bf16[4,64,3200]{2,1,0:T(8,128)(2,1)}, u32[]{:S(2)}, u32[]{:S(2)}) %all-to-all-start) | async-done | bytes 1638432 | tf_op jit(solution)/shard_map/all_to_all | solution.py:46
  86.3 6.3 %collective-permute-done.2.refs_3_ = bf16[512,384]{1,0:T(8,128)(2,1)S(1)} collective-permute-done((bf16[512,384]{1,0:T(8,128)(2,1)}, bf16[512,384]{1,0:T(8,128)(2,1)S(1)}, u32[]{:S(2)}, u32[]{:S(2)}) %collective-permute-start.2) | collective-permute-done | bytes 393248 | tf_op jit(solution)/shard_map/ppermute | solution.py:77
  95.8 2.9 %convolution_convert_fusion = bf16[128,3200]{1,0:T(8,128)(2,1)} fusion(bf16[256,3200]{1,0:T(8,128)(2,1)} %bitcast.4, s32[128]{0:T(128)} %get-tuple-element.52, s32[128]{0:T(128)S(1)} %get-tuple-element.51, s32[256]{0:T(256)S(1)} %and_select_fusion, s32[256]{0:T(256)S(1)} %get-tuple-element.38, s32[256]{0:T(256)S(1)} %get-tuple-element.37), kind=kOutput, calls=%fused_computation | convolution fusion | flops 210288640 | bytes 2461696 | tf_op jit(solution)/shard_map/dot_general | solution.py:19
  102.5 4.5 %all-to-all-start.2 = ((bf16[4,64,3072]{2,1,0:T(8,128)(2,1)}), bf16[4,64,3072]{2,1,0:T(8,128)(2,1)}, u32[]{:S(2)}, u32[]{:S(2)}) async-start(bf16[4,64,3072]{2,1,0:T(8,128)(2,1)} %broadcast_in_dim.8), calls=%async_computation.2 | async-start | bytes 3145728 | tf_op jit(solution)/shard_map/all_to_all | solution.py:46
  107.1 2.0 convolution_convert_fusion.1
  111.1 5.1 %fusion.2 = f32[256,1024]{1,0:T(8,128)S(1)} fusion(bf16[3072,1024]{1,0:T(8,128)(2,1)} %all-gather.4.cloned.1.call-done, bf16[128,3200]{1,0:T(8,128)(2,1)} %collective-permute-done.4, bf16[128,3200]{1,0:T(8,128)(2,1)} %copy-done.8), kind=kOutput, calls=%fused_computation.12 | convolution fusion | flops 1613758464 | bytes 8978432 | tf_op jit(solution)/shard_map/dot_general | solution.py:19
  120.5 2.4 collective-permute-start.5
  132.7 2.0 convolution_convert_fusion.4
  135.4 4.4 %all-to-all-start.1 = ((bf16[4,64,3072]{2,1,0:T(8,128)(2,1)}), bf16[4,64,3072]{2,1,0:T(8,128)(2,1)}, u32[]{:S(2)}, u32[]{:S(2)}) async-start(bf16[4,64,3072]{2,1,0:T(8,128)(2,1)} %bitcast.54), calls=%async_computation.1 | async-start | bytes 3145728 | tf_op jit(solution)/shard_map/all_to_all | solution.py:53
  143.7 4.6 %convolution_convert_fusion.2 = bf16[256,3072]{1,0:T(8,128)(2,1)S(1)} fusion(bf16[3072,1024]{1,0:T(8,128)(2,1)} %all-gather.4.cloned.1.call-done, bf16[256,512]{1,0:T(8,128)(2,1)S(1)} %get-tuple-element.40, bf16[256,512]{1,0:T(8,128)(2,1)S(1)} %get-tuple-element.39), kind=kOutput, calls=%fused_computation.6 | convolution fusion | flops 1612447744 | bytes 8388608 | tf_op jit(solution)/shard_map/dot_general | solution.py:19
  149.3 2.1 collective-permute-start.7
  151.5 2.3 fusion.18
  153.8 7.5 %all-to-all-done.1 = bf16[4,64,3072]{2,1,0:T(8,128)(2,1)} async-done(((bf16[4,64,3072]{2,1,0:T(8,128)(2,1)}), bf16[4,64,3072]{2,1,0:T(8,128)(2,1)}, u32[]{:S(2)}, u32[]{:S(2)}) %all-to-all-start.1) | async-done | bytes 1572896 | tf_op jit(solution)/shard_map/all_to_all | solution.py:53
  163.0 4.0 %fusion.1 = bf16[256,3072]{1,0:T(8,128)(2,1)} fusion(f32[256,3072]{1,0:T(8,128)} %fusion.18, bf16[128,3072]{1,0:T(8,128)(2,1)} %collective-permute-done.7, s32[128]{0:T(128)S(1)} %copy-done.22, s32[128]{0:T(128)S(1)} %get-tuple-element.51, s32[256]{0:T(256)S(1)} %and_select_fusion.2, s32[256]{0:T(256)S(1)} %bitcast.67, s32[256]{0:T(256)S(1)} %bitcast.63), kind=kOutput, calls=%fused_computation.5 | convolution fusion | flops 203063296 | bytes 5509120 | tf_op jit(solution)/shard_map/dot_general | solution.py:19
  170.4 3.6 %all-to-all-start.3 = ((bf16[4,64,3072]{2,1,0:T(8,128)(2,1)}), bf16[4,64,3072]{2,1,0:T(8,128)(2,1)S(1)}, u32[]{:S(2)}, u32[]{:S(2)}) async-start(bf16[4,64,3072]{2,1,0:T(8,128)(2,1)} %bitcast.12), calls=%async_computation.3 | async-start | bytes 3145728 | tf_op jit(solution)/shard_map/all_to_all | solution.py:53
  174.1 2.4 collective-permute-start.10
  176.5 3.5 %collective-permute-start.8 = (bf16[16,3072]{1,0:T(8,128)(2,1)S(1)}, bf16[16,3072]{1,0:T(8,128)(2,1)S(1)}, u32[]{:S(2)}, u32[]{:S(2)}) collective-permute-start(bf16[16,3072]{1,0:T(8,128)(2,1)S(1)} %get-tuple-element.41), channel_id=1, source_target_pairs={{0,32},{32,64},{64,96},{96,0},{1,33},{33,65},{65,97},{97,1},{2,34}... | collective-permute-start | bytes 294920 | tf_op jit(solution)/shard_map/ppermute | solution.py:67
  179.9 3.1 %collective-permute-start.9 = (bf16[16,3072]{1,0:T(8,128)(2,1)S(1)}, bf16[16,3072]{1,0:T(8,128)(2,1)S(1)}, u32[]{:S(2)}, u32[]{:S(2)}) collective-permute-start(bf16[16,3072]{1,0:T(8,128)(2,1)S(1)} %get-tuple-element.43), channel_id=1, source_target_pairs={{0,64},{32,96},{64,0},{96,32},{1,65},{33,97},{65,1},{97,33},{2,66}... | collective-permute-start | bytes 294920 | tf_op jit(solution)/shard_map/ppermute | solution.py:67
  183.0 2.3 collective-permute-done.8
  185.3 3.7 %collective-permute-done.9 = bf16[16,3072]{1,0:T(8,128)(2,1)S(1)} collective-permute-done((bf16[16,3072]{1,0:T(8,128)(2,1)S(1)}, bf16[16,3072]{1,0:T(8,128)(2,1)S(1)}, u32[]{:S(2)}, u32[]{:S(2)}) %collective-permute-start.9) | collective-permute-done | bytes 98336 | tf_op jit(solution)/shard_map/ppermute | solution.py:67
  189.0 5.5 %all-to-all-done.3 = bf16[4,64,3072]{2,1,0:T(8,128)(2,1)S(1)} async-done(((bf16[4,64,3072]{2,1,0:T(8,128)(2,1)}), bf16[4,64,3072]{2,1,0:T(8,128)(2,1)S(1)}, u32[]{:S(2)}, u32[]{:S(2)}) %all-to-all-start.3) | async-done | bytes 1572896 | tf_op jit(solution)/shard_map/all_to_all | solution.py:53
  194.9 13.0 %all_to_all.30 = bf16[4,16,3072]{2,1,0:T(8,128)(2,1)S(1)} all-to-all(bf16[4,16,3072]{2,1,0:T(8,128)(2,1)S(1)} %bitcast.56), channel_id=1, replica_groups=mesh['x'=4,'zl'=4,'c'=2,'zh'=4,'y'=4] {'zl'}, dimensions={0} | all-to-all | bytes 786432 | tf_op jit(solution)/shard_map/all_to_all | solution.py:53
  208.7 7.5 %all-to-all-start.5 = ((bf16[4,4,6144]{2,1,0:T(4,128)(2,1)}), bf16[4,4,6144]{2,1,0:T(4,128)(2,1)S(1)}, u32[]{:S(2)}, u32[]{:S(2)}) async-start(bf16[4,4,6144]{2,1,0:T(4,128)(2,1)} %reshape.289), calls=%async_computation.5 | async-start | bytes 393216 | tf_op jit(solution)/shard_map/all_to_all | solution.py:53
  216.3 15.4 %all-to-all-done.5 = bf16[4,4,6144]{2,1,0:T(4,128)(2,1)S(1)} async-done(((bf16[4,4,6144]{2,1,0:T(4,128)(2,1)}), bf16[4,4,6144]{2,1,0:T(4,128)(2,1)S(1)}, u32[]{:S(2)}, u32[]{:S(2)}) %all-to-all-start.5) | async-done | bytes 196640 | tf_op jit(solution)/shard_map/all_to_all | solution.py:53
  (132 shorter events, 42.4 us)
Async XLA Ops:
  7.2 104.0 %all-gather.4.cloned.1.call-start = ((), (), s32[]{:S(2)}) async-start(), calls=%async_computation.7 | async-start | bytes 7864320 | tf_op jit(solution)/shard_map/all_gather | solution.py:119
  10.0 10.8 %copy-start.20 = (s32[4,2]{0,1:T(2,128)S(1)}, s32[4,2]{0,1:T(2,128)}, u32[]{:S(2)}) copy-start(s32[4,2]{0,1:T(2,128)} %param.8) | copy-start | bytes 100
  10.0 11.1 %copy-start.28 = (f32[4,2]{0,1:T(2,128)S(1)}, f32[4,2]{0,1:T(2,128)}, u32[]{:S(2)}) copy-start(f32[4,2]{0,1:T(2,128)} %param.9) | copy-start | bytes 100
  10.0 11.2 %copy-start.16 = (bf16[4,3072]{1,0:T(4,128)(2,1)S(1)}, bf16[4,3072]{1,0:T(4,128)(2,1)}, u32[]{:S(2)}) copy-start(bf16[4,3072]{1,0:T(4,128)(2,1)} %param.13) | copy-start | bytes 73732
  10.0 11.4 %copy-start.17 = (bf16[4,3072]{1,0:T(4,128)(2,1)S(1)}, bf16[4,3072]{1,0:T(4,128)(2,1)}, u32[]{:S(2)}) copy-start(bf16[4,3072]{1,0:T(4,128)(2,1)} %param.7) | copy-start | bytes 73732
  11.1 49.9 %collective-permute-start = (bf16[512,768]{1,0:T(8,128)(2,1)S(1)}, bf16[512,768]{1,0:T(8,128)(2,1)S(1)}, u32[]{:S(2)}, u32[]{:S(2)}) collective-permute-start(bf16[512,768]{1,0:T(8,128)(2,1)S(1)} %bitcast.50), channel_id=1, source_target_pairs={{0,384},{128,0},{256,128},{384,256},{1,385},{129,1},{257,129},{385... | collective-permute-start | bytes 2359304 | tf_op jit(solution)/shard_map/ppermute | solution.py:77
  13.9 47.1 %collective-permute-start.1 = (bf16[512,768]{1,0:T(8,128)(2,1)S(1)}, bf16[512,768]{1,0:T(8,128)(2,1)S(1)}, u32[]{:S(2)}, u32[]{:S(2)}) collective-permute-start(bf16[512,768]{1,0:T(8,128)(2,1)S(1)} %bitcast.51), channel_id=1, source_target_pairs={{0,128},{128,256},{256,384},{384,0},{1,129},{129,257},{257,385},{3... | collective-permute-start | bytes 2359304 | tf_op jit(solution)/shard_map/ppermute | solution.py:77
  65.7 20.6 %all-to-all-start = ((bf16[4,64,3200]{2,1,0:T(8,128)(2,1)}), bf16[4,64,3200]{2,1,0:T(8,128)(2,1)}, u32[]{:S(2)}, u32[]{:S(2)}) async-start(bf16[4,64,3200]{2,1,0:T(8,128)(2,1)} %broadcast_in_dim.7), calls=%async_computation | async-start | bytes 3276800 | tf_op jit(solution)/shard_map/all_to_all | solution.py:46
  71.3 21.3 %collective-permute-start.2 = (bf16[512,384]{1,0:T(8,128)(2,1)}, bf16[512,384]{1,0:T(8,128)(2,1)S(1)}, u32[]{:S(2)}, u32[]{:S(2)}) collective-permute-start(bf16[512,384]{1,0:T(8,128)(2,1)} %slice.84), channel_id=1, source_target_pairs={{0,384},{128,0},{256,128},{384,256},{1,385},{129,1},{257,129},{385... | collective-permute-start | bytes 1179656 | tf_op jit(solution)/shard_map/ppermute | solution.py:77
  74.1 20.0 %collective-permute-start.3 = (bf16[512,384]{1,0:T(8,128)(2,1)}, bf16[512,384]{1,0:T(8,128)(2,1)S(1)}, u32[]{:S(2)}, u32[]{:S(2)}) collective-permute-start(bf16[512,384]{1,0:T(8,128)(2,1)} %slice.85), channel_id=1, source_target_pairs={{0,128},{128,256},{256,384},{384,0},{1,129},{129,257},{257,385},{3... | collective-permute-start | bytes 1179656 | tf_op jit(solution)/shard_map/ppermute | solution.py:77
  79.1 27.9 %copy-start.18 = (s32[256]{0:T(256)}, s32[256]{0:T(256)S(1)}, u32[]{:S(2)}) copy-start(s32[256]{0:T(256)S(1)} %and_select_fusion) | copy-start | bytes 3076
  79.6 21.5 %slice-start = ((bf16[64,6272]{1,0:T(8,128)(2,1)}), bf16[64,3072]{1,0:T(8,128)(2,1)S(1)}, s32[]{:S(2)}) async-start(bf16[64,6272]{1,0:T(8,128)(2,1)} %reshape.280), calls=%async_computation.9 | async-start | bytes 786432 | tf_op jit(solution)/shard_map/slice | solution.py:130
  94.0 23.6 %copy-start.2 = (bf16[512,384]{1,0:T(8,128)(2,1)}, bf16[512,384]{1,0:T(8,128)(2,1)S(1)}, u32[]{:S(2)}) copy-start(bf16[512,384]{1,0:T(8,128)(2,1)S(1)} %collective-permute-done.3.refs_4_) | copy-start | bytes 1179652
  98.7 10.4 %collective-permute-start.4 = (bf16[128,3200]{1,0:T(8,128)(2,1)}, bf16[128,3200]{1,0:T(8,128)(2,1)}, u32[]{:S(2)}, u32[]{:S(2)}) collective-permute-start(bf16[128,3200]{1,0:T(8,128)(2,1)} %convolution_convert_fusion), channel_id=1, source_target_pairs={{0,16},{16,0},{1,17},{17,1},{2,18},{18,2},{3,19},{19,3},{4,20},{20... | collective-permute-start | bytes 2457608 | tf_op jit(solution)/shard_map/ppermute | solution.py:149
  102.5 4.6 %copy-start.23 = (s32[128]{0:T(128)S(1)}, s32[128]{0:T(128)}, u32[]{:S(2)}) copy-start(s32[128]{0:T(128)} %fusion.49) | copy-start | bytes 1540
  102.5 26.3 %all-to-all-start.2 = ((bf16[4,64,3072]{2,1,0:T(8,128)(2,1)}), bf16[4,64,3072]{2,1,0:T(8,128)(2,1)}, u32[]{:S(2)}, u32[]{:S(2)}) async-start(bf16[4,64,3072]{2,1,0:T(8,128)(2,1)} %broadcast_in_dim.8), calls=%async_computation.2 | async-start | bytes 3145728 | tf_op jit(solution)/shard_map/all_to_all | solution.py:46
  111.1 6.8 %copy-start.26 = (f32[256]{0:T(256)}, f32[256]{0:T(256)S(1)}, u32[]{:S(2)}) copy-start(f32[256]{0:T(256)S(1)} %fusion.33) | copy-start | bytes 3076
  117.9 5.1 %copy-start.10 = (s32[256,2]{1,0:T(8,128)S(1)}, s32[256,2]{1,0:T(8,128)}, u32[]{:S(2)}) copy-start(s32[256,2]{1,0:T(8,128)} %copy-done.9) | copy-start | bytes 6148
  118.0 5.8 %copy-start.24 = (s32[128]{0:T(128)S(1)}, s32[128]{0:T(128)}, u32[]{:S(2)}) copy-start(s32[128]{0:T(128)} %fusion.49) | copy-start | bytes 1540
  120.5 5.0 %collective-permute-start.5 = (bf16[128,3072]{1,0:T(8,128)(2,1)}, bf16[128,3072]{1,0:T(8,128)(2,1)S(1)}, u32[]{:S(2)}, u32[]{:S(2)}) collective-permute-start(bf16[128,3072]{1,0:T(8,128)(2,1)} %slice.124), channel_id=1, source_target_pairs={{0,16},{16,0},{1,17},{17,1},{2,18},{18,2},{3,19},{19,3},{4,20},{20... | collective-permute-start | bytes 2359304 | tf_op jit(solution)/shard_map/ppermute | solution.py:172
  130.7 4.2 %copy-start.27 = (f32[256]{0:T(256)S(1)}, f32[256]{0:T(256)}, u32[]{:S(2)}) copy-start(f32[256]{0:T(256)} %copy-done.26) | copy-start | bytes 3076
  130.8 4.2 %collective-permute-start.6 = (bf16[128,3072]{1,0:T(8,128)(2,1)S(1)}, bf16[128,3072]{1,0:T(8,128)(2,1)S(1)}, u32[]{:S(2)}, u32[]{:S(2)}) collective-permute-start(bf16[128,3072]{1,0:T(8,128)(2,1)S(1)} %convolution_convert_fusion.3), channel_id=1, source_target_pairs={{0,16},{16,0},{1,17},{17,1},{2,18},{18,2},{3,19},{19,3},{4,20},{20... | collective-permute-start | bytes 2359304 | tf_op jit(solution)/shard_map/ppermute | solution.py:149
  135.4 25.8 %all-to-all-start.1 = ((bf16[4,64,3072]{2,1,0:T(8,128)(2,1)}), bf16[4,64,3072]{2,1,0:T(8,128)(2,1)}, u32[]{:S(2)}, u32[]{:S(2)}) async-start(bf16[4,64,3072]{2,1,0:T(8,128)(2,1)} %bitcast.54), calls=%async_computation.1 | async-start | bytes 3145728 | tf_op jit(solution)/shard_map/all_to_all | solution.py:53
  139.8 93.3 %reduce-scatter.2.cloned.1.call-start = ((), (), s32[]{:S(2)}) async-start(), calls=%async_computation.8 | async-start | bytes 3932160 | tf_op jit(solution)/shard_map/reduce_scatter | solution.py:200
  149.3 13.6 %collective-permute-start.7 = (bf16[128,3072]{1,0:T(8,128)(2,1)}, bf16[128,3072]{1,0:T(8,128)(2,1)}, u32[]{:S(2)}, u32[]{:S(2)}) collective-permute-start(bf16[128,3072]{1,0:T(8,128)(2,1)} %slice.126), channel_id=1, source_target_pairs={{0,16},{16,0},{1,17},{17,1},{2,18},{18,2},{3,19},{19,3},{4,20},{20... | collective-permute-start | bytes 2359304 | tf_op jit(solution)/shard_map/ppermute | solution.py:172
  153.8 9.2 %copy-start.22 = (s32[128]{0:T(128)S(1)}, s32[128]{0:T(128)}, u32[]{:S(2)}) copy-start(s32[128]{0:T(128)} %get-tuple-element.52) | copy-start | bytes 1540
  162.9 4.0 %copy-start.5 = (bf16[256,512]{1,0:T(8,128)(2,1)S(1)}, bf16[256,512]{1,0:T(8,128)(2,1)}, u32[]{:S(2)}) copy-start(bf16[256,512]{1,0:T(8,128)(2,1)} %copy-done.4) | copy-start | bytes 786436
  170.4 24.1 %all-to-all-start.3 = ((bf16[4,64,3072]{2,1,0:T(8,128)(2,1)}), bf16[4,64,3072]{2,1,0:T(8,128)(2,1)S(1)}, u32[]{:S(2)}, u32[]{:S(2)}) async-start(bf16[4,64,3072]{2,1,0:T(8,128)(2,1)} %bitcast.12), calls=%async_computation.3 | async-start | bytes 3145728 | tf_op jit(solution)/shard_map/all_to_all | solution.py:53
  174.1 9.0 %collective-permute-start.10 = (bf16[16,3072]{1,0:T(8,128)(2,1)S(1)}, bf16[16,3072]{1,0:T(8,128)(2,1)S(1)}, u32[]{:S(2)}, u32[]{:S(2)}) collective-permute-start(bf16[16,3072]{1,0:T(8,128)(2,1)S(1)} %get-tuple-element.42), channel_id=1, source_target_pairs={{0,96},{32,0},{64,32},{96,64},{1,97},{33,1},{65,33},{97,65},{2,98}... | collective-permute-start | bytes 294920 | tf_op jit(solution)/shard_map/ppermute | solution.py:67
  176.5 8.8 %collective-permute-start.8 = (bf16[16,3072]{1,0:T(8,128)(2,1)S(1)}, bf16[16,3072]{1,0:T(8,128)(2,1)S(1)}, u32[]{:S(2)}, u32[]{:S(2)}) collective-permute-start(bf16[16,3072]{1,0:T(8,128)(2,1)S(1)} %get-tuple-element.41), channel_id=1, source_target_pairs={{0,32},{32,64},{64,96},{96,0},{1,33},{33,65},{65,97},{97,1},{2,34}... | collective-permute-start | bytes 294920 | tf_op jit(solution)/shard_map/ppermute | solution.py:67
  179.9 9.1 %collective-permute-start.9 = (bf16[16,3072]{1,0:T(8,128)(2,1)S(1)}, bf16[16,3072]{1,0:T(8,128)(2,1)S(1)}, u32[]{:S(2)}, u32[]{:S(2)}) collective-permute-start(bf16[16,3072]{1,0:T(8,128)(2,1)S(1)} %get-tuple-element.43), channel_id=1, source_target_pairs={{0,64},{32,96},{64,0},{96,32},{1,65},{33,97},{65,1},{97,33},{2,66}... | collective-permute-start | bytes 294920 | tf_op jit(solution)/shard_map/ppermute | solution.py:67
  208.7 22.9 %all-to-all-start.5 = ((bf16[4,4,6144]{2,1,0:T(4,128)(2,1)}), bf16[4,4,6144]{2,1,0:T(4,128)(2,1)S(1)}, u32[]{:S(2)}, u32[]{:S(2)}) async-start(bf16[4,4,6144]{2,1,0:T(4,128)(2,1)} %reshape.289), calls=%async_computation.5 | async-start | bytes 393216 | tf_op jit(solution)/shard_map/all_to_all | solution.py:53
  (16 other events, 28.0 us)
Sparse Core Ops, SparseCore 0:
  10.2 84.6 all-gather.3
  170.6 39.5 reduce-scatter.1

commit v6 on v4

--- a/solution.py
+++ b/solution.py
@@ -1,7 +1,9 @@
 import jax
 import jax.numpy as jnp
 from jax import lax
+from jax.experimental import pallas as pl
 from jax.experimental.layout import Layout, with_layout_constraint
+from jax.experimental.pallas import tpu as pltpu
 from jax.sharding import Mesh
 from jax.sharding import PartitionSpec as P
 
@@ -75,6 +77,60 @@
     return lax.ppermute(x, axis, [(i, (i + shift) % size) for i in range(size)])
 
 
+VMEM = pl.BlockSpec(memory_space=pltpu.VMEM)
+PARAMS = pltpu.CompilerParams(vmem_limit_bytes=24 * 1024 * 1024)
+
+
+def product_kernel(*refs):
+    rows_ref, block_refs, total_ref = refs[0], refs[1:-1], refs[-1]
+    column, total = 0, 0.0
+    for block_ref in block_refs:
+        size = block_ref.shape[1]
+        piece = rows_ref[:, column : column + size]
+        total, column = total + dot(piece, block_ref[...], LAST), column + size
+    total_ref[...] = total
+
+
+def product(rows, blocks):
+    return pl.pallas_call(
+        product_kernel,
+        out_shape=jax.ShapeDtypeStruct((rows.shape[0], blocks[0].shape[0]), F32),
+        in_specs=[VMEM] * (1 + len(blocks)),
+        out_specs=VMEM,
+        compiler_params=PARAMS,
+        cost_estimate=pl.CostEstimate(flops=1000, bytes_accessed=1000, transcendentals=0),
+    )(rows, *blocks)
+
+
+def scaled_kernel(hidden_ref, scale_ref, *refs):
+    block_refs, first_ref, second_ref = refs[:-2], refs[-2], refs[-1]
+    half, column = first_ref.shape[0], 0
+    for block_ref in block_refs:
+        end = column + block_ref.shape[1]
+        result = (scale_ref[...] * dot(hidden_ref[...], block_ref[...])).astype(BF16)
+        first_ref[:, column:end] = result[:half]
+        second_ref[:, column:end] = result[half:]
+        column = end
+
+
+def scaled_product(hidden, scale, blocks):
+    count, depth = hidden.shape
+    width = sum(block.shape[1] for block in blocks)
+    half = jax.ShapeDtypeStruct((count // 2, width), BF16)
+    return pl.pallas_call(
+        scaled_kernel,
+        out_shape=(half, half),
+        in_specs=[VMEM] * (2 + len(blocks)),
+        out_specs=(VMEM, VMEM),
+        compiler_params=PARAMS,
+        cost_estimate=pl.CostEstimate(
+            flops=2 * count * depth * width,
+            bytes_accessed=2 * (count + depth) * width,
+            transcendentals=0,
+        ),
+    )(hidden, scale, *blocks)
+
+
 def roll_columns(x, start):
     return lax.dynamic_slice_in_dim(jnp.concatenate([x, x], axis=1), start, x.shape[1], axis=1)
 
@@ -137,11 +193,10 @@
     prob1 = about[:, 3:4] + about[:, 5:6] + about[:, 7:8]
     prob = jnp.where(first, prob0, prob1)
     token_rows = rows[:, :width]
-    cot_rows = (prob * rows[:, width : 2 * width].astype(F32)).astype(BF16)
-
-    def leave(part):
-        returned = lax.ppermute(part[half:], "c", [(0, 1), (1, 0)])
-        return (dot(back_own, part[:half]) + dot(back_other, returned)).astype(BF16)
+
+    def leave(here, there):
+        returned = lax.ppermute(there, "c", [(0, 1), (1, 0)])
+        return (dot(back_own, here) + dot(back_other, returned)).astype(BF16)
 
     gate_up = dot(token_rows, full_both)
     gate_pre, up_pre = gate_up[:, :ff], gate_up[:, ff:]
@@ -149,20 +204,20 @@
     activated = gate_pre * sigmoid_gate
     slope_gate = sigmoid_gate * (1.0 + gate_pre * (1.0 - sigmoid_gate))
     hidden = (activated * up_pre).astype(BF16)
-    out_part = jnp.concatenate([(prob * dot(hidden, down)).astype(BF16) for down in downs], axis=1)
-    out_tokens = leave(out_part)
+    cot_given, hidden = lax.optimization_barrier((rows[:, width : 2 * width], hidden))
+    cot_rows = (prob * cot_given.astype(F32)).astype(BF16)
+    out_here, out_there = scaled_product(hidden, prob, downs)
+    out_tokens = leave(out_here, out_there)
     out_y = scatter_sum_by_exchange(out_tokens, "y", y_size)
 
-    late_cot, _ = lax.optimization_barrier((cot_rows, out_part))
-    grad_hidden, column = 0.0, 0
-    for down in downs:
-        piece = late_cot[:, column : column + down.shape[1]]
-        grad_hidden, column = grad_hidden + dot(piece, down, LAST), column + down.shape[1]
+    late_cot, _ = lax.optimization_barrier((cot_rows, out_tokens))
+    grad_hidden = product(late_cot, downs)
     grad_up = (grad_hidden * activated).astype(BF16)
     grad_gate = (grad_hidden * up_pre * slope_gate).astype(BF16)
     grad_both = jnp.concatenate([grad_gate, grad_up], axis=1)
-    grad_both, late_hidden, _ = lax.optimization_barrier((grad_both, hidden, out_tokens))
-    grad_tokens = leave(dot(grad_both, full_both, LAST).astype(BF16))
+    late_hidden, _ = lax.optimization_barrier((hidden, out_tokens))
+    grad_part = dot(grad_both, full_both, LAST).astype(BF16)
+    grad_tokens = leave(grad_part[:half], grad_part[half:])
     partial_down = []
     for q in range(quarters):
         start = lax.rem(q - group + quarters, quarters) * quarter

time: 225 us -> 226 us (level)
  matrix products: 29 us -> 24 us
  other arithmetic: 11.3 us -> 14.1 us
  local copies, waits for them, and re-layouts: 11 us -> 13.3 us
    dot_general x22 -> x12, matrix products: 29 us -> 24 us  [dot(): return lax.dot_general(a, b, dims, preferred_element_type=F32)]
    all_to_all x1, waiting for transfers between devices: 4.79 us -> 9.04 us  [gather_by_exchange(): lax.all_to_all(spread, axes, split_axis=0, concat_axis=0, tiled=True)]
    ppermute x4, waiting for transfers between devices: 19.2 us -> 16.1 us  [pass_on(): return lax.ppermute(x, axis, [(i, (i + shift) % size) for i in range(size)])]
    unnamed x29 -> x41, local copies, waits for them, and re-layouts: 1.79 us -> 4.25 us
  transfers between devices with their start and end apart: 16 -> 16, of which waited for: 9 -> 9; matrix products, arithmetic and copies ran while one was open for 14% -> 16% of each run, Pallas kernels for 0% -> 0%
where the time goes in v6:
time: 226 us; the launch traced here: 225 us
  waiting for transfers between devices  55.6 us (25%)
  starting transfers between devices  50.5 us (22%)
  blocking collectives  50.5 us (22%)
  matrix products  24 us (11%)
  between operations  14.7 us (7%)
  other arithmetic  14.1 us (6%)
  local copies, waits for them, and re-layouts  13.3 us (6%)
    all_gather x1, blocking collectives, on_device(): by_z = lax.all_gather(packed[None], ('zh', 'zl'), axis=0, tiled=True)  37.4 us
    all_to_all x3, waiting for transfers between devices, scatter_sum_by_exchange(): parts = lax.all_to_all(parts, axes, split_axis=0, concat_axis=0, tiled=True)  24.3 us
    dot_general x12, matrix products, dot(): return lax.dot_general(a, b, dims, preferred_element_type=F32)  24 us
    ppermute x4, starting transfers between devices, pass_on(): return lax.ppermute(x, axis, [(i, (i + shift) % size) for i in range(size)])  16.7 us
    ppermute x4, waiting for transfers between devices, pass_on(): return lax.ppermute(x, axis, [(i, (i + shift) % size) for i in range(size)])  16.1 us
    all_to_all x3, starting transfers between devices, scatter_sum_by_exchange(): parts = lax.all_to_all(parts, axes, split_axis=0, concat_axis=0, tiled=True)  14.5 us
    all_to_all x1, blocking collectives, scatter_sum_by_exchange(): parts = lax.all_to_all(parts, axes, split_axis=0, concat_axis=0, tiled=True)  13.1 us
    all_to_all x1, waiting for transfers between devices, gather_by_exchange(): lax.all_to_all(spread, axes, split_axis=0, concat_axis=0, tiled=True)  9.04 us
  transfers between devices with their start and end apart: 16, of which 9 were waited for; matrix products, arithmetic and copies ran while one was open for 16% of the time, Pallas kernels for 0%

profile of v6, /device:TPU:6, one launch (start us, length us, event | category | flops | bytes accessed | tf_op | source)
XLA Modules:
  0.0 224.8 jit_solution(11997477902655167830)
XLA Ops:
  7.3 2.8 %pad_maximum_fusion.1 = bf16[768,1024]{1,0:T(8,128)(2,1)} fusion(bf16[768,512]{1,0:T(8,128)(2,1)} %bitcast.45, bf16[768,512]{1,0:T(8,128)(2,1)} %bitcast.46), kind=kLoop, calls=%fused_computation.16 | loop fusion | flops 3145728 | bytes 3145728 | tf_op jit(solution)/shard_map/concatenate | solution.py:149
  10.1 2.7 %collective-permute-start = (bf16[512,768]{1,0:T(8,128)(2,1)S(1)}, bf16[512,768]{1,0:T(8,128)(2,1)S(1)}, u32[]{:S(2)}, u32[]{:S(2)}) collective-permute-start(bf16[512,768]{1,0:T(8,128)(2,1)S(1)} %bitcast.38), channel_id=1, source_target_pairs={{0,384},{128,0},{256,128},{384,256},{1,385},{129,1},{257,129},{385... | collective-permute-start | bytes 2359304 | tf_op jit(solution)/shard_map/ppermute | solution.py:77
  12.8 6.9 %collective-permute-start.1 = (bf16[512,768]{1,0:T(8,128)(2,1)S(1)}, bf16[512,768]{1,0:T(8,128)(2,1)S(1)}, u32[]{:S(2)}, u32[]{:S(2)}) collective-permute-start(bf16[512,768]{1,0:T(8,128)(2,1)S(1)} %bitcast.39), channel_id=1, source_target_pairs={{0,128},{128,256},{256,384},{384,0},{1,129},{129,257},{257,385},{3... | collective-permute-start | bytes 2359304 | tf_op jit(solution)/shard_map/ppermute | solution.py:77
  20.3 37.4 %all-gather.1 = bf16[16,4,6272]{2,1,0:T(4,128)(2,1)S(1)} all-gather(bf16[1,4,6272]{2,1,0:T(4,128)(2,1)S(1)} %fusion.45), channel_id=2, replica_groups=mesh['x'=4,'zl'=4,'c'=2,'zh'=4,'y'=4] {'zh','zl'}, dimensions={0}, use_global_device_ids=true | all-gather | bytes 852992 | tf_op jit(solution)/shard_map/all_gather | solution.py:158
  58.8 3.1 %broadcast_in_dim.16 = bf16[4,64,6272]{2,1,0:T(8,128)(2,1)} broadcast(bf16[64,6272]{1,0:T(8,128)(2,1)} %broadcast_in_dim.7), dimensions={1,2} | broadcast | bytes 4014080 | tf_op jit(solution)/shard_map/broadcast_in_dim | solution.py:45
  61.9 4.7 %all-to-all-start = ((bf16[4,64,6272]{2,1,0:T(8,128)(2,1)}), bf16[4,64,6272]{2,1,0:T(8,128)(2,1)}, u32[]{:S(2)}, u32[]{:S(2)}) async-start(bf16[4,64,6272]{2,1,0:T(8,128)(2,1)} %broadcast_in_dim.16), calls=%async_computation | async-start | bytes 6422528 | tf_op jit(solution)/shard_map/all_to_all | solution.py:46
  67.3 1.9 collective-permute-start.2
  70.0 5.1 %collective-permute-start.3 = (bf16[512,384]{1,0:T(8,128)(2,1)}, bf16[512,384]{1,0:T(8,128)(2,1)S(1)}, u32[]{:S(2)}, u32[]{:S(2)}) collective-permute-start(bf16[512,384]{1,0:T(8,128)(2,1)} %slice.74), channel_id=1, source_target_pairs={{0,128},{128,256},{256,384},{384,0},{1,129},{129,257},{257,385},{3... | collective-permute-start | bytes 1179656 | tf_op jit(solution)/shard_map/ppermute | solution.py:77
  75.2 13.8 %collective-permute-done.2.refs_2_.refs_3_ = bf16[512,384]{1,0:T(8,128)(2,1)S(1)} collective-permute-done((bf16[512,384]{1,0:T(8,128)(2,1)}, bf16[512,384]{1,0:T(8,128)(2,1)S(1)}, u32[]{:S(2)}, u32[]{:S(2)}) %collective-permute-start.2) | collective-permute-done | bytes 393248 | tf_op jit(solution)/shard_map/ppermute | solution.py:77
  89.0 2.3 %collective-permute-done.3.refs_3_.refs_4_ = bf16[512,384]{1,0:T(8,128)(2,1)S(1)} collective-permute-done((bf16[512,384]{1,0:T(8,128)(2,1)}, bf16[512,384]{1,0:T(8,128)(2,1)S(1)}, u32[]{:S(2)}, u32[]{:S(2)}) %collective-permute-start.3) | collective-permute-done | bytes 393248 | tf_op jit(solution)/shard_map/ppermute | solution.py:77
  91.3 9.0 %all-to-all-done = bf16[4,64,6272]{2,1,0:T(8,128)(2,1)} async-done(((bf16[4,64,6272]{2,1,0:T(8,128)(2,1)}), bf16[4,64,6272]{2,1,0:T(8,128)(2,1)}, u32[]{:S(2)}, u32[]{:S(2)}) %all-to-all-start) | async-done | bytes 3211296 | tf_op jit(solution)/shard_map/all_to_all | solution.py:46
  101.4 3.9 %convolution_convert_fusion = bf16[128,6272]{1,0:T(8,128)(2,1)} fusion(bf16[256,6272]{1,0:T(8,128)(2,1)} %bitcast.4, s32[128]{0:T(128)S(1)} %get-tuple-element.58, s32[128]{0:T(128)S(1)} %get-tuple-element.57, s32[256]{0:T(256)S(1)} %and_select_fusion, s32[256]{0:T(256)S(1)} %get-tuple-element.42, s32[256]{0:T(256)S(1)} %get-tuple-element.41), kind=kOutput, calls=%fused_computation | convolution fusion | flops 412008448 | bytes 4820992 | tf_op jit(solution)/shard_map/dot_general | solution.py:19
  105.3 1.9 collective-permute-start.4
  108.1 2.7 %convolution_convert_fusion.1 = bf16[128,6272]{1,0:T(8,128)(2,1)S(1)} fusion(bf16[256,6272]{1,0:T(8,128)(2,1)} %bitcast.4, s32[128]{0:T(128)S(1)} %get-tuple-element.57, s32[128]{0:T(128)S(1)} %fusion.54, s32[256]{0:T(256)S(1)} %and_select_fusion, s32[256]{0:T(256)S(1)} %get-tuple-element.42, s32[256]{0:T(256)S(1)} %get-tuple-element.41), kind=kOutput, calls=%fused_computation.1 | convolution fusion | flops 412008448 | bytes 4820992 | tf_op jit(solution)/shard_map/dot_general | solution.py:19
  112.7 2.6 %fusion.5 = bf16[256,3072]{1,0:T(8,128)(2,1)} fusion(bf16[128,6272]{1,0:T(8,128)(2,1)S(1)} %convolution_convert_fusion.1, bf16[128,6272]{1,0:T(8,128)(2,1)} %collective-permute-done.4), kind=kLoop, calls=%fused_computation.15 | loop fusion | flops 3145728 | bytes 4784128 | tf_op jit(solution)/shard_map/concatenate | solution.py:178
  115.3 5.1 %fusion.3 = f32[256,1024]{1,0:T(8,128)S(1)} fusion(bf16[3072,1024]{1,0:T(8,128)(2,1)} %all-gather.4.cloned.1.call-done, bf16[128,6272]{1,0:T(8,128)(2,1)} %copy-done.6, bf16[128,6272]{1,0:T(8,128)(2,1)} %collective-permute-done.4), kind=kOutput, calls=%fused_computation.14 | convolution fusion | flops 1613758464 | bytes 10551296 | tf_op jit(solution)/shard_map/dot_general | solution.py:19
  122.4 2.2 collective-permute-start.5
  126.6 1.9 fusion
  128.5 4.4 %all-to-all-start.1 = ((bf16[4,64,3072]{2,1,0:T(8,128)(2,1)}), bf16[4,64,3072]{2,1,0:T(8,128)(2,1)}, u32[]{:S(2)}, u32[]{:S(2)}) async-start(bf16[4,64,3072]{2,1,0:T(8,128)(2,1)} %bitcast.42), calls=%async_computation.1 | async-start | bytes 3145728 | tf_op jit(solution)/shard_map/all_to_all | solution.py:53
  137.6 4.6 %convolution_convert_fusion.2 = bf16[256,3072]{1,0:T(8,128)(2,1)S(1)} fusion(bf16[3072,1024]{1,0:T(8,128)(2,1)} %all-gather.4.cloned.1.call-done, bf16[256,512]{1,0:T(8,128)(2,1)S(1)} %get-tuple-element.46, bf16[256,512]{1,0:T(8,128)(2,1)S(1)} %get-tuple-element.45), kind=kOutput, calls=%fused_computation.6 | convolution fusion | flops 1612447744 | bytes 8388608 | tf_op jit(solution)/shard_map/dot_general | solution.py:19
  143.2 2.4 %collective-permute-start.6 = (bf16[128,3072]{1,0:T(8,128)(2,1)}, bf16[128,3072]{1,0:T(8,128)(2,1)}, u32[]{:S(2)}, u32[]{:S(2)}) collective-permute-start(bf16[128,3072]{1,0:T(8,128)(2,1)} %slice.114), channel_id=1, source_target_pairs={{0,16},{16,0},{1,17},{17,1},{2,18},{18,2},{3,19},{19,3},{4,20},{20... | collective-permute-start | bytes 2359304 | tf_op jit(solution)/shard_map/ppermute | solution.py:198
  147.2 1.8 pad_maximum_fusion
  149.7 3.0 %fusion.1 = bf16[256,3072]{1,0:T(8,128)(2,1)} fusion(f32[256,3072]{1,0:T(8,128)S(1)} %fusion.10, bf16[128,3072]{1,0:T(8,128)(2,1)} %collective-permute-done.6, s32[128]{0:T(128)S(1)} %copy-done.14, s32[128]{0:T(128)S(1)} %get-tuple-element.57, s32[256]{0:T(256)S(1)} %and_select_fusion.2, s32[256]{0:T(256)S(1)} %bitcast.55, s32[256]{0:T(256)S(1)} %bitcast.51), kind=kOutput, calls=%fused_computation.5 | convolution fusion | flops 203063296 | bytes 5509120 | tf_op jit(solution)/shard_map/dot_general | solution.py:19
  156.1 3.6 %all-to-all-start.2 = ((bf16[4,64,3072]{2,1,0:T(8,128)(2,1)}), bf16[4,64,3072]{2,1,0:T(8,128)(2,1)S(1)}, u32[]{:S(2)}, u32[]{:S(2)}) async-start(bf16[4,64,3072]{2,1,0:T(8,128)(2,1)} %bitcast.15), calls=%async_computation.2 | async-start | bytes 3145728 | tf_op jit(solution)/shard_map/all_to_all | solution.py:53
  159.8 1.9 collective-permute-start.9
  161.7 2.8 %collective-permute-start.8 = (bf16[16,3072]{1,0:T(8,128)(2,1)S(1)}, bf16[16,3072]{1,0:T(8,128)(2,1)S(1)}, u32[]{:S(2)}, u32[]{:S(2)}) collective-permute-start(bf16[16,3072]{1,0:T(8,128)(2,1)S(1)} %get-tuple-element.49), channel_id=1, source_target_pairs={{0,64},{32,96},{64,0},{96,32},{1,65},{33,97},{65,1},{97,33},{2,66}... | collective-permute-start | bytes 294920 | tf_op jit(solution)/shard_map/ppermute | solution.py:67
  164.5 3.3 %collective-permute-start.7 = (bf16[16,3072]{1,0:T(8,128)(2,1)S(1)}, bf16[16,3072]{1,0:T(8,128)(2,1)S(1)}, u32[]{:S(2)}, u32[]{:S(2)}) collective-permute-start(bf16[16,3072]{1,0:T(8,128)(2,1)S(1)} %get-tuple-element.47), channel_id=1, source_target_pairs={{0,32},{32,64},{64,96},{96,0},{1,33},{33,65},{65,97},{97,1},{2,34}... | collective-permute-start | bytes 294920 | tf_op jit(solution)/shard_map/ppermute | solution.py:67
  167.8 5.2 %collective-permute-done.8 = bf16[16,3072]{1,0:T(8,128)(2,1)S(1)} collective-permute-done((bf16[16,3072]{1,0:T(8,128)(2,1)S(1)}, bf16[16,3072]{1,0:T(8,128)(2,1)S(1)}, u32[]{:S(2)}, u32[]{:S(2)}) %collective-permute-start.8) | collective-permute-done | bytes 98336 | tf_op jit(solution)/shard_map/ppermute | solution.py:67
  173.1 7.3 %all-to-all-done.2 = bf16[4,64,3072]{2,1,0:T(8,128)(2,1)S(1)} async-done(((bf16[4,64,3072]{2,1,0:T(8,128)(2,1)}), bf16[4,64,3072]{2,1,0:T(8,128)(2,1)S(1)}, u32[]{:S(2)}, u32[]{:S(2)}) %all-to-all-start.2) | async-done | bytes 1572896 | tf_op jit(solution)/shard_map/all_to_all | solution.py:53
  180.7 13.1 %all_to_all.25 = bf16[4,16,3072]{2,1,0:T(8,128)(2,1)S(1)} all-to-all(bf16[4,16,3072]{2,1,0:T(8,128)(2,1)S(1)} %bitcast.44), channel_id=1, replica_groups=mesh['x'=4,'zl'=4,'c'=2,'zh'=4,'y'=4] {'zl'}, dimensions={0} | all-to-all | bytes 786432 | tf_op jit(solution)/shard_map/all_to_all | solution.py:53
  194.6 6.6 %all-to-all-start.4 = ((bf16[4,4,6144]{2,1,0:T(4,128)(2,1)}), bf16[4,4,6144]{2,1,0:T(4,128)(2,1)S(1)}, u32[]{:S(2)}, u32[]{:S(2)}) async-start(bf16[4,4,6144]{2,1,0:T(4,128)(2,1)} %reshape.280), calls=%async_computation.4 | async-start | bytes 393216 | tf_op jit(solution)/shard_map/all_to_all | solution.py:53
  201.2 15.3 %all-to-all-done.4 = bf16[4,4,6144]{2,1,0:T(4,128)(2,1)S(1)} async-done(((bf16[4,4,6144]{2,1,0:T(4,128)(2,1)}), bf16[4,4,6144]{2,1,0:T(4,128)(2,1)S(1)}, u32[]{:S(2)}, u32[]{:S(2)}) %all-to-all-start.4) | async-done | bytes 196640 | tf_op jit(solution)/shard_map/all_to_all | solution.py:53
  (100 shorter events, 25.0 us)
Async XLA Ops:
  7.2 2.9 %copy-start = (bf16[1,512,768]{2,1,0:T(8,128)(2,1)S(1)}, bf16[1,512,768]{2,1,0:T(8,128)(2,1)}, u32[]{:S(2)}) copy-start(bf16[1,512,768]{2,1,0:T(8,128)(2,1)} %param.12) | copy-start | bytes 2359300
  7.2 12.6 %copy-start.12 = (s32[4,2]{0,1:T(2,128)S(1)}, s32[4,2]{0,1:T(2,128)}, u32[]{:S(2)}) copy-start(s32[4,2]{0,1:T(2,128)} %param.8) | copy-start | bytes 100
  7.2 12.8 %copy-start.19 = (f32[4,2]{0,1:T(2,128)S(1)}, f32[4,2]{0,1:T(2,128)}, u32[]{:S(2)}) copy-start(f32[4,2]{0,1:T(2,128)} %param.9) | copy-start | bytes 100
  7.2 13.0 %copy-start.10 = (bf16[4,3072]{1,0:T(4,128)(2,1)S(1)}, bf16[4,3072]{1,0:T(4,128)(2,1)}, u32[]{:S(2)}) copy-start(bf16[4,3072]{1,0:T(4,128)(2,1)} %param.13) | copy-start | bytes 73732
  7.2 13.1 %copy-start.11 = (bf16[4,3072]{1,0:T(4,128)(2,1)S(1)}, bf16[4,3072]{1,0:T(4,128)(2,1)}, u32[]{:S(2)}) copy-start(bf16[4,3072]{1,0:T(4,128)(2,1)} %param.7) | copy-start | bytes 73732
  7.2 108.0 %all-gather.4.cloned.1.call-start = ((), (), s32[]{:S(2)}) async-start(), calls=%async_computation.6 | async-start | bytes 7864320 | tf_op jit(solution)/shard_map/all_gather | solution.py:152
  10.1 47.6 %collective-permute-start = (bf16[512,768]{1,0:T(8,128)(2,1)S(1)}, bf16[512,768]{1,0:T(8,128)(2,1)S(1)}, u32[]{:S(2)}, u32[]{:S(2)}) collective-permute-start(bf16[512,768]{1,0:T(8,128)(2,1)S(1)} %bitcast.38), channel_id=1, source_target_pairs={{0,384},{128,0},{256,128},{384,256},{1,385},{129,1},{257,129},{385... | collective-permute-start | bytes 2359304 | tf_op jit(solution)/shard_map/ppermute | solution.py:77
  12.8 44.9 %collective-permute-start.1 = (bf16[512,768]{1,0:T(8,128)(2,1)S(1)}, bf16[512,768]{1,0:T(8,128)(2,1)S(1)}, u32[]{:S(2)}, u32[]{:S(2)}) collective-permute-start(bf16[512,768]{1,0:T(8,128)(2,1)S(1)} %bitcast.39), channel_id=1, source_target_pairs={{0,128},{128,256},{256,384},{384,0},{1,129},{129,257},{257,385},{3... | collective-permute-start | bytes 2359304 | tf_op jit(solution)/shard_map/ppermute | solution.py:77
  61.9 38.5 %all-to-all-start = ((bf16[4,64,6272]{2,1,0:T(8,128)(2,1)}), bf16[4,64,6272]{2,1,0:T(8,128)(2,1)}, u32[]{:S(2)}, u32[]{:S(2)}) async-start(bf16[4,64,6272]{2,1,0:T(8,128)(2,1)} %broadcast_in_dim.16), calls=%async_computation | async-start | bytes 6422528 | tf_op jit(solution)/shard_map/all_to_all | solution.py:46
  67.3 21.7 %collective-permute-start.2 = (bf16[512,384]{1,0:T(8,128)(2,1)}, bf16[512,384]{1,0:T(8,128)(2,1)S(1)}, u32[]{:S(2)}, u32[]{:S(2)}) collective-permute-start(bf16[512,384]{1,0:T(8,128)(2,1)} %slice.73), channel_id=1, source_target_pairs={{0,384},{128,0},{256,128},{384,256},{1,385},{129,1},{257,129},{385... | collective-permute-start | bytes 1179656 | tf_op jit(solution)/shard_map/ppermute | solution.py:77
  70.0 21.2 %collective-permute-start.3 = (bf16[512,384]{1,0:T(8,128)(2,1)}, bf16[512,384]{1,0:T(8,128)(2,1)S(1)}, u32[]{:S(2)}, u32[]{:S(2)}) collective-permute-start(bf16[512,384]{1,0:T(8,128)(2,1)} %slice.74), channel_id=1, source_target_pairs={{0,128},{128,256},{256,384},{384,0},{1,129},{129,257},{257,385},{3... | collective-permute-start | bytes 1179656 | tf_op jit(solution)/shard_map/ppermute | solution.py:77
  75.2 32.7 %copy-start.13 = (s32[128]{0:T(128)}, s32[128]{0:T(128)S(1)}, u32[]{:S(2)}) copy-start(s32[128]{0:T(128)S(1)} %get-tuple-element.58) | copy-start | bytes 1540
  89.0 32.3 %copy-start.2 = (bf16[512,384]{1,0:T(8,128)(2,1)}, bf16[512,384]{1,0:T(8,128)(2,1)S(1)}, u32[]{:S(2)}) copy-start(bf16[512,384]{1,0:T(8,128)(2,1)S(1)} %collective-permute-done.2.refs_2_.refs_3_) | copy-start | bytes 1179652
  91.3 30.1 %copy-start.4 = (bf16[512,384]{1,0:T(8,128)(2,1)}, bf16[512,384]{1,0:T(8,128)(2,1)S(1)}, u32[]{:S(2)}) copy-start(bf16[512,384]{1,0:T(8,128)(2,1)S(1)} %collective-permute-done.3.refs_3_.refs_4_) | copy-start | bytes 1179652
  105.3 5.7 %collective-permute-start.4 = (bf16[128,6272]{1,0:T(8,128)(2,1)}, bf16[128,6272]{1,0:T(8,128)(2,1)}, u32[]{:S(2)}, u32[]{:S(2)}) collective-permute-start(bf16[128,6272]{1,0:T(8,128)(2,1)} %convolution_convert_fusion), channel_id=1, source_target_pairs={{0,16},{16,0},{1,17},{17,1},{2,18},{18,2},{3,19},{19,3},{4,20},{20... | collective-permute-start | bytes 4816904 | tf_op jit(solution)/shard_map/ppermute | solution.py:177
  107.4 4.4 %copy-start.15 = (s32[128]{0:T(128)}, s32[128]{0:T(128)S(1)}, u32[]{:S(2)}) copy-start(s32[128]{0:T(128)S(1)} %fusion.54) | copy-start | bytes 1540
  110.8 1.9 copy-start.6
  120.3 4.3 %copy-start.16 = (s32[128]{0:T(128)S(1)}, s32[128]{0:T(128)}, u32[]{:S(2)}) copy-start(s32[128]{0:T(128)} %copy-done.15) | copy-start | bytes 1540
  121.3 4.0 %copy-start.7 = (bf16[256,3072]{1,0:T(8,128)(2,1)S(1)}, bf16[256,3072]{1,0:T(8,128)(2,1)}, u32[]{:S(2)}) copy-start(bf16[256,3072]{1,0:T(8,128)(2,1)} %fusion.5) | copy-start | bytes 4718596
  121.3 4.0 %copy-start.18 = (f32[256]{0:T(256)S(1)}, f32[256]{0:T(256)}, u32[]{:S(2)}) copy-start(f32[256]{0:T(256)} %get-tuple-element.43) | copy-start | bytes 3076
  122.4 4.2 %collective-permute-start.5 = (bf16[128,3072]{1,0:T(8,128)(2,1)S(1)}, bf16[128,3072]{1,0:T(8,128)(2,1)S(1)}, u32[]{:S(2)}, u32[]{:S(2)}) collective-permute-start(bf16[128,3072]{1,0:T(8,128)(2,1)S(1)} %get-tuple-element.32), channel_id=1, source_target_pairs={{0,16},{16,0},{1,17},{17,1},{2,18},{18,2},{3,19},{19,3},{4,20},{20... | collective-permute-start | bytes 2359304 | tf_op jit(solution)/shard_map/ppermute | solution.py:198
  124.7 1.9 copy-start.14
  128.5 25.9 %all-to-all-start.1 = ((bf16[4,64,3072]{2,1,0:T(8,128)(2,1)}), bf16[4,64,3072]{2,1,0:T(8,128)(2,1)}, u32[]{:S(2)}, u32[]{:S(2)}) async-start(bf16[4,64,3072]{2,1,0:T(8,128)(2,1)} %bitcast.42), calls=%async_computation.1 | async-start | bytes 3145728 | tf_op jit(solution)/shard_map/all_to_all | solution.py:53
  132.9 85.1 %reduce-scatter.2.cloned.1.call-start = ((), (), s32[]{:S(2)}) async-start(), calls=%async_computation.7 | async-start | bytes 3932160 | tf_op jit(solution)/shard_map/reduce_scatter | solution.py:228
  136.1 1.2 copy-start.9
  143.2 6.6 %collective-permute-start.6 = (bf16[128,3072]{1,0:T(8,128)(2,1)}, bf16[128,3072]{1,0:T(8,128)(2,1)}, u32[]{:S(2)}, u32[]{:S(2)}) collective-permute-start(bf16[128,3072]{1,0:T(8,128)(2,1)} %slice.114), channel_id=1, source_target_pairs={{0,16},{16,0},{1,17},{17,1},{2,18},{18,2},{3,19},{19,3},{4,20},{20... | collective-permute-start | bytes 2359304 | tf_op jit(solution)/shard_map/ppermute | solution.py:198
  147.2 1.8 copy-start.17
  156.1 24.2 %all-to-all-start.2 = ((bf16[4,64,3072]{2,1,0:T(8,128)(2,1)}), bf16[4,64,3072]{2,1,0:T(8,128)(2,1)S(1)}, u32[]{:S(2)}, u32[]{:S(2)}) async-start(bf16[4,64,3072]{2,1,0:T(8,128)(2,1)} %bitcast.15), calls=%async_computation.2 | async-start | bytes 3145728 | tf_op jit(solution)/shard_map/all_to_all | solution.py:53
  159.8 8.0 %collective-permute-start.9 = (bf16[16,3072]{1,0:T(8,128)(2,1)S(1)}, bf16[16,3072]{1,0:T(8,128)(2,1)S(1)}, u32[]{:S(2)}, u32[]{:S(2)}) collective-permute-start(bf16[16,3072]{1,0:T(8,128)(2,1)S(1)} %get-tuple-element.48), channel_id=1, source_target_pairs={{0,96},{32,0},{64,32},{96,64},{1,97},{33,1},{65,33},{97,65},{2,98}... | collective-permute-start | bytes 294920 | tf_op jit(solution)/shard_map/ppermute | solution.py:67
  161.7 11.3 %collective-permute-start.8 = (bf16[16,3072]{1,0:T(8,128)(2,1)S(1)}, bf16[16,3072]{1,0:T(8,128)(2,1)S(1)}, u32[]{:S(2)}, u32[]{:S(2)}) collective-permute-start(bf16[16,3072]{1,0:T(8,128)(2,1)S(1)} %get-tuple-element.49), channel_id=1, source_target_pairs={{0,64},{32,96},{64,0},{96,32},{1,65},{33,97},{65,1},{97,33},{2,66}... | collective-permute-start | bytes 294920 | tf_op jit(solution)/shard_map/ppermute | solution.py:67
  164.5 8.5 %collective-permute-start.7 = (bf16[16,3072]{1,0:T(8,128)(2,1)S(1)}, bf16[16,3072]{1,0:T(8,128)(2,1)S(1)}, u32[]{:S(2)}, u32[]{:S(2)}) collective-permute-start(bf16[16,3072]{1,0:T(8,128)(2,1)S(1)} %get-tuple-element.47), channel_id=1, source_target_pairs={{0,32},{32,64},{64,96},{96,0},{1,33},{33,65},{65,97},{97,1},{2,34}... | collective-permute-start | bytes 294920 | tf_op jit(solution)/shard_map/ppermute | solution.py:67
  194.6 21.9 %all-to-all-start.4 = ((bf16[4,4,6144]{2,1,0:T(4,128)(2,1)}), bf16[4,4,6144]{2,1,0:T(4,128)(2,1)S(1)}, u32[]{:S(2)}, u32[]{:S(2)}) async-start(bf16[4,4,6144]{2,1,0:T(4,128)(2,1)} %reshape.280), calls=%async_computation.4 | async-start | bytes 393216 | tf_op jit(solution)/shard_map/all_to_all | solution.py:53
  (4 other events, 4.1 us)
Sparse Core Ops, SparseCore 0:
  10.2 84.6 all-gather.3
  156.2 38.0 reduce-scatter.1

commit v7 on v4

--- a/solution.py
+++ b/solution.py
@@ -105,10 +105,10 @@
     if quarters == 4:
         cut = quarter // 2
         across = pass_on(from_next[:, :cut], "x", -1), pass_on(from_last[:, cut:], "x", 1)
-        plane, across = lax.optimization_barrier((plane, across))
-        downs = [own_down, from_next, *across, from_last]
+        full_down = jnp.concatenate([own_down, from_next, *across, from_last], axis=1)
     else:
-        downs = [own_down, from_next]
+        full_down = jnp.concatenate([own_down, from_next], axis=1)
+    plane, full_down = lax.optimization_barrier((plane, full_down))
 
     count = plane.shape[0]
     code = plane[:, 2 * width : 2 * width + 2].astype(jnp.int32)
@@ -127,8 +127,8 @@
 
     code_back = low_first(code)
     place_back = low_first(place)
-    back_own = slot_table(code_back, place_back, expert, block)
-    back_other = slot_table(code_back, place_back, other, block)
+    back = [slot_table(code_back, place_back, which, block) for which in (expert, other)]
+    back = lax.optimization_barrier(jnp.concatenate(back, axis=1))
 
     about = rows[:, 2 * width :].astype(F32)
     slot = lax.broadcasted_iota(jnp.int32, (2 * half, 1), 0)
@@ -137,11 +137,12 @@
     prob1 = about[:, 3:4] + about[:, 5:6] + about[:, 7:8]
     prob = jnp.where(first, prob0, prob1)
     token_rows = rows[:, :width]
-    cot_rows = (prob * rows[:, width : 2 * width].astype(F32)).astype(BF16)
-
-    def leave(part):
-        returned = lax.ppermute(part[half:], "c", [(0, 1), (1, 0)])
-        return (dot(back_own, part[:half]) + dot(back_other, returned)).astype(BF16)
+
+    def swap_back(part):
+        return jnp.concatenate([part[:half], lax.ppermute(part[half:], "c", [(0, 1), (1, 0)])])
+
+    def by_token(rows_back):
+        return dot(back, rows_back).astype(BF16)
 
     gate_up = dot(token_rows, full_both)
     gate_pre, up_pre = gate_up[:, :ff], gate_up[:, ff:]
@@ -149,27 +150,28 @@
     activated = gate_pre * sigmoid_gate
     slope_gate = sigmoid_gate * (1.0 + gate_pre * (1.0 - sigmoid_gate))
     hidden = (activated * up_pre).astype(BF16)
-    out_part = jnp.concatenate([(prob * dot(hidden, down)).astype(BF16) for down in downs], axis=1)
-    out_tokens = leave(out_part)
+    late_prob, hidden = lax.optimization_barrier((prob, hidden))
+    cot_rows = (late_prob * rows[:, width : 2 * width].astype(F32)).astype(BF16)
+    out_part = (prob * dot(hidden, full_down)).astype(BF16)
+    out_tokens = by_token(swap_back(out_part))
     out_y = scatter_sum_by_exchange(out_tokens, "y", y_size)
 
-    late_cot, _ = lax.optimization_barrier((cot_rows, out_part))
-    grad_hidden, column = 0.0, 0
-    for down in downs:
-        piece = late_cot[:, column : column + down.shape[1]]
-        grad_hidden, column = grad_hidden + dot(piece, down, LAST), column + down.shape[1]
+    late_cot, _ = lax.optimization_barrier((cot_rows, out_tokens))
+    grad_hidden = dot(late_cot, full_down, LAST)
     grad_up = (grad_hidden * activated).astype(BF16)
     grad_gate = (grad_hidden * up_pre * slope_gate).astype(BF16)
     grad_both = jnp.concatenate([grad_gate, grad_up], axis=1)
-    grad_both, late_hidden, _ = lax.optimization_barrier((grad_both, hidden, out_tokens))
-    grad_tokens = leave(dot(grad_both, full_both, LAST).astype(BF16))
+    late_hidden, _ = lax.optimization_barrier((hidden, out_part))
+    grad_both, _ = lax.optimization_barrier((grad_both, out_tokens))
+    grad_part = dot(grad_both, full_both, LAST).astype(BF16)
+    grad_tokens = by_token(swap_back(grad_part))
+    out_y, grad_tokens = lax.optimization_barrier((out_y, grad_tokens))
     partial_down = []
     for q in range(quarters):
         start = lax.rem(q - group + quarters, quarters) * quarter
-        block_q = lax.dynamic_slice_in_dim(late_cot, start, quarter, axis=1)
+        block_q = lax.dynamic_slice_in_dim(cot_rows, start, quarter, axis=1)
         partial_down.append(dot(late_hidden, block_q, FIRST).astype(BF16))
     partial_down = jnp.stack(partial_down)
-    out_y, grad_tokens, partial_down = lax.optimization_barrier((out_y, grad_tokens, partial_down))
     down_grads = lax.psum_scatter(partial_down, "x", scatter_dimension=0)[None]
 
     grad_y = scatter_sum_by_exchange(grad_tokens, "y", y_size)

time: 225 us -> 224 us (level)
  local copies, waits for them, and re-layouts: 11 us -> 20 us
  waiting for transfers between devices: 57.2 us -> 53 us
  matrix products: 29 us -> 25.1 us
    ppermute x4, waiting for transfers between devices: 19.2 us -> 9.62 us  [pass_on(): return lax.ppermute(x, axis, [(i, (i + shift) % size) for i in range(size)])]
    unnamed x29 -> x27, local copies, waits for them, and re-layouts: 1.79 us -> 9.07 us
    all_to_all x3, waiting for transfers between devices: 25.6 us -> 30 us  [scatter_sum_by_exchange(): parts = lax.all_to_all(parts, axes, split_axis=0, concat_axis=0, tiled=True)]
    dot_general x22 -> x12, matrix products: 29 us -> 25.1 us  [dot(): return lax.dot_general(a, b, dims, preferred_element_type=F32)]
  transfers between devices with their start and end apart: 16 -> 16, of which waited for: 9 -> 10; matrix products, arithmetic and copies ran while one was open for 14% -> 19% of each run, Pallas kernels for 0% -> 0%
where the time goes in v7:
time: 224 us; the launch traced here: 223 us
  waiting for transfers between devices  53 us (24%)
  blocking collectives  50.1 us (22%)
  starting transfers between devices  49.4 us (22%)
  matrix products  25.1 us (11%)
  local copies, waits for them, and re-layouts  20 us (9%)
  between operations  14.6 us (7%)
  other arithmetic  10.7 us (5%)
    all_gather x1, blocking collectives, on_device(): by_z = lax.all_gather(packed[None], ('zh', 'zl'), axis=0, tiled=True)  37.4 us
    all_to_all x3, waiting for transfers between devices, scatter_sum_by_exchange(): parts = lax.all_to_all(parts, axes, split_axis=0, concat_axis=0, tiled=True)  30 us
    dot_general x12, matrix products, dot(): return lax.dot_general(a, b, dims, preferred_element_type=F32)  25.1 us
    ppermute x4, starting transfers between devices, pass_on(): return lax.ppermute(x, axis, [(i, (i + shift) % size) for i in range(size)])  16.7 us
    all_to_all x3, starting transfers between devices, scatter_sum_by_exchange(): parts = lax.all_to_all(parts, axes, split_axis=0, concat_axis=0, tiled=True)  13.9 us
    all_to_all x1, blocking collectives, scatter_sum_by_exchange(): parts = lax.all_to_all(parts, axes, split_axis=0, concat_axis=0, tiled=True)  12.8 us
    ppermute x4, waiting for transfers between devices, pass_on(): return lax.ppermute(x, axis, [(i, (i + shift) % size) for i in range(size)])  9.62 us
    unnamed x27, local copies, waits for them, and re-layouts  9.07 us
  transfers between devices with their start and end apart: 16, of which 10 were waited for; matrix products, arithmetic and copies ran while one was open for 19% of the time, Pallas kernels for 0%

profile of v7, /device:TPU:6, one launch (start us, length us, event | category | flops | bytes accessed | tf_op | source)
XLA Modules:
  0.0 222.8 jit_solution(2435803634832235815)
XLA Ops:
  7.3 2.8 %pad_maximum_fusion.2 = bf16[768,1024]{1,0:T(8,128)(2,1)} fusion(bf16[768,512]{1,0:T(8,128)(2,1)} %bitcast.52, bf16[768,512]{1,0:T(8,128)(2,1)} %bitcast.53), kind=kLoop, calls=%fused_computation.14 | loop fusion | flops 3145728 | bytes 3145728 | tf_op jit(solution)/shard_map/concatenate | solution.py:93
  10.1 2.7 %collective-permute-start = (bf16[512,768]{1,0:T(8,128)(2,1)S(1)}, bf16[512,768]{1,0:T(8,128)(2,1)S(1)}, u32[]{:S(2)}, u32[]{:S(2)}) collective-permute-start(bf16[512,768]{1,0:T(8,128)(2,1)S(1)} %bitcast.50), channel_id=1, source_target_pairs={{0,384},{128,0},{256,128},{384,256},{1,385},{129,1},{257,129},{385... | collective-permute-start | bytes 2359304 | tf_op jit(solution)/shard_map/ppermute | solution.py:75
  12.8 6.9 %collective-permute-start.1 = (bf16[512,768]{1,0:T(8,128)(2,1)S(1)}, bf16[512,768]{1,0:T(8,128)(2,1)}, u32[]{:S(2)}, u32[]{:S(2)}) collective-permute-start(bf16[512,768]{1,0:T(8,128)(2,1)S(1)} %bitcast.51), channel_id=1, source_target_pairs={{0,128},{128,256},{256,384},{384,0},{1,129},{129,257},{257,385},{3... | collective-permute-start | bytes 2359304 | tf_op jit(solution)/shard_map/ppermute | solution.py:75
  20.4 37.4 %all-gather.1 = bf16[16,4,6272]{2,1,0:T(4,128)(2,1)S(1)} all-gather(bf16[1,4,6272]{2,1,0:T(4,128)(2,1)S(1)} %fusion.44), channel_id=2, replica_groups=mesh['x'=4,'zl'=4,'c'=2,'zh'=4,'y'=4] {'zh','zl'}, dimensions={0}, use_global_device_ids=true | all-gather | bytes 852992 | tf_op jit(solution)/shard_map/all_gather | solution.py:102
  58.8 2.0 broadcast_in_dim.16
  60.7 4.5 %all-to-all-start = ((bf16[4,64,6272]{2,1,0:T(8,128)(2,1)}), bf16[4,64,6272]{2,1,0:T(8,128)(2,1)S(1)}, u32[]{:S(2)}, u32[]{:S(2)}) async-start(bf16[4,64,6272]{2,1,0:T(8,128)(2,1)} %broadcast_in_dim.16), calls=%async_computation | async-start | bytes 6422528 | tf_op jit(solution)/shard_map/all_to_all | solution.py:44
  70.0 5.1 %collective-permute-start.3 = (bf16[512,384]{1,0:T(8,128)(2,1)S(1)}, bf16[512,384]{1,0:T(8,128)(2,1)S(1)}, u32[]{:S(2)}, u32[]{:S(2)}) collective-permute-start(bf16[512,384]{1,0:T(8,128)(2,1)S(1)} %slice.80), channel_id=1, source_target_pairs={{0,128},{128,256},{256,384},{384,0},{1,129},{129,257},{257,385},{3... | collective-permute-start | bytes 1179656 | tf_op jit(solution)/shard_map/ppermute | solution.py:75
  75.1 2.1 constant_dynamic-update-slice_fusion.4
  77.3 2.1 constant_dynamic-update-slice_fusion.3
  79.4 9.4 %collective-permute-done.2 = bf16[512,384]{1,0:T(8,128)(2,1)} collective-permute-done((bf16[512,384]{1,0:T(8,128)(2,1)}, bf16[512,384]{1,0:T(8,128)(2,1)}, u32[]{:S(2)}, u32[]{:S(2)}) %collective-permute-start.2) | collective-permute-done | bytes 393248 | tf_op jit(solution)/shard_map/ppermute | solution.py:75
  91.7 2.2 constant_dynamic-update-slice_fusion
  93.9 4.8 %all-to-all-done = bf16[4,64,6272]{2,1,0:T(8,128)(2,1)S(1)} async-done(((bf16[4,64,6272]{2,1,0:T(8,128)(2,1)}), bf16[4,64,6272]{2,1,0:T(8,128)(2,1)S(1)}, u32[]{:S(2)}, u32[]{:S(2)}) %all-to-all-start) | async-done | bytes 3211296 | tf_op jit(solution)/shard_map/all_to_all | solution.py:44
  98.9 2.0 convolution_convert_fusion
  107.7 5.1 %fusion.1 = f32[256,1024]{1,0:T(8,128)S(1)} fusion(bf16[3072,1024]{1,0:T(8,128)(2,1)} %all-gather.4.cloned.1.call-done, bf16[128,6272]{1,0:T(8,128)(2,1)} %collective-permute-done.4, bf16[128,6272]{1,0:T(8,128)(2,1)} %copy-done), kind=kOutput, calls=%fused_computation.10 | convolution fusion | flops 1613758464 | bytes 10551296 | tf_op jit(solution)/shard_map/dot_general | solution.py:17
  113.0 3.1 %fusion = bf16[256,3072]{1,0:T(8,128)(2,1)S(1)} fusion(bf16[256,512]{1,0:T(8,128)(2,1)S(1)} %multiply_convert_fusion.3, bf16[512,3072]{1,0:T(8,128)(2,1)} %constant_dynamic-update-slice_fusion, f32[256]{0:T(256)S(1)} %get-tuple-element.37), kind=kOutput, calls=%fused_computation.4 | convolution fusion | flops 806879232 | bytes 4981760 | tf_op jit(solution)/shard_map/dot_general | solution.py:17
  117.4 2.4 %collective-permute-start.5 = (bf16[128,3072]{1,0:T(8,128)(2,1)}, bf16[128,3072]{1,0:T(8,128)(2,1)}, u32[]{:S(2)}, u32[]{:S(2)}) collective-permute-start(bf16[128,3072]{1,0:T(8,128)(2,1)} %get-tuple-element.44), channel_id=1, source_target_pairs={{0,16},{16,0},{1,17},{17,1},{2,18},{18,2},{3,19},{19,3},{4,20},{20... | collective-permute-start | bytes 2359304 | tf_op jit(solution)/shard_map/ppermute | solution.py:142
  126.2 2.9 %convolution_convert_fusion.4 = bf16[256,3072]{1,0:T(8,128)(2,1)} fusion(bf16[256,256]{1,0:T(8,128)(2,1)S(1)} %copy-done.6, bf16[128,3072]{1,0:T(8,128)(2,1)} %collective-permute-done.5, bf16[128,3072]{1,0:T(8,128)(2,1)S(1)} %copy-done.5), kind=kOutput, calls=%fused_computation.6 | convolution fusion | flops 406585344 | bytes 3276800 | tf_op jit(solution)/shard_map/dot_general | solution.py:17
  129.1 3.7 %all-to-all-start.1 = ((bf16[4,64,3072]{2,1,0:T(8,128)(2,1)}), bf16[4,64,3072]{2,1,0:T(8,128)(2,1)S(1)}, u32[]{:S(2)}, u32[]{:S(2)}) async-start(bf16[4,64,3072]{2,1,0:T(8,128)(2,1)} %bitcast.47), calls=%async_computation.1 | async-start | bytes 3145728 | tf_op jit(solution)/shard_map/all_to_all | solution.py:51
  132.9 3.3 %multiply_convert_fusion.2 = (bf16[256,512]{1,0:T(8,128)(2,1)S(1)}, bf16[256,512]{1,0:T(8,128)(2,1)S(1)}) fusion(f32[256,1024]{1,0:T(8,128)} %copy-done.3, bf16[256,3072]{1,0:T(8,128)(2,1)S(1)} %multiply_convert_fusion, bf16[512,3072]{1,0:T(8,128)(2,1)} %constant_dynamic-update-slice_fusion), kind=kOutput, calls=%fused_computation.31 | convolution fusion | flops 807010304 | bytes 6291456 | tf_op jit(solution)/shard_map/dot_general | solution.py:17
  136.2 4.6 %convolution_convert_fusion.2 = bf16[256,3072]{1,0:T(8,128)(2,1)S(1)} fusion(bf16[256,1024]{1,0:T(8,128)(2,1)S(1)} %pad_maximum_fusion.3, bf16[3072,1024]{1,0:T(8,128)(2,1)} %all-gather.4.cloned.1.call-done), kind=kOutput, calls=%fused_computation.3 | convolution fusion | flops 1611399168 | bytes 8388608 | tf_op jit(solution)/shard_map/dot_general | solution.py:17
  140.9 1.9 collective-permute-start.6
  142.9 2.2 collective-permute-done.6
  146.8 7.0 %all-to-all-done.1 = bf16[4,64,3072]{2,1,0:T(8,128)(2,1)S(1)} async-done(((bf16[4,64,3072]{2,1,0:T(8,128)(2,1)}), bf16[4,64,3072]{2,1,0:T(8,128)(2,1)S(1)}, u32[]{:S(2)}, u32[]{:S(2)}) %all-to-all-start.1) | async-done | bytes 1572896 | tf_op jit(solution)/shard_map/all_to_all | solution.py:51
  154.2 3.6 %all-to-all-start.2 = ((bf16[4,64,3072]{2,1,0:T(8,128)(2,1)}), bf16[4,64,3072]{2,1,0:T(8,128)(2,1)S(1)}, u32[]{:S(2)}, u32[]{:S(2)}) async-start(bf16[4,64,3072]{2,1,0:T(8,128)(2,1)} %bitcast.46), calls=%async_computation.2 | async-start | bytes 3145728 | tf_op jit(solution)/shard_map/all_to_all | solution.py:51
  157.8 2.0 collective-permute-start.9
  159.8 2.8 %collective-permute-start.8 = (bf16[16,3072]{1,0:T(8,128)(2,1)S(1)}, bf16[16,3072]{1,0:T(8,128)(2,1)S(1)}, u32[]{:S(2)}, u32[]{:S(2)}) collective-permute-start(bf16[16,3072]{1,0:T(8,128)(2,1)S(1)} %get-tuple-element.47), channel_id=1, source_target_pairs={{0,64},{32,96},{64,0},{96,32},{1,65},{33,97},{65,1},{97,33},{2,66}... | collective-permute-start | bytes 294920 | tf_op jit(solution)/shard_map/ppermute | solution.py:65
  162.5 3.3 %collective-permute-start.7 = (bf16[16,3072]{1,0:T(8,128)(2,1)S(1)}, bf16[16,3072]{1,0:T(8,128)(2,1)S(1)}, u32[]{:S(2)}, u32[]{:S(2)}) collective-permute-start(bf16[16,3072]{1,0:T(8,128)(2,1)S(1)} %get-tuple-element.45), channel_id=1, source_target_pairs={{0,32},{32,64},{64,96},{96,0},{1,33},{33,65},{65,97},{97,1},{2,34}... | collective-permute-start | bytes 294920 | tf_op jit(solution)/shard_map/ppermute | solution.py:65
  165.8 3.8 %collective-permute-done.8 = bf16[16,3072]{1,0:T(8,128)(2,1)S(1)} collective-permute-done((bf16[16,3072]{1,0:T(8,128)(2,1)S(1)}, bf16[16,3072]{1,0:T(8,128)(2,1)S(1)}, u32[]{:S(2)}, u32[]{:S(2)}) %collective-permute-start.8) | collective-permute-done | bytes 98336 | tf_op jit(solution)/shard_map/ppermute | solution.py:65
  170.9 7.1 %all-to-all-done.2 = bf16[4,64,3072]{2,1,0:T(8,128)(2,1)S(1)} async-done(((bf16[4,64,3072]{2,1,0:T(8,128)(2,1)}), bf16[4,64,3072]{2,1,0:T(8,128)(2,1)S(1)}, u32[]{:S(2)}, u32[]{:S(2)}) %all-to-all-start.2) | async-done | bytes 1572896 | tf_op jit(solution)/shard_map/all_to_all | solution.py:51
  178.4 12.8 %all_to_all.25 = bf16[4,16,3072]{2,1,0:T(8,128)(2,1)S(1)} all-to-all(bf16[4,16,3072]{2,1,0:T(8,128)(2,1)S(1)} %bitcast.48), channel_id=1, replica_groups=mesh['x'=4,'zl'=4,'c'=2,'zh'=4,'y'=4] {'zl'}, dimensions={0} | all-to-all | bytes 786432 | tf_op jit(solution)/shard_map/all_to_all | solution.py:51
  192.0 6.6 %all-to-all-start.4 = ((bf16[4,4,6144]{2,1,0:T(4,128)(2,1)}), bf16[4,4,6144]{2,1,0:T(4,128)(2,1)S(1)}, u32[]{:S(2)}, u32[]{:S(2)}) async-start(bf16[4,4,6144]{2,1,0:T(4,128)(2,1)} %reshape.280), calls=%async_computation.4 | async-start | bytes 393216 | tf_op jit(solution)/shard_map/all_to_all | solution.py:51
  198.6 15.9 %all-to-all-done.4 = bf16[4,4,6144]{2,1,0:T(4,128)(2,1)S(1)} async-done(((bf16[4,4,6144]{2,1,0:T(4,128)(2,1)}), bf16[4,4,6144]{2,1,0:T(4,128)(2,1)S(1)}, u32[]{:S(2)}, u32[]{:S(2)}) %all-to-all-start.4) | async-done | bytes 196640 | tf_op jit(solution)/shard_map/all_to_all | solution.py:51
  (89 shorter events, 30.3 us)
Async XLA Ops:
  7.2 2.9 %copy-start.4 = (bf16[1,512,768]{2,1,0:T(8,128)(2,1)S(1)}, bf16[1,512,768]{2,1,0:T(8,128)(2,1)}, u32[]{:S(2)}) copy-start(bf16[1,512,768]{2,1,0:T(8,128)(2,1)} %param.12) | copy-start | bytes 2359300
  7.2 12.6 %copy-start.9 = (s32[4,2]{0,1:T(2,128)S(1)}, s32[4,2]{0,1:T(2,128)}, u32[]{:S(2)}) copy-start(s32[4,2]{0,1:T(2,128)} %param.8) | copy-start | bytes 100
  7.2 12.8 %copy-start.10 = (f32[4,2]{0,1:T(2,128)S(1)}, f32[4,2]{0,1:T(2,128)}, u32[]{:S(2)}) copy-start(f32[4,2]{0,1:T(2,128)} %param.9) | copy-start | bytes 100
  7.2 13.0 %copy-start.7 = (bf16[4,3072]{1,0:T(4,128)(2,1)S(1)}, bf16[4,3072]{1,0:T(4,128)(2,1)}, u32[]{:S(2)}) copy-start(bf16[4,3072]{1,0:T(4,128)(2,1)} %param.13) | copy-start | bytes 73732
  7.2 13.1 %copy-start.8 = (bf16[4,3072]{1,0:T(4,128)(2,1)S(1)}, bf16[4,3072]{1,0:T(4,128)(2,1)}, u32[]{:S(2)}) copy-start(bf16[4,3072]{1,0:T(4,128)(2,1)} %param.7) | copy-start | bytes 73732
  7.2 100.5 %all-gather.4.cloned.1.call-start = ((), (), s32[]{:S(2)}) async-start(), calls=%async_computation.6 | async-start | bytes 7864320 | tf_op jit(solution)/shard_map/all_gather | solution.py:96
  10.1 47.6 %collective-permute-start = (bf16[512,768]{1,0:T(8,128)(2,1)S(1)}, bf16[512,768]{1,0:T(8,128)(2,1)S(1)}, u32[]{:S(2)}, u32[]{:S(2)}) collective-permute-start(bf16[512,768]{1,0:T(8,128)(2,1)S(1)} %bitcast.50), channel_id=1, source_target_pairs={{0,384},{128,0},{256,128},{384,256},{1,385},{129,1},{257,129},{385... | collective-permute-start | bytes 2359304 | tf_op jit(solution)/shard_map/ppermute | solution.py:75
  12.8 45.8 %collective-permute-start.1 = (bf16[512,768]{1,0:T(8,128)(2,1)S(1)}, bf16[512,768]{1,0:T(8,128)(2,1)}, u32[]{:S(2)}, u32[]{:S(2)}) collective-permute-start(bf16[512,768]{1,0:T(8,128)(2,1)S(1)} %bitcast.51), channel_id=1, source_target_pairs={{0,128},{128,256},{256,384},{384,0},{1,129},{129,257},{257,385},{3... | collective-permute-start | bytes 2359304 | tf_op jit(solution)/shard_map/ppermute | solution.py:75
  57.7 0.9 copy-start.2
  60.7 37.9 %all-to-all-start = ((bf16[4,64,6272]{2,1,0:T(8,128)(2,1)}), bf16[4,64,6272]{2,1,0:T(8,128)(2,1)S(1)}, u32[]{:S(2)}, u32[]{:S(2)}) async-start(bf16[4,64,6272]{2,1,0:T(8,128)(2,1)} %broadcast_in_dim.16), calls=%async_computation | async-start | bytes 6422528 | tf_op jit(solution)/shard_map/all_to_all | solution.py:44
  65.2 150.8 %reduce-scatter.2.cloned.1.call-start = ((), (), s32[]{:S(2)}) async-start(), calls=%async_computation.7 | async-start | bytes 3932160 | tf_op jit(solution)/shard_map/reduce_scatter | solution.py:175
  67.0 21.7 %collective-permute-start.2 = (bf16[512,384]{1,0:T(8,128)(2,1)}, bf16[512,384]{1,0:T(8,128)(2,1)}, u32[]{:S(2)}, u32[]{:S(2)}) collective-permute-start(bf16[512,384]{1,0:T(8,128)(2,1)} %slice.79), channel_id=1, source_target_pairs={{0,384},{128,0},{256,128},{384,256},{1,385},{129,1},{257,129},{385... | collective-permute-start | bytes 1179656 | tf_op jit(solution)/shard_map/ppermute | solution.py:75
  70.0 20.8 %collective-permute-start.3 = (bf16[512,384]{1,0:T(8,128)(2,1)S(1)}, bf16[512,384]{1,0:T(8,128)(2,1)S(1)}, u32[]{:S(2)}, u32[]{:S(2)}) collective-permute-start(bf16[512,384]{1,0:T(8,128)(2,1)S(1)} %slice.80), channel_id=1, source_target_pairs={{0,128},{128,256},{256,384},{384,0},{1,129},{129,257},{257,385},{3... | collective-permute-start | bytes 1179656 | tf_op jit(solution)/shard_map/ppermute | solution.py:75
  100.9 5.7 %collective-permute-start.4 = (bf16[128,6272]{1,0:T(8,128)(2,1)}, bf16[128,6272]{1,0:T(8,128)(2,1)}, u32[]{:S(2)}, u32[]{:S(2)}) collective-permute-start(bf16[128,6272]{1,0:T(8,128)(2,1)} %convolution_convert_fusion), channel_id=1, source_target_pairs={{0,16},{16,0},{1,17},{17,1},{2,18},{18,2},{3,19},{19,3},{4,20},{20... | collective-permute-start | bytes 4816904 | tf_op jit(solution)/shard_map/ppermute | solution.py:121
  105.3 1.3 copy-start
  112.8 3.3 %copy-start.3 = (f32[256,1024]{1,0:T(8,128)}, f32[256,1024]{1,0:T(8,128)S(1)}, u32[]{:S(2)}) copy-start(f32[256,1024]{1,0:T(8,128)S(1)} %fusion.1) | copy-start | bytes 3145732
  113.0 6.9 %copy-start.1 = (bf16[128,6272]{1,0:T(8,128)(2,1)S(1)}, bf16[128,6272]{1,0:T(8,128)(2,1)}, u32[]{:S(2)}) copy-start(bf16[128,6272]{1,0:T(8,128)(2,1)} %copy-done) | copy-start | bytes 4816900
  117.4 7.7 %collective-permute-start.5 = (bf16[128,3072]{1,0:T(8,128)(2,1)}, bf16[128,3072]{1,0:T(8,128)(2,1)}, u32[]{:S(2)}, u32[]{:S(2)}) collective-permute-start(bf16[128,3072]{1,0:T(8,128)(2,1)} %get-tuple-element.44), channel_id=1, source_target_pairs={{0,16},{16,0},{1,17},{17,1},{2,18},{18,2},{3,19},{19,3},{4,20},{20... | collective-permute-start | bytes 2359304 | tf_op jit(solution)/shard_map/ppermute | solution.py:142
  125.1 1.1 copy-start.5
  125.1 1.1 copy-start.6
  129.1 24.7 %all-to-all-start.1 = ((bf16[4,64,3072]{2,1,0:T(8,128)(2,1)}), bf16[4,64,3072]{2,1,0:T(8,128)(2,1)S(1)}, u32[]{:S(2)}, u32[]{:S(2)}) async-start(bf16[4,64,3072]{2,1,0:T(8,128)(2,1)} %bitcast.47), calls=%async_computation.1 | async-start | bytes 3145728 | tf_op jit(solution)/shard_map/all_to_all | solution.py:51
  140.9 4.2 %collective-permute-start.6 = (bf16[128,3072]{1,0:T(8,128)(2,1)S(1)}, bf16[128,3072]{1,0:T(8,128)(2,1)S(1)}, u32[]{:S(2)}, u32[]{:S(2)}) collective-permute-start(bf16[128,3072]{1,0:T(8,128)(2,1)S(1)} %get-tuple-element.40), channel_id=1, source_target_pairs={{0,16},{16,0},{1,17},{17,1},{2,18},{18,2},{3,19},{19,3},{4,20},{20... | collective-permute-start | bytes 2359304 | tf_op jit(solution)/shard_map/ppermute | solution.py:142
  154.2 23.9 %all-to-all-start.2 = ((bf16[4,64,3072]{2,1,0:T(8,128)(2,1)}), bf16[4,64,3072]{2,1,0:T(8,128)(2,1)S(1)}, u32[]{:S(2)}, u32[]{:S(2)}) async-start(bf16[4,64,3072]{2,1,0:T(8,128)(2,1)} %bitcast.46), calls=%async_computation.2 | async-start | bytes 3145728 | tf_op jit(solution)/shard_map/all_to_all | solution.py:51
  157.8 8.0 %collective-permute-start.9 = (bf16[16,3072]{1,0:T(8,128)(2,1)S(1)}, bf16[16,3072]{1,0:T(8,128)(2,1)S(1)}, u32[]{:S(2)}, u32[]{:S(2)}) collective-permute-start(bf16[16,3072]{1,0:T(8,128)(2,1)S(1)} %get-tuple-element.46), channel_id=1, source_target_pairs={{0,96},{32,0},{64,32},{96,64},{1,97},{33,1},{65,33},{97,65},{2,98}... | collective-permute-start | bytes 294920 | tf_op jit(solution)/shard_map/ppermute | solution.py:65
  159.8 9.9 %collective-permute-start.8 = (bf16[16,3072]{1,0:T(8,128)(2,1)S(1)}, bf16[16,3072]{1,0:T(8,128)(2,1)S(1)}, u32[]{:S(2)}, u32[]{:S(2)}) collective-permute-start(bf16[16,3072]{1,0:T(8,128)(2,1)S(1)} %get-tuple-element.47), channel_id=1, source_target_pairs={{0,64},{32,96},{64,0},{96,32},{1,65},{33,97},{65,1},{97,33},{2,66}... | collective-permute-start | bytes 294920 | tf_op jit(solution)/shard_map/ppermute | solution.py:65
  162.5 8.3 %collective-permute-start.7 = (bf16[16,3072]{1,0:T(8,128)(2,1)S(1)}, bf16[16,3072]{1,0:T(8,128)(2,1)S(1)}, u32[]{:S(2)}, u32[]{:S(2)}) collective-permute-start(bf16[16,3072]{1,0:T(8,128)(2,1)S(1)} %get-tuple-element.45), channel_id=1, source_target_pairs={{0,32},{32,64},{64,96},{96,0},{1,33},{33,65},{65,97},{97,1},{2,34}... | collective-permute-start | bytes 294920 | tf_op jit(solution)/shard_map/ppermute | solution.py:65
  192.0 22.5 %all-to-all-start.4 = ((bf16[4,4,6144]{2,1,0:T(4,128)(2,1)}), bf16[4,4,6144]{2,1,0:T(4,128)(2,1)S(1)}, u32[]{:S(2)}, u32[]{:S(2)}) async-start(bf16[4,4,6144]{2,1,0:T(4,128)(2,1)} %reshape.280), calls=%async_computation.4 | async-start | bytes 393216 | tf_op jit(solution)/shard_map/all_to_all | solution.py:51
Sparse Core Ops, SparseCore 0:
  10.2 84.6 all-gather.3
  125.2 37.6 reduce-scatter.1

commit v8 on v7

--- a/solution.py
+++ b/solution.py
@@ -161,7 +161,7 @@
     grad_up = (grad_hidden * activated).astype(BF16)
     grad_gate = (grad_hidden * up_pre * slope_gate).astype(BF16)
     grad_both = jnp.concatenate([grad_gate, grad_up], axis=1)
-    late_hidden, _ = lax.optimization_barrier((hidden, out_part))
+    late_hidden, _ = lax.optimization_barrier((hidden, out_tokens))
     grad_both, _ = lax.optimization_barrier((grad_both, out_tokens))
     grad_part = dot(grad_both, full_both, LAST).astype(BF16)
     grad_tokens = by_token(swap_back(grad_part))

time: 224 us -> 221 us (0.987)
  waiting for transfers between devices: 53 us -> 49 us
    all_to_all x3, waiting for transfers between devices: 30 us -> 25.2 us  [scatter_sum_by_exchange(): parts = lax.all_to_all(parts, axes, split_axis=0, concat_axis=0, tiled=True)]
    unnamed x27 -> x29, local copies, waits for them, and re-layouts: 9.07 us -> 8.07 us
  transfers between devices with their start and end apart: 16 -> 16, of which waited for: 10 -> 9; matrix products, arithmetic and copies ran while one was open for 19% -> 18% of each run, Pallas kernels for 0% -> 0%
where the time goes in v8:
time: 221 us; the launch traced here: 219 us
  blocking collectives  50.4 us (23%)
  starting transfers between devices  49.7 us (22%)
  waiting for transfers between devices  49 us (22%)
  matrix products  25.1 us (11%)
  local copies, waits for them, and re-layouts  19 us (9%)
  between operations  14.7 us (7%)
  other arithmetic  11.5 us (5%)
    all_gather x1, blocking collectives, on_device(): by_z = lax.all_gather(packed[None], ('zh', 'zl'), axis=0, tiled=True)  37.3 us
    all_to_all x3, waiting for transfers between devices, scatter_sum_by_exchange(): parts = lax.all_to_all(parts, axes, split_axis=0, concat_axis=0, tiled=True)  25.2 us
    dot_general x12, matrix products, dot(): return lax.dot_general(a, b, dims, preferred_element_type=F32)  25.1 us
    ppermute x4, starting transfers between devices, pass_on(): return lax.ppermute(x, axis, [(i, (i + shift) % size) for i in range(size)])  16.7 us
    all_to_all x3, starting transfers between devices, scatter_sum_by_exchange(): parts = lax.all_to_all(parts, axes, split_axis=0, concat_axis=0, tiled=True)  14.1 us
    all_to_all x1, blocking collectives, scatter_sum_by_exchange(): parts = lax.all_to_all(parts, axes, split_axis=0, concat_axis=0, tiled=True)  13.2 us
    ppermute x4, waiting for transfers between devices, pass_on(): return lax.ppermute(x, axis, [(i, (i + shift) % size) for i in range(size)])  9.7 us
    unnamed x29, local copies, waits for them, and re-layouts  8.07 us
  transfers between devices with their start and end apart: 16, of which 9 were waited for; matrix products, arithmetic and copies ran while one was open for 18% of the time, Pallas kernels for 0%

profile of v8, /device:TPU:6, one launch (start us, length us, event | category | flops | bytes accessed | tf_op | source)
XLA Modules:
  0.0 219.4 jit_solution(4835604201786213192)
XLA Ops:
  7.3 2.8 %pad_maximum_fusion.2 = bf16[768,1024]{1,0:T(8,128)(2,1)} fusion(bf16[768,512]{1,0:T(8,128)(2,1)} %bitcast.51, bf16[768,512]{1,0:T(8,128)(2,1)} %bitcast.52), kind=kLoop, calls=%fused_computation.14 | loop fusion | flops 3145728 | bytes 3145728 | tf_op jit(solution)/shard_map/concatenate | solution.py:93
  10.1 2.7 %collective-permute-start = (bf16[512,768]{1,0:T(8,128)(2,1)S(1)}, bf16[512,768]{1,0:T(8,128)(2,1)}, u32[]{:S(2)}, u32[]{:S(2)}) collective-permute-start(bf16[512,768]{1,0:T(8,128)(2,1)S(1)} %bitcast.49), channel_id=1, source_target_pairs={{0,384},{128,0},{256,128},{384,256},{1,385},{129,1},{257,129},{385... | collective-permute-start | bytes 2359304 | tf_op jit(solution)/shard_map/ppermute | solution.py:75
  12.8 6.9 %collective-permute-start.1 = (bf16[512,768]{1,0:T(8,128)(2,1)S(1)}, bf16[512,768]{1,0:T(8,128)(2,1)}, u32[]{:S(2)}, u32[]{:S(2)}) collective-permute-start(bf16[512,768]{1,0:T(8,128)(2,1)S(1)} %bitcast.50), channel_id=1, source_target_pairs={{0,128},{128,256},{256,384},{384,0},{1,129},{129,257},{257,385},{3... | collective-permute-start | bytes 2359304 | tf_op jit(solution)/shard_map/ppermute | solution.py:75
  20.4 37.3 %all-gather.1 = bf16[16,4,6272]{2,1,0:T(4,128)(2,1)S(1)} all-gather(bf16[1,4,6272]{2,1,0:T(4,128)(2,1)S(1)} %fusion.44), channel_id=2, replica_groups=mesh['x'=4,'zl'=4,'c'=2,'zh'=4,'y'=4] {'zh','zl'}, dimensions={0}, use_global_device_ids=true | all-gather | bytes 852992 | tf_op jit(solution)/shard_map/all_gather | solution.py:102
  57.8 2.0 broadcast_in_dim.16
  59.8 4.5 %all-to-all-start = ((bf16[4,64,6272]{2,1,0:T(8,128)(2,1)}), bf16[4,64,6272]{2,1,0:T(8,128)(2,1)S(1)}, u32[]{:S(2)}, u32[]{:S(2)}) async-start(bf16[4,64,6272]{2,1,0:T(8,128)(2,1)} %broadcast_in_dim.16), calls=%async_computation | async-start | bytes 6422528 | tf_op jit(solution)/shard_map/all_to_all | solution.py:44
  66.0 1.9 collective-permute-start.2
  69.0 5.1 %collective-permute-start.3 = (bf16[512,384]{1,0:T(8,128)(2,1)S(1)}, bf16[512,384]{1,0:T(8,128)(2,1)S(1)}, u32[]{:S(2)}, u32[]{:S(2)}) collective-permute-start(bf16[512,384]{1,0:T(8,128)(2,1)S(1)} %slice.80), channel_id=1, source_target_pairs={{0,128},{128,256},{256,384},{384,0},{1,129},{129,257},{257,385},{3... | collective-permute-start | bytes 1179656 | tf_op jit(solution)/shard_map/ppermute | solution.py:75
  74.2 2.1 constant_dynamic-update-slice_fusion.4
  76.3 2.1 constant_dynamic-update-slice_fusion.3
  78.4 9.4 %collective-permute-done.2 = bf16[512,384]{1,0:T(8,128)(2,1)} collective-permute-done((bf16[512,384]{1,0:T(8,128)(2,1)}, bf16[512,384]{1,0:T(8,128)(2,1)}, u32[]{:S(2)}, u32[]{:S(2)}) %collective-permute-start.2) | collective-permute-done | bytes 393248 | tf_op jit(solution)/shard_map/ppermute | solution.py:75
  90.8 2.1 constant_dynamic-update-slice_fusion
  92.9 5.0 %all-to-all-done = bf16[4,64,6272]{2,1,0:T(8,128)(2,1)S(1)} async-done(((bf16[4,64,6272]{2,1,0:T(8,128)(2,1)}), bf16[4,64,6272]{2,1,0:T(8,128)(2,1)S(1)}, u32[]{:S(2)}, u32[]{:S(2)}) %all-to-all-start) | async-done | bytes 3211296 | tf_op jit(solution)/shard_map/all_to_all | solution.py:44
  98.1 2.0 convolution_convert_fusion
  103.9 1.9 collective-permute-done.4
  107.0 5.1 %fusion.1 = f32[256,1024]{1,0:T(8,128)S(1)} fusion(bf16[3072,1024]{1,0:T(8,128)(2,1)} %all-gather.4.cloned.1.call-done, bf16[128,6272]{1,0:T(8,128)(2,1)} %collective-permute-done.4, bf16[128,6272]{1,0:T(8,128)(2,1)} %copy-done), kind=kOutput, calls=%fused_computation.10 | convolution fusion | flops 1613758464 | bytes 10551296 | tf_op jit(solution)/shard_map/dot_general | solution.py:17
  112.2 3.1 %fusion = bf16[256,3072]{1,0:T(8,128)(2,1)S(1)} fusion(bf16[256,512]{1,0:T(8,128)(2,1)S(1)} %multiply_convert_fusion.3, bf16[512,3072]{1,0:T(8,128)(2,1)} %constant_dynamic-update-slice_fusion, f32[256]{0:T(256)S(1)} %get-tuple-element.37), kind=kOutput, calls=%fused_computation.4 | convolution fusion | flops 806879232 | bytes 4981760 | tf_op jit(solution)/shard_map/dot_general | solution.py:17
  116.7 2.0 collective-permute-start.5
  121.2 2.9 %convolution_convert_fusion.4 = bf16[256,3072]{1,0:T(8,128)(2,1)} fusion(bf16[256,256]{1,0:T(8,128)(2,1)S(1)} %copy-done.6, bf16[128,3072]{1,0:T(8,128)(2,1)} %collective-permute-done.5, bf16[128,3072]{1,0:T(8,128)(2,1)S(1)} %copy-done.4), kind=kOutput, calls=%fused_computation.6 | convolution fusion | flops 406585344 | bytes 3276800 | tf_op jit(solution)/shard_map/dot_general | solution.py:17
  124.1 3.6 %all-to-all-start.1 = ((bf16[4,64,3072]{2,1,0:T(8,128)(2,1)}), bf16[4,64,3072]{2,1,0:T(8,128)(2,1)S(1)}, u32[]{:S(2)}, u32[]{:S(2)}) async-start(bf16[4,64,3072]{2,1,0:T(8,128)(2,1)} %bitcast.46), calls=%async_computation.1 | async-start | bytes 3145728 | tf_op jit(solution)/shard_map/all_to_all | solution.py:51
  127.9 3.3 %multiply_convert_fusion.2 = (bf16[256,512]{1,0:T(8,128)(2,1)S(1)}, bf16[256,512]{1,0:T(8,128)(2,1)S(1)}) fusion(f32[256,1024]{1,0:T(8,128)} %copy-done.2, bf16[256,3072]{1,0:T(8,128)(2,1)S(1)} %multiply_convert_fusion, bf16[512,3072]{1,0:T(8,128)(2,1)} %constant_dynamic-update-slice_fusion), kind=kOutput, calls=%fused_computation.31 | convolution fusion | flops 807010304 | bytes 6291456 | tf_op jit(solution)/shard_map/dot_general | solution.py:17
  136.7 4.6 %convolution_convert_fusion.2 = bf16[256,3072]{1,0:T(8,128)(2,1)S(1)} fusion(bf16[256,1024]{1,0:T(8,128)(2,1)S(1)} %copy-done.5, bf16[3072,1024]{1,0:T(8,128)(2,1)} %all-gather.4.cloned.1.call-done), kind=kOutput, calls=%fused_computation.3 | convolution fusion | flops 1611399168 | bytes 8388608 | tf_op jit(solution)/shard_map/dot_general | solution.py:17
  141.4 2.3 %collective-permute-start.6 = (bf16[128,3072]{1,0:T(8,128)(2,1)S(1)}, bf16[128,3072]{1,0:T(8,128)(2,1)S(1)}, u32[]{:S(2)}, u32[]{:S(2)}) collective-permute-start(bf16[128,3072]{1,0:T(8,128)(2,1)S(1)} %get-tuple-element.40), channel_id=1, source_target_pairs={{0,16},{16,0},{1,17},{17,1},{2,18},{18,2},{3,19},{19,3},{4,20},{20... | collective-permute-start | bytes 2359304 | tf_op jit(solution)/shard_map/ppermute | solution.py:142
  149.5 3.6 %all-to-all-start.2 = ((bf16[4,64,3072]{2,1,0:T(8,128)(2,1)}), bf16[4,64,3072]{2,1,0:T(8,128)(2,1)S(1)}, u32[]{:S(2)}, u32[]{:S(2)}) async-start(bf16[4,64,3072]{2,1,0:T(8,128)(2,1)} %bitcast.11), calls=%async_computation.2 | async-start | bytes 3145728 | tf_op jit(solution)/shard_map/all_to_all | solution.py:51
  153.2 2.0 collective-permute-start.9
  155.1 2.7 %collective-permute-start.8 = (bf16[16,3072]{1,0:T(8,128)(2,1)S(1)}, bf16[16,3072]{1,0:T(8,128)(2,1)S(1)}, u32[]{:S(2)}, u32[]{:S(2)}) collective-permute-start(bf16[16,3072]{1,0:T(8,128)(2,1)S(1)} %get-tuple-element.47), channel_id=1, source_target_pairs={{0,64},{32,96},{64,0},{96,32},{1,65},{33,97},{65,1},{97,33},{2,66}... | collective-permute-start | bytes 294920 | tf_op jit(solution)/shard_map/ppermute | solution.py:65
  157.8 3.3 %collective-permute-start.7 = (bf16[16,3072]{1,0:T(8,128)(2,1)S(1)}, bf16[16,3072]{1,0:T(8,128)(2,1)S(1)}, u32[]{:S(2)}, u32[]{:S(2)}) collective-permute-start(bf16[16,3072]{1,0:T(8,128)(2,1)S(1)} %get-tuple-element.45), channel_id=1, source_target_pairs={{0,32},{32,64},{64,96},{96,0},{1,33},{33,65},{65,97},{97,1},{2,34}... | collective-permute-start | bytes 294920 | tf_op jit(solution)/shard_map/ppermute | solution.py:65
  161.2 5.3 %collective-permute-done.8 = bf16[16,3072]{1,0:T(8,128)(2,1)S(1)} collective-permute-done((bf16[16,3072]{1,0:T(8,128)(2,1)S(1)}, bf16[16,3072]{1,0:T(8,128)(2,1)S(1)}, u32[]{:S(2)}, u32[]{:S(2)}) %collective-permute-start.8) | collective-permute-done | bytes 98336 | tf_op jit(solution)/shard_map/ppermute | solution.py:65
  166.5 7.3 %all-to-all-done.2 = bf16[4,64,3072]{2,1,0:T(8,128)(2,1)S(1)} async-done(((bf16[4,64,3072]{2,1,0:T(8,128)(2,1)}), bf16[4,64,3072]{2,1,0:T(8,128)(2,1)S(1)}, u32[]{:S(2)}, u32[]{:S(2)}) %all-to-all-start.2) | async-done | bytes 1572896 | tf_op jit(solution)/shard_map/all_to_all | solution.py:51
  174.1 13.2 %all_to_all.25 = bf16[4,16,3072]{2,1,0:T(8,128)(2,1)S(1)} all-to-all(bf16[4,16,3072]{2,1,0:T(8,128)(2,1)S(1)} %bitcast.47), channel_id=1, replica_groups=mesh['x'=4,'zl'=4,'c'=2,'zh'=4,'y'=4] {'zl'}, dimensions={0} | all-to-all | bytes 786432 | tf_op jit(solution)/shard_map/all_to_all | solution.py:51
  188.1 6.9 %all-to-all-start.4 = ((bf16[4,4,6144]{2,1,0:T(4,128)(2,1)}), bf16[4,4,6144]{2,1,0:T(4,128)(2,1)S(1)}, u32[]{:S(2)}, u32[]{:S(2)}) async-start(bf16[4,4,6144]{2,1,0:T(4,128)(2,1)} %reshape.280), calls=%async_computation.4 | async-start | bytes 393216 | tf_op jit(solution)/shard_map/all_to_all | solution.py:51
  195.1 16.1 %all-to-all-done.4 = bf16[4,4,6144]{2,1,0:T(4,128)(2,1)S(1)} async-done(((bf16[4,4,6144]{2,1,0:T(4,128)(2,1)}), bf16[4,4,6144]{2,1,0:T(4,128)(2,1)S(1)}, u32[]{:S(2)}, u32[]{:S(2)}) %all-to-all-start.4) | async-done | bytes 196640 | tf_op jit(solution)/shard_map/all_to_all | solution.py:51
  (91 shorter events, 29.8 us)
Async XLA Ops:
  7.2 2.9 %copy-start.3 = (bf16[1,512,768]{2,1,0:T(8,128)(2,1)S(1)}, bf16[1,512,768]{2,1,0:T(8,128)(2,1)}, u32[]{:S(2)}) copy-start(bf16[1,512,768]{2,1,0:T(8,128)(2,1)} %param.12) | copy-start | bytes 2359300
  7.2 12.6 %copy-start.10 = (s32[4,2]{0,1:T(2,128)S(1)}, s32[4,2]{0,1:T(2,128)}, u32[]{:S(2)}) copy-start(s32[4,2]{0,1:T(2,128)} %param.8) | copy-start | bytes 100
  7.2 12.8 %copy-start.11 = (f32[4,2]{0,1:T(2,128)S(1)}, f32[4,2]{0,1:T(2,128)}, u32[]{:S(2)}) copy-start(f32[4,2]{0,1:T(2,128)} %param.9) | copy-start | bytes 100
  7.2 13.0 %copy-start.8 = (bf16[4,3072]{1,0:T(4,128)(2,1)S(1)}, bf16[4,3072]{1,0:T(4,128)(2,1)}, u32[]{:S(2)}) copy-start(bf16[4,3072]{1,0:T(4,128)(2,1)} %param.13) | copy-start | bytes 73732
  7.2 13.1 %copy-start.9 = (bf16[4,3072]{1,0:T(4,128)(2,1)S(1)}, bf16[4,3072]{1,0:T(4,128)(2,1)}, u32[]{:S(2)}) copy-start(bf16[4,3072]{1,0:T(4,128)(2,1)} %param.7) | copy-start | bytes 73732
  7.2 99.7 %all-gather.4.cloned.1.call-start = ((), (), s32[]{:S(2)}) async-start(), calls=%async_computation.6 | async-start | bytes 7864320 | tf_op jit(solution)/shard_map/all_gather | solution.py:96
  10.1 47.6 %collective-permute-start = (bf16[512,768]{1,0:T(8,128)(2,1)S(1)}, bf16[512,768]{1,0:T(8,128)(2,1)}, u32[]{:S(2)}, u32[]{:S(2)}) collective-permute-start(bf16[512,768]{1,0:T(8,128)(2,1)S(1)} %bitcast.49), channel_id=1, source_target_pairs={{0,384},{128,0},{256,128},{384,256},{1,385},{129,1},{257,129},{385... | collective-permute-start | bytes 2359304 | tf_op jit(solution)/shard_map/ppermute | solution.py:75
  12.8 44.8 %collective-permute-start.1 = (bf16[512,768]{1,0:T(8,128)(2,1)S(1)}, bf16[512,768]{1,0:T(8,128)(2,1)}, u32[]{:S(2)}, u32[]{:S(2)}) collective-permute-start(bf16[512,768]{1,0:T(8,128)(2,1)S(1)} %bitcast.50), channel_id=1, source_target_pairs={{0,128},{128,256},{256,384},{384,0},{1,129},{129,257},{257,385},{3... | collective-permute-start | bytes 2359304 | tf_op jit(solution)/shard_map/ppermute | solution.py:75
  59.8 38.1 %all-to-all-start = ((bf16[4,64,6272]{2,1,0:T(8,128)(2,1)}), bf16[4,64,6272]{2,1,0:T(8,128)(2,1)S(1)}, u32[]{:S(2)}, u32[]{:S(2)}) async-start(bf16[4,64,6272]{2,1,0:T(8,128)(2,1)} %broadcast_in_dim.16), calls=%async_computation | async-start | bytes 6422528 | tf_op jit(solution)/shard_map/all_to_all | solution.py:44
  66.0 21.8 %collective-permute-start.2 = (bf16[512,384]{1,0:T(8,128)(2,1)}, bf16[512,384]{1,0:T(8,128)(2,1)}, u32[]{:S(2)}, u32[]{:S(2)}) collective-permute-start(bf16[512,384]{1,0:T(8,128)(2,1)} %slice.79), channel_id=1, source_target_pairs={{0,384},{128,0},{256,128},{384,256},{1,385},{129,1},{257,129},{385... | collective-permute-start | bytes 1179656 | tf_op jit(solution)/shard_map/ppermute | solution.py:75
  69.0 20.9 %collective-permute-start.3 = (bf16[512,384]{1,0:T(8,128)(2,1)S(1)}, bf16[512,384]{1,0:T(8,128)(2,1)S(1)}, u32[]{:S(2)}, u32[]{:S(2)}) collective-permute-start(bf16[512,384]{1,0:T(8,128)(2,1)S(1)} %slice.80), channel_id=1, source_target_pairs={{0,128},{128,256},{256,384},{384,0},{1,129},{129,257},{257,385},{3... | collective-permute-start | bytes 1179656 | tf_op jit(solution)/shard_map/ppermute | solution.py:75
  100.1 5.7 %collective-permute-start.4 = (bf16[128,6272]{1,0:T(8,128)(2,1)}, bf16[128,6272]{1,0:T(8,128)(2,1)}, u32[]{:S(2)}, u32[]{:S(2)}) collective-permute-start(bf16[128,6272]{1,0:T(8,128)(2,1)} %convolution_convert_fusion), channel_id=1, source_target_pairs={{0,16},{16,0},{1,17},{17,1},{2,18},{18,2},{3,19},{19,3},{4,20},{20... | collective-permute-start | bytes 4816904 | tf_op jit(solution)/shard_map/ppermute | solution.py:121
  103.9 1.9 copy-start
  112.0 3.3 %copy-start.2 = (f32[256,1024]{1,0:T(8,128)}, f32[256,1024]{1,0:T(8,128)S(1)}, u32[]{:S(2)}) copy-start(f32[256,1024]{1,0:T(8,128)S(1)} %fusion.1) | copy-start | bytes 3145732
  112.2 7.3 %copy-start.1 = (bf16[128,6272]{1,0:T(8,128)(2,1)S(1)}, bf16[128,6272]{1,0:T(8,128)(2,1)}, u32[]{:S(2)}) copy-start(bf16[128,6272]{1,0:T(8,128)(2,1)} %copy-done) | copy-start | bytes 4816900
  116.7 4.5 %collective-permute-start.5 = (bf16[128,3072]{1,0:T(8,128)(2,1)}, bf16[128,3072]{1,0:T(8,128)(2,1)}, u32[]{:S(2)}, u32[]{:S(2)}) collective-permute-start(bf16[128,3072]{1,0:T(8,128)(2,1)} %get-tuple-element.44), channel_id=1, source_target_pairs={{0,16},{16,0},{1,17},{17,1},{2,18},{18,2},{3,19},{19,3},{4,20},{20... | collective-permute-start | bytes 2359304 | tf_op jit(solution)/shard_map/ppermute | solution.py:142
  119.5 1.7 copy-start.4
  119.5 1.7 copy-start.6
  124.1 25.1 %all-to-all-start.1 = ((bf16[4,64,3072]{2,1,0:T(8,128)(2,1)}), bf16[4,64,3072]{2,1,0:T(8,128)(2,1)S(1)}, u32[]{:S(2)}, u32[]{:S(2)}) async-start(bf16[4,64,3072]{2,1,0:T(8,128)(2,1)} %bitcast.46), calls=%async_computation.1 | async-start | bytes 3145728 | tf_op jit(solution)/shard_map/all_to_all | solution.py:51
  127.7 84.9 %reduce-scatter.2.cloned.1.call-start = ((), (), s32[]{:S(2)}) async-start(), calls=%async_computation.7 | async-start | bytes 3932160 | tf_op jit(solution)/shard_map/reduce_scatter | solution.py:175
  135.6 1.0 copy-start.5
  141.3 4.3 %copy-start.7 = (bf16[256,256]{1,0:T(8,128)(2,1)S(1)}, bf16[256,256]{1,0:T(8,128)(2,1)}, u32[]{:S(2)}) copy-start(bf16[256,256]{1,0:T(8,128)(2,1)} %add_convert_fusion) | copy-start | bytes 393220
  141.4 4.2 %collective-permute-start.6 = (bf16[128,3072]{1,0:T(8,128)(2,1)S(1)}, bf16[128,3072]{1,0:T(8,128)(2,1)S(1)}, u32[]{:S(2)}, u32[]{:S(2)}) collective-permute-start(bf16[128,3072]{1,0:T(8,128)(2,1)S(1)} %get-tuple-element.40), channel_id=1, source_target_pairs={{0,16},{16,0},{1,17},{17,1},{2,18},{18,2},{3,19},{19,3},{4,20},{20... | collective-permute-start | bytes 2359304 | tf_op jit(solution)/shard_map/ppermute | solution.py:142
  149.5 24.3 %all-to-all-start.2 = ((bf16[4,64,3072]{2,1,0:T(8,128)(2,1)}), bf16[4,64,3072]{2,1,0:T(8,128)(2,1)S(1)}, u32[]{:S(2)}, u32[]{:S(2)}) async-start(bf16[4,64,3072]{2,1,0:T(8,128)(2,1)} %bitcast.11), calls=%async_computation.2 | async-start | bytes 3145728 | tf_op jit(solution)/shard_map/all_to_all | solution.py:51
  153.2 8.0 %collective-permute-start.9 = (bf16[16,3072]{1,0:T(8,128)(2,1)S(1)}, bf16[16,3072]{1,0:T(8,128)(2,1)S(1)}, u32[]{:S(2)}, u32[]{:S(2)}) collective-permute-start(bf16[16,3072]{1,0:T(8,128)(2,1)S(1)} %get-tuple-element.46), channel_id=1, source_target_pairs={{0,96},{32,0},{64,32},{96,64},{1,97},{33,1},{65,33},{97,65},{2,98}... | collective-permute-start | bytes 294920 | tf_op jit(solution)/shard_map/ppermute | solution.py:65
  155.1 11.3 %collective-permute-start.8 = (bf16[16,3072]{1,0:T(8,128)(2,1)S(1)}, bf16[16,3072]{1,0:T(8,128)(2,1)S(1)}, u32[]{:S(2)}, u32[]{:S(2)}) collective-permute-start(bf16[16,3072]{1,0:T(8,128)(2,1)S(1)} %get-tuple-element.47), channel_id=1, source_target_pairs={{0,64},{32,96},{64,0},{96,32},{1,65},{33,97},{65,1},{97,33},{2,66}... | collective-permute-start | bytes 294920 | tf_op jit(solution)/shard_map/ppermute | solution.py:65
  157.8 8.6 %collective-permute-start.7 = (bf16[16,3072]{1,0:T(8,128)(2,1)S(1)}, bf16[16,3072]{1,0:T(8,128)(2,1)S(1)}, u32[]{:S(2)}, u32[]{:S(2)}) collective-permute-start(bf16[16,3072]{1,0:T(8,128)(2,1)S(1)} %get-tuple-element.45), channel_id=1, source_target_pairs={{0,32},{32,64},{64,96},{96,0},{1,33},{33,65},{65,97},{97,1},{2,34}... | collective-permute-start | bytes 294920 | tf_op jit(solution)/shard_map/ppermute | solution.py:65
  188.1 23.0 %all-to-all-start.4 = ((bf16[4,4,6144]{2,1,0:T(4,128)(2,1)}), bf16[4,4,6144]{2,1,0:T(4,128)(2,1)S(1)}, u32[]{:S(2)}, u32[]{:S(2)}) async-start(bf16[4,4,6144]{2,1,0:T(4,128)(2,1)} %reshape.280), calls=%async_computation.4 | async-start | bytes 393216 | tf_op jit(solution)/shard_map/all_to_all | solution.py:51
Sparse Core Ops, SparseCore 0:
  10.2 84.6 all-gather.3
  135.8 40.1 reduce-scatter.1
